TPU v7x, 32 devices: a whole 2x2x4 slice. The times are simulated.
32 devices in a mesh: seq: 4 (over x, core), expert: 8 (over z, y).
Axes of the slice: x: 2, y: 2, z: 4, core: 2. Of those that a mesh axis runs over, the one named last changes fastest.
Arguments:
- queries: bfloat16 [8, 512, 2048], P('expert', 'seq'), may hold values from -8 to 8
- keys: bfloat16 [8, 512, 2048], P('expert', 'seq'), may hold values from -8 to 8
- values: bfloat16 [8, 512, 2048], P('expert', 'seq'), may hold values from -12 to 12
- hidden: bfloat16 [8, 512, 2048], P('expert', 'seq'), may hold values from -6 to 6
- out_proj: bfloat16 [2048, 2048], P('expert'), may hold values from -0.125 to 0.125
- ln_gain: float32 [2048], replicated, may hold values from 0.1 to 1.9
- w_router: bfloat16 [2048, 16], replicated, may hold values from -0.125 to 0.125
- routes: int32 [8, 512, 2], P('expert', 'seq'), may hold values from 0 to 15, all different within a row; in each aligned block of 128 rows (0 to 127, 128 to 255, ..., all dimensions but the last counted through in order) at most 32 rows name the same one
- w_in: bfloat16 [32, 2048, 2048], P(('seq', 'expert')), may hold values from -0.125 to 0.125
- w_out: bfloat16 [32, 2048, 2048], P(('seq', 'expert')), may hold values from -0.09375 to 0.09375
Outputs:
- layer_out: bfloat16 [8, 512, 2048], P('expert', 'seq')
Inputs may be any that keep to these rules, and one draw needn't show every extreme that they name: `routes`: each token names two different experts. Among the 128 tokens of one device (rows in order of document, then position) no expert is named by more than 32 tokens, and in some such blocks one expert is named by exactly 32.
All inputs are finite; a program needn't handle non-finite values.
Results may differ from a plain program's by a relative error of at most 0.007.
Values may be sent and summed in bfloat16 or wider, within the bound.
No kernel may reach another device: no remote copies, remote signals or barrier semaphores. Data moves between devices by JAX's collectives and lax.ppermute only.
A program may use at most 128 MiB of HBM per device.

v0:
```python
import jax
import jax.numpy as jnp
from jax import lax
from jax.sharding import PartitionSpec as P

HEADS = 16


NORM_EPS = 1e-05


def blockwise(query_rows, key_rows, value_rows, head_count):
    row_count, model_width = query_rows.shape
    shard_len = key_rows.shape[0]
    head_dim = model_width // head_count
    query_heads = query_rows.reshape(row_count, head_count, head_dim)
    key_heads = key_rows.reshape(shard_len, head_count, head_dim)
    value_heads = value_rows.reshape(shard_len, head_count, head_dim)
    scores = jnp.einsum(
        "rhd,shd->hrs", query_heads, key_heads, preferred_element_type=jnp.float32
    ) * head_dim ** (-0.5)
    peak_score = jnp.max(scores, axis=2)
    weights = jnp.exp(scores - peak_score[:, :, None]).astype(jnp.bfloat16)
    block_total = jnp.sum(weights.astype(jnp.float32), axis=2)
    block_value = jnp.einsum(
        "hrs,shd->hrd", weights, value_heads, preferred_element_type=jnp.float32
    )
    return (block_value, peak_score, block_total)


def on_device(queries, keys, values, hidden, out_proj, ln_gain, w_router, routes, w_in, w_out):
    row_count = queries.shape[1]
    model_width = queries.shape[2]
    head_count = HEADS
    head_dim = model_width // head_count
    query_rows = queries[0]
    every_query = lax.all_gather(query_rows, "seq", axis=0, tiled=True)
    block_value, peak_score, block_total = blockwise(every_query, keys[0], values[0], head_count)
    shards = every_query.shape[0] // row_count
    block_value = block_value.reshape(head_count, shards, row_count, head_dim)
    peak_score = peak_score.reshape(head_count, shards, row_count)
    block_total = block_total.reshape(head_count, shards, row_count)
    block_value, peak_score, block_total = (
        lax.all_to_all(block_value, "seq", split_axis=1, concat_axis=1, tiled=True),
        lax.all_to_all(peak_score, "seq", split_axis=1, concat_axis=1, tiled=True),
        lax.all_to_all(block_total, "seq", split_axis=1, concat_axis=1, tiled=True),
    )
    top_peak = jnp.max(peak_score, axis=1)
    new_scale = jnp.exp(peak_score - top_peak[:, None])
    denominator = jnp.sum(new_scale * block_total, axis=1)
    numerator = jnp.sum(new_scale[..., None] * block_value, axis=1)
    attended = (
        (numerator / denominator[:, :, None])
        .transpose(1, 0, 2)
        .reshape(row_count, model_width)
        .astype(jnp.bfloat16)
    )
    projected = jnp.dot(
        attended,
        lax.all_gather(out_proj, "expert", axis=0, tiled=True),
        preferred_element_type=jnp.float32,
    )
    residual = hidden[0].astype(jnp.float32) + projected
    row_mean = jnp.mean(residual, axis=1, keepdims=True)
    centered = residual - row_mean
    row_var = jnp.mean(centered * centered, axis=1, keepdims=True)
    normed = (centered * lax.rsqrt(row_var + NORM_EPS) * ln_gain).astype(jnp.bfloat16)
    logits = jnp.dot(normed, w_router, preferred_element_type=jnp.float32)
    expert_count = w_router.shape[1]
    slot_count = 4 * row_count // expert_count
    chosen = routes[0]
    expert_ids = jnp.arange(expert_count, dtype=jnp.int32)
    pick_mask = chosen[:, :, None] == expert_ids[None, None, :]
    picked = jnp.sum(jnp.where(pick_mask, logits[:, None, :], 0.0), axis=2)
    gate_first = 1.0 / (1.0 + jnp.exp(picked[:, 1] - picked[:, 0]))
    gate_second = 1.0 / (1.0 + jnp.exp(picked[:, 0] - picked[:, 1]))
    route_flat = chosen.reshape(-1)
    one_hot = (route_flat[:, None] == expert_ids[None, :]).astype(jnp.int32)
    slot_index = jnp.sum(jnp.cumsum(one_hot, axis=0) * one_hot, axis=1) - 1
    target = route_flat * slot_count + slot_index
    place_map = (
        target[:, None] == jnp.arange(expert_count * slot_count, dtype=jnp.int32)[None, :]
    ).astype(jnp.bfloat16)
    place_map = jnp.sum(place_map.reshape(row_count, 2, expert_count * slot_count), axis=1)
    dispatch = jnp.einsum(
        "ts,td->sd", place_map, normed, preferred_element_type=jnp.float32
    ).astype(jnp.bfloat16)
    send_buf = jnp.broadcast_to(
        dispatch.reshape(expert_count, 1, slot_count, model_width),
        (expert_count, 2, slot_count, model_width),
    ).reshape(2 * expert_count, slot_count, model_width)
    arrived = lax.all_to_all(send_buf, ("seq", "expert"), split_axis=0, concat_axis=0, tiled=True)
    sources = arrived.shape[0]
    slot_dim = arrived.shape[1]
    flat_rows = arrived.reshape(sources * slot_dim, model_width)
    inner_act = jnp.maximum(
        jnp.dot(flat_rows, w_in[0], preferred_element_type=jnp.float32), 0.0
    ).astype(jnp.bfloat16)
    half_out = jnp.dot(inner_act, w_out[0], preferred_element_type=jnp.float32).astype(jnp.bfloat16)
    returned = lax.all_to_all(
        half_out.reshape(sources, slot_dim, model_width),
        ("seq", "expert"),
        split_axis=0,
        concat_axis=0,
        tiled=True,
    )
    slot_table = jnp.sum(
        returned.reshape(expert_count, 2, slot_count, model_width).astype(jnp.float32), axis=1
    )
    slot_table = slot_table.reshape(expert_count * slot_count, model_width)
    expert_out = jnp.take(slot_table, target, axis=0).reshape(row_count, 2, model_width)
    layer_out = (
        residual + gate_first[:, None] * expert_out[:, 0] + gate_second[:, None] * expert_out[:, 1]
    )
    return layer_out.astype(jnp.bfloat16)[None]


def solution(mesh):
    in_specs = (
        P("expert", "seq", None),
        P("expert", "seq", None),
        P("expert", "seq", None),
        P("expert", "seq", None),
        P("expert", None),
        P(),
        P(),
        P("expert", "seq", None),
        P(("seq", "expert"), None, None),
        P(("seq", "expert"), None, None),
    )
    out_specs = P("expert", "seq", None)
    return jax.shard_map(
        on_device, mesh=mesh, in_specs=in_specs, out_specs=out_specs, check_vma=False
    )
```

profile of v0, /device:TPU:0, one launch (start us, length us, event | category | flops | bytes accessed | tf_op | source)
XLA Modules:
  0.0 414.1 jit_solution(5017831847292280241)
XLA Ops:
  6.5 0.0 copy-start
  6.5 0.0 all-gather.6.cloned.1.call-start
  6.5 2.1 copy.83
  8.6 0.0 all-gather.6.cloned.1.call-update
  8.6 0.0 all-gather.4.cloned.1.call-start
  8.7 0.7 all-gather.4.cloned.1.call-update
  9.4 1.1 copy.105
  10.5 1.1 copy.106
  11.7 22.8 %all-gather.6.cloned.1.call-done = bf16[1,512,2048]{1,2,0:T(8,128)(2,1)} async-done(((bf16[1,128,2048]{1,2,0:T(8,128)(2,1)}), bf16[1,512,2048]{1,2,0:T(8,128)(2,1)}) %all-gather.6.cloned.1.call-update) | async-done | bytes 2097168 | tf_op jit(solution)/shard_map/all_gather | solution.py:37
  34.5 2.3 multiply_reduce_fusion.1
  36.8 0.0 copy-start.1
  36.8 2.0 copy-done.1
  38.8 0.8 convert_reduce_fusion.1
  39.6 0.6 copy_bitcast_fusion
  40.2 3.3 all-to-all-start.2
  43.5 0.6 copy_bitcast_fusion.1
  44.1 3.3 all-to-all-done.2
  47.4 3.3 all-to-all-start
  50.6 3.2 fusion.16
  53.9 2.5 copy.89
  56.4 0.0 copy-start.3
  56.4 0.0 all-to-all-done
  56.4 5.1 %all-to-all-start.1 = ((f32[16,4,128,128]{3,2,0,1:T(8,128)}), f32[16,4,128,128]{3,2,0,1:T(8,128)}, u32[]{:S(2)}, u32[]{:S(2)}) async-start(f32[16,4,128,128]{3,2,0,1:T(8,128)} %copy.89), calls=%async_computation.1 | async-start | bytes 8388608 | tf_op jit(solution)/shard_map/all_to_all | solution.py:44
  61.4 0.0 copy-done.3
  61.4 0.1 copy.93
  61.6 0.1 eq.59
  61.7 0.1 reshape_squeeze.11
  61.9 0.6 reduce-window.6
  62.4 0.0 copy-start.2
  62.4 0.2 slice_reduce_fusion
  62.7 0.1 fusion.23
  62.8 0.1 sub.48
  62.9 0.1 copy.96
  63.0 0.1 fusion.21
  63.2 46.5 %all-to-all-done.1 = f32[16,4,128,128]{3,2,0,1:T(8,128)} async-done(((f32[16,4,128,128]{3,2,0,1:T(8,128)}), f32[16,4,128,128]{3,2,0,1:T(8,128)}, u32[]{:S(2)}, u32[]{:S(2)}) %all-to-all-start.1) | async-done | bytes 4194336 | tf_op jit(solution)/shard_map/all_to_all | solution.py:44
  109.7 2.9 multiply_reduce_fusion
  112.6 0.3 fusion.14
  112.9 0.3 copy.92
  113.2 48.4 %all-gather.4.cloned.1.call-done = bf16[2048,2048]{1,0:T(8,128)(2,1)} async-done(((bf16[256,2048]{1,0:T(8,128)(2,1)}), bf16[2048,2048]{1,0:T(8,128)(2,1)}) %all-gather.4.cloned.1.call-update) | async-done | bytes 8388624 | tf_op jit(solution)/shard_map/all_gather | solution.py:60
  161.6 0.0 copy-done.2
  161.6 0.0 copy-start.4
  161.6 4.7 %fusion.26 = (f32[128]{0:T(128)S(1)}, f32[128,2048]{1,0:T(8,128)S(1)}) fusion(bf16[128,2048]{0,1:T(8,128)(2,1)S(1)} %bitcast.114, bf16[2048,2048]{1,0:T(8,128)(2,1)} %all-gather.4.cloned.1.call-done, bf16[1,128,2048]{2,1,0:T(8,128)(2,1)S(1)} %copy-done.2), kind=kOutput, calls=%fused_computation.60 | convolution fusion | flops 1074528128 | bytes 10486272 | tf_op jit(solution)/shard_map/dot_general | solution.py:58
  166.4 0.3 multiply_reduce_fusion.2
  166.6 0.0 copy-done.4
  166.6 0.2 multiply_convert_fusion
  166.8 0.7 convolution_convert_fusion
  167.6 0.5 broadcast_in_dim.50
  168.1 97.7 %all_to_all.25 = bf16[32,32,2048]{2,1,0:T(8,128)(2,1)} all-to-all(bf16[32,32,2048]{2,1,0:T(8,128)(2,1)S(1)} %bitcast.110), channel_id=1, replica_groups=mesh['seq'=4,'expert'=8] {'seq','expert'}, dimensions={0} | all-to-all | bytes 8388608 | tf_op jit(solution)/shard_map/all_to_all | solution.py:92
  265.8 25.4 %fusion.6 = bf16[1024,2048]{1,0:T(8,128)(2,1)} fusion(bf16[1,2048,2048]{2,1,0:T(8,128)(2,1)} %param.19, bf16[1024,2048]{1,0:T(8,128)(2,1)} %bitcast.113, bf16[1,2048,2048]{2,1,0:T(8,128)(2,1)} %param.18), kind=kOutput, calls=%fused_computation.11 | convolution fusion | flops 17186160640 | bytes 25165824 | tf_op jit(solution)/shard_map/dot_general | solution.py:99
  291.2 3.6 all-to-all-start.4
  294.8 0.1 copy.97
  294.9 0.1 mul.102
  295.1 0.0 copy-done
  295.1 0.2 fusion.27
  295.4 95.4 %all-to-all-done.4 = bf16[32,32,2048]{2,1,0:T(8,128)(2,1)} async-done(((bf16[32,32,2048]{2,1,0:T(8,128)(2,1)}), bf16[32,32,2048]{2,1,0:T(8,128)(2,1)}, u32[]{:S(2)}, u32[]{:S(2)}) %all-to-all-start.4) | async-done | bytes 4194336 | tf_op jit(solution)/shard_map/all_to_all | solution.py:100
  390.8 5.6 %convert_reduce_fusion = f32[16,32,2048]{2,1,0:T(8,128)} fusion(bf16[32,32,2048]{2,1,0:T(8,128)(2,1)} %all-to-all-done.4), kind=kLoop, calls=%fused_computation.1 | loop fusion | flops 3145728 | bytes 8388608 | tf_op jit(solution)/shard_map/reduce_sum | solution.py:107
  396.3 4.6 %gather_fusion = f32[256,2048]{1,0:T(8,128)S(1)} fusion(f32[512,2048]{1,0:T(8,128)} %bitcast.108, s32[1024]{0:T(1024)S(1)} %pad_clamp_fusion), kind=kCustom, calls=%fused_computation | custom fusion | bytes 4195328 | tf_op jit(solution)/shard_map/jit(_take)/gather | solution.py:111
  400.9 2.3 gather.7
  403.2 3.0 copy_select_fusion
  406.2 1.1 fusion.15
  (14 shorter events, 0.2 us)
Async XLA Ops:
  6.5 288.6 %copy-start = (bf16[2048,16]{0,1:T(8,128)(2,1)S(1)}, bf16[2048,16]{0,1:T(8,128)(2,1)}, u32[]{:S(2)}) copy-start(bf16[2048,16]{0,1:T(8,128)(2,1)} %param.16) | copy-start | bytes 196612
  6.5 27.9 %all-gather.6.cloned.1.call-start = ((), (), s32[]{:S(2)}) async-start(), calls=%async_computation.6 | async-start | bytes 2621440 | tf_op jit(solution)/shard_map/all_gather | solution.py:37
  8.6 153.0 %all-gather.4.cloned.1.call-start = ((), (), s32[]{:S(2)}) async-start(), calls=%async_computation.5 | async-start | bytes 9437184 | tf_op jit(solution)/shard_map/all_gather | solution.py:60
  36.8 2.0 copy-start.1
  40.2 7.2 %all-to-all-start.2 = ((f32[16,4,128]{2,0,1:T(8,128)}), f32[16,4,128]{2,0,1:T(8,128)S(1)}, u32[]{:S(2)}, u32[]{:S(2)}) async-start(f32[16,4,128]{2,0,1:T(8,128)} %copy_bitcast_fusion), calls=%async_computation.2 | async-start | bytes 65536 | tf_op jit(solution)/shard_map/all_to_all | solution.py:46
  47.4 9.0 %all-to-all-start = ((f32[16,4,128]{2,0,1:T(8,128)}), f32[16,4,128]{2,0,1:T(8,128)S(1)}, u32[]{:S(2)}, u32[]{:S(2)}) async-start(f32[16,4,128]{2,0,1:T(8,128)} %copy_bitcast_fusion.1), calls=%async_computation | async-start | bytes 65536 | tf_op jit(solution)/shard_map/all_to_all | solution.py:45
  56.4 5.1 %copy-start.3 = (s32[1,128,2]{1,2,0:T(2,128)S(1)}, s32[1,128,2]{1,2,0:T(2,128)}, u32[]{:S(2)}) copy-start(s32[1,128,2]{1,2,0:T(2,128)} %param.17) | copy-start | bytes 3076
  56.4 53.3 %all-to-all-start.1 = ((f32[16,4,128,128]{3,2,0,1:T(8,128)}), f32[16,4,128,128]{3,2,0,1:T(8,128)}, u32[]{:S(2)}, u32[]{:S(2)}) async-start(f32[16,4,128,128]{3,2,0,1:T(8,128)} %copy.89), calls=%async_computation.1 | async-start | bytes 8388608 | tf_op jit(solution)/shard_map/all_to_all | solution.py:44
  62.4 99.2 %copy-start.2 = (bf16[1,128,2048]{2,1,0:T(8,128)(2,1)S(1)}, bf16[1,128,2048]{2,1,0:T(8,128)(2,1)}, u32[]{:S(2)}) copy-start(bf16[1,128,2048]{2,1,0:T(8,128)(2,1)} %param.13) | copy-start | bytes 1572868
  161.6 5.0 %copy-start.4 = (f32[2048]{0:T(1024)S(1)}, f32[2048]{0:T(1024)}, u32[]{:S(2)}) copy-start(f32[2048]{0:T(1024)} %param.15) | copy-start | bytes 24580
  291.2 99.5 %all-to-all-start.4 = ((bf16[32,32,2048]{2,1,0:T(8,128)(2,1)}), bf16[32,32,2048]{2,1,0:T(8,128)(2,1)}, u32[]{:S(2)}, u32[]{:S(2)}) async-start(bf16[32,32,2048]{2,1,0:T(8,128)(2,1)} %bitcast.112), calls=%async_computation.4 | async-start | bytes 8388608 | tf_op jit(solution)/shard_map/all_to_all | solution.py:100
Sparse Core Ops, SparseCore 0:
  8.9 25.5 all-gather.5
  36.6 124.9 all-gather.3
where the time goes:
time: 415 us; the launch traced here: 414 us
  waiting for transfers between devices  217 us (52%)
  blocking collectives  97.7 us (24%)
  matrix products  36.7 us (9%)
  local copies, waits for them, and re-layouts  18.8 us (5%)
  starting transfers between devices  15.2 us (4%)
  other arithmetic  15.1 us (4%)
  between operations  13.6 us (3%)
    all_to_all x1, blocking collectives, on_device(): lax.all_to_all(send_buf, ('seq', 'expert'), split_axis=0, concat_axis=0,...  97.7 us
    all_to_all x1, waiting for transfers between devices, on_device(): lax.all_to_all(half_out.reshape(sources, slot_dim, model_width), ('seq',...  95.4 us
    all_gather x1, waiting for transfers between devices, on_device(): lax.all_gather(out_proj, 'expert', axis=0, tiled=True)  48.4 us
    all_to_all x1, waiting for transfers between devices, on_device(): lax.all_to_all(block_value, 'seq', split_axis=1, concat_axis=1, tiled=True)  46.5 us
    dot_general x1, matrix products, on_device(): jnp.dot(inner_act, w_out[0], preferred_element_type=jnp.float32)  25.4 us
    all_gather x1, waiting for transfers between devices, on_device(): every_query = lax.all_gather(query_rows, 'seq', axis=0, tiled=True)  22.8 us
  transfers between devices with their start and end apart: 6, of which 5 were waited for; matrix products, arithmetic and copies ran while one was open for 4% of the time, Pallas kernels for 0%

commit v1 on v0

v1 whole, which is shorter than its diff:
```python
import functools

import jax
import jax.numpy as jnp
from jax import lax
from jax.experimental import pallas as pl
from jax.experimental.pallas import tpu as pltpu
from jax.sharding import PartitionSpec as P

HEADS = 16
HALVES = 2


NORM_EPS = 1e-05


def line_ring(count):
    return [0] + list(range(1, count, 2)) + [i for i in range(count - 1, 0, -1) if i % 2 == 0]


def swap_pairs(count, offset):
    return [(i, i ^ offset) for i in range(count)]


def after(block, earlier):
    return lax.optimization_barrier((block, *earlier))[0] if earlier else block


def attention_kernel(block_count, head_dim, *refs):
    query_ref, key_refs = refs[0], refs[1 : 1 + block_count]
    value_refs, out_ref = refs[1 + block_count : 1 + 2 * block_count], refs[-1]
    source_count = key_refs[0].shape[0]
    heads = [
        slice(at * head_dim, (at + 1) * head_dim) for at in range(query_ref.shape[1] // head_dim)
    ]
    ones = jnp.ones((source_count, head_dim), jnp.bfloat16)
    scores = [
        [
            lax.dot_general(
                query_ref[:, head],
                key_ref[:, head],
                (((1,), (1,)), ((), ())),
                preferred_element_type=jnp.float32,
            )
            for key_ref in key_refs
        ]
        for head in heads
    ]
    tops = [
        jnp.max(functools.reduce(jnp.maximum, blocks), axis=1, keepdims=True) for blocks in scores
    ]
    weights = [
        [jnp.exp((block - top) * head_dim ** (-0.5)).astype(jnp.bfloat16) for block in blocks]
        for blocks, top in zip(scores, tops)
    ]
    for head, blocks in zip(heads, weights):
        sums = sum(
            jnp.dot(
                block,
                jnp.concatenate([value_ref[:, head], ones], axis=1),
                preferred_element_type=jnp.float32,
            )
            for block, value_ref in zip(blocks, value_refs)
        )
        out_ref[:, head] = (sums[:, :head_dim] / sums[:, head_dim:]).astype(out_ref.dtype)


VMEM_BYTES = 56 * 1024 * 1024


def attention(query_rows, key_blocks, value_blocks, head_count, earlier):
    row_count, model_width = query_rows.shape
    head_dim = model_width // head_count
    width = model_width // 4
    operands = [query_rows, *key_blocks, *value_blocks]
    return pl.pallas_call(
        functools.partial(attention_kernel, len(key_blocks), head_dim),
        grid=(model_width // width,),
        in_specs=[pl.BlockSpec((block.shape[0], width), lambda i: (0, i)) for block in operands]
        + [pl.BlockSpec(memory_space=pl.ANY) for _ in earlier],
        out_specs=pl.BlockSpec((row_count, width), lambda i: (0, i)),
        out_shape=jax.ShapeDtypeStruct((row_count, model_width), jnp.bfloat16),
        compiler_params=pltpu.CompilerParams(vmem_limit_bytes=VMEM_BYTES),
        cost_estimate=pl.CostEstimate(flops=1000, bytes_accessed=1000, transcendentals=0),
    )(*operands, *earlier)


def expert_kernel(own_ref, other_ref, first_ref, second_ref, *refs):
    own_out, other_out, rows, inner, outs, first, second, weight_sems, row_sems, out_sems = refs[-10:]
    count = own_ref.shape[0]
    tile = first.shape[1] // 2

    def columns(at):
        return pl.ds(at * tile, tile)

    weight_copies = [
        pltpu.make_async_copy(
            source.at[:, columns(at)], held.at[:, columns(at)], weight_sems.at[2 * which + at]
        )
        for which, (source, held) in enumerate(((first_ref, first), (second_ref, second)))
        for at in range(2)
    ]
    row_copies = [
        pltpu.make_async_copy(own_ref, rows.at[:count], row_sems.at[0]),
        pltpu.make_async_copy(other_ref, rows.at[count:], row_sems.at[1]),
    ]
    out_copies = [
        pltpu.make_async_copy(
            outs.at[which * count : (which + 1) * count, columns(at)],
            target.at[:, columns(at)],
            out_sems.at[2 * at + which],
        )
        for at in range(2)
        for which, target in enumerate((own_out, other_out))
    ]
    for copy in row_copies + weight_copies[:2]:
        copy.start()
    for copy in row_copies:
        copy.wait()
    for at in range(2):
        weight_copies[2 + at].start()
        weight_copies[at].wait()
        act = jnp.dot(rows[...], first[:, columns(at)], preferred_element_type=jnp.float32)
        inner[:, columns(at)] = jnp.maximum(act, 0.0).astype(inner.dtype)
    for at in range(2):
        weight_copies[2 + at].wait()
        outs[:, columns(at)] = jnp.dot(
            inner[...], second[:, columns(at)], preferred_element_type=jnp.float32
        ).astype(outs.dtype)
        for copy in out_copies[2 * at : 2 * at + 2]:
            copy.start()
    for copy in out_copies:
        copy.wait()


def expert_half(own_rows, other_rows, first, second, earlier):
    count, model_width = own_rows.shape
    hidden_width = first.shape[1]
    out_type = jax.ShapeDtypeStruct((count, model_width), jnp.bfloat16)
    anywhere = pl.BlockSpec(memory_space=pl.ANY)
    return pl.pallas_call(
        expert_kernel,
        in_specs=[anywhere] * (4 + len(earlier)),
        out_specs=[anywhere, anywhere],
        out_shape=[out_type, out_type],
        scratch_shapes=[
            pltpu.VMEM((2 * count, model_width), jnp.bfloat16),
            pltpu.VMEM((2 * count, hidden_width), jnp.bfloat16),
            pltpu.VMEM((2 * count, model_width), jnp.bfloat16),
            pltpu.VMEM(first.shape, jnp.bfloat16),
            pltpu.VMEM(second.shape, jnp.bfloat16),
            pltpu.SemaphoreType.DMA((4,)),
            pltpu.SemaphoreType.DMA((2,)),
            pltpu.SemaphoreType.DMA((4,)),
        ],
        compiler_params=pltpu.CompilerParams(vmem_limit_bytes=VMEM_BYTES),
        cost_estimate=pl.CostEstimate(flops=1000, bytes_accessed=1000, transcendentals=0),
    )(own_rows, other_rows, first, second, *earlier)


def on_device(
    seq_count, expert_dev, queries, keys, values, hidden, out_proj, ln_gain, w_router, routes, w_in, w_out
):
    row_count, model_width = queries.shape[1:]
    expert_count = w_router.shape[1]
    slot_count = 4 * row_count // expert_count
    planes = expert_dev // HALVES
    seq_at = lax.axis_index("seq")
    expert_at = lax.axis_index("expert")
    plane, half = expert_at // HALVES, expert_at % HALVES
    core = seq_at % 2

    ring = line_ring(planes)
    ring_pairs = [
        [
            (ring[i] * HALVES + j, ring[(i + hop) % planes] * HALVES + j)
            for i in range(planes)
            for j in range(HALVES)
        ]
        for hop in range(planes)
    ]
    place_of = {ring[i]: i for i in range(planes)}
    source_plane = [
        sum(
            jnp.where(plane == i, ring[(place_of[i] - step) % planes], 0) for i in range(planes)
        )
        for step in range(planes)
    ]
    half_pairs = swap_pairs(expert_dev, 1)
    core_pairs = swap_pairs(seq_count, 1)

    def around(block, hop=1):
        with jax.named_scope("ring"):
            return lax.ppermute(block, "expert", ring_pairs[hop])

    def other_half(block):
        with jax.named_scope("half"):
            return lax.ppermute(block, "expert", half_pairs)

    def other_core(block):
        with jax.named_scope("core"):
            return lax.ppermute(block, "seq", core_pairs)

    chosen = routes[0].reshape(-1)
    expert_ids = jnp.arange(expert_count, dtype=jnp.int32)
    one_hot = (chosen[:, None] == expert_ids[None, :]).astype(jnp.int32)
    slot_index = jnp.sum(jnp.cumsum(one_hot, axis=0) * one_hot, axis=1) - 1
    target = (chosen * slot_count + slot_index).reshape(row_count, 2)

    depth = out_proj.shape[0]
    half_width = model_width // 2
    proj_part = lax.dynamic_slice_in_dim(out_proj, core * half_width, half_width, axis=1)
    proj_blocks, proj_others = [proj_part], []
    sources = [keys[0], values[0], target.T]
    gathered = [[source] + [None] * (seq_count - 1) for source in sources[:2]]
    hops = [(which, across) for which in range(2) for across in range(2, seq_count, 2)]
    for step in range(max(planes - 1, len(hops))):
        with jax.named_scope(f"gather_{step}"):
            arrived = []
            if step < planes - 1:
                arrived = [other_half(proj_blocks[step]), around(proj_blocks[step])]
            if step < len(hops):
                which, across = hops[step]
                arrived.append(
                    lax.ppermute(sources[which], "seq", swap_pairs(seq_count, across))
                )
            *sources, = lax.optimization_barrier((*sources, *arrived))
            sources, arrived = sources[:3], sources[3:]
            if step < planes - 1:
                proj_others.append(arrived[0])
                proj_blocks.append(arrived[1])
            if step < len(hops):
                gathered[which][across] = arrived[-1]
            if step == 0:
                targets = [target.T] + [around(sources[2], hop) for hop in range(1, planes)]
    depth_cut = depth // 2 if planes > 1 else depth
    last_other = [other_half(proj_blocks[-1][:depth_cut])]
    if planes > 1:
        last_other.append(around(proj_others[-1][depth_cut:]))
    for blocks in gathered:
        for across in range(0, seq_count, 2):
            blocks[across + 1] = other_core(blocks[across])
    key_blocks, value_blocks = gathered
    attended = attention(
        queries[0], key_blocks, value_blocks, HEADS, []
    )
    both_attended = jnp.concatenate([attended, other_core(attended)], axis=0)
    projected = 0.0
    for step in range(planes):
        own_at = source_plane[step] * HALVES + half
        other_at = source_plane[step] * HALVES + (1 - half)
        pieces = [(own_at * depth, proj_blocks[step])]
        if step < planes - 1:
            pieces.append((other_at * depth, proj_others[step]))
        else:
            pieces += [
                (other_at * depth + cut, block)
                for cut, block in zip((0, depth_cut), last_other)
            ]
        for at, block in pieces:
            columns = lax.dynamic_slice_in_dim(both_attended, at, block.shape[0], axis=1)
            projected = projected + jnp.dot(columns, block, preferred_element_type=jnp.float32)
    mine, theirs = projected[:row_count], other_core(projected[row_count:])
    projected = jnp.concatenate(
        [jnp.where(core == 0, mine, theirs), jnp.where(core == 0, theirs, mine)], axis=1
    )

    residual = hidden[0].astype(jnp.float32) + projected
    row_mean = jnp.mean(residual, axis=1, keepdims=True)
    centered = residual - row_mean
    row_var = jnp.mean(centered * centered, axis=1, keepdims=True)
    normed = (centered * lax.rsqrt(row_var + NORM_EPS) * ln_gain).astype(jnp.bfloat16)

    block_rows = seq_count * slot_count
    pair_rows = 2 * slot_count
    slot_ids = jnp.arange(block_rows, dtype=jnp.int32)
    served = jnp.bitwise_xor(slot_ids // slot_count, seq_at) * planes + plane
    served_target = served * slot_count + slot_ids % slot_count

    def exchange(rows):
        parts = [rows[i * slot_count : (i + 1) * slot_count] for i in range(seq_count)]
        for i in range(1, seq_count):
            parts[i] = lax.ppermute(parts[i], "seq", swap_pairs(seq_count, i))
        return jnp.concatenate(parts, axis=0)

    with jax.named_scope("tokens"):
        blocks = [normed]
        for _ in range(1, planes):
            blocks.append(around(blocks[-1]))

    def around_add(passing, part):
        with jax.named_scope("back_home"):
            if passing is not None:
                part = part + around(passing).astype(jnp.float32)
            return part.astype(jnp.bfloat16)

    matches, slot_rows, other_rows = [], [], []
    for step in range(planes):
        with jax.named_scope(f"out_{step}"):
            target = targets[step].T
            matches.append([target[:, k : k + 1] == served_target[None, :] for k in range(2)])
            place_map = (matches[step][0] | matches[step][1]).astype(jnp.bfloat16)
            slots = jnp.einsum(
                "ts,td->sd", place_map, blocks[step], preferred_element_type=jnp.float32
            ).astype(jnp.bfloat16)
            slot_rows.append(exchange(slots))
            other_rows.append(other_half(slot_rows[step]))

    def expert_step(step, earlier):
        with jax.named_scope(f"expert_{step}"):
            return expert_half(slot_rows[step], other_rows[step], w_in[0], w_out[0], earlier)

    def combine(step, outs, later):
        with jax.named_scope(f"back_{step}"):
            own_out, other_out = outs
            own_out = after(own_out, later)
            out_sum = own_out.astype(jnp.float32) + other_half(other_out).astype(jnp.float32)
            returned = exchange(out_sum.astype(jnp.bfloat16))
            logits = jnp.dot(blocks[step], w_router, preferred_element_type=jnp.float32)
            named = (targets[step].T // slot_count)[:, :, None] == expert_ids[None, None, :]
            picked = jnp.sum(jnp.where(named, logits[:, None, :], 0.0), axis=2)
            gate_first = 1.0 / (1.0 + jnp.exp(picked[:, 1:2] - picked[:, 0:1]))
            gate_second = 1.0 / (1.0 + jnp.exp(picked[:, 0:1] - picked[:, 1:2]))
            gate_map = jnp.where(matches[step][0], gate_first, 0.0) + jnp.where(
                matches[step][1], gate_second, 0.0
            )
            gate_high = gate_map.astype(jnp.bfloat16)
            gate_low = (gate_map - gate_high.astype(jnp.float32)).astype(jnp.bfloat16)
            return jnp.dot(gate_high, returned, preferred_element_type=jnp.float32) + jnp.dot(
                gate_low, returned, preferred_element_type=jnp.float32
            )

    outs = [None] * planes
    passing, waiting = None, []
    for step in range(1, planes):
        ahead = slot_rows[step + 1 : step + 2]
        outs[step] = expert_step(step, ahead + other_rows[:1] if step == 1 else ahead)
        if step > 1:
            later = [outs[step][0], *other_rows[step + 1 : step + 2]]
            passing = around_add(passing, combine(step - 1, outs[step - 1], later))
            waiting = waiting or [passing]
    outs[0] = expert_step(0, waiting + [outs[-1][1]])
    if planes > 1:
        passing = around_add(passing, combine(planes - 1, outs[-1], outs[0][:1]))
    layer_out = residual + combine(0, outs[0], [])
    if planes > 1:
        layer_out = layer_out + around(passing).astype(jnp.float32)
    return layer_out.astype(jnp.bfloat16)[None]


def solution(mesh):
    seq_count, expert_dev = mesh.shape["seq"], mesh.shape["expert"]
    in_specs = (
        P("expert", "seq", None),
        P("expert", "seq", None),
        P("expert", "seq", None),
        P("expert", "seq", None),
        P("expert", None),
        P(),
        P(),
        P("expert", "seq", None),
        P(("seq", "expert"), None, None),
        P(("seq", "expert"), None, None),
    )
    out_specs = P("expert", "seq", None)

    def device_part(*arrays):
        return on_device(seq_count, expert_dev, *arrays)

    return jax.shard_map(
        device_part, mesh=mesh, in_specs=in_specs, out_specs=out_specs, check_vma=False
    )
```

time: 415 us -> 218 us (0.53)
  waiting for transfers between devices: 217 us -> 104 us
  blocking collectives: 97.7 us -> 0 us
  Pallas kernels: 0 us -> 40.7 us
  starting transfers between devices: 15.2 us -> 49.1 us
  matrix products: 36.7 us -> 13.5 us
  between operations: 13.6 us -> 0.79 us
  other arithmetic: 15.1 us -> 2.54 us
  local copies, waits for them, and re-layouts: 18.8 us -> 6.39 us
    all_to_all x4 -> x0, waiting for transfers between devices: 145 us -> none  [the longest x1 95.4 us: on_device(): lax.all_to_all(half_out.reshape(sources, slot_dim, model_width), ('seq',...]
    ppermute x0 -> x57, waiting for transfers between devices: none -> 104 us  [the longest x13 53 us: around(): return lax.ppermute(block, 'expert', ring_pairs[hop])]
    all_to_all x1 -> x0, blocking collectives: 97.7 us -> none  [on_device(): lax.all_to_all(send_buf, ('seq', 'expert'), split_axis=0, concat_axis=0,...]
    all_gather x2 -> x0, waiting for transfers between devices: 71.1 us -> none  [the longest x1 48.4 us: on_device(): lax.all_gather(out_proj, 'expert', axis=0, tiled=True)]
    ppermute x0 -> x57, starting transfers between devices: none -> 49.1 us  [the longest x13 16.3 us: around(): return lax.ppermute(block, 'expert', ring_pairs[hop])]
    pallas_call x0 -> x5, Pallas kernels: none -> 40.7 us  [the longest x4 34.6 us: expert_half(): pl.pallas_call(expert_kernel, in_specs=[anywhere] * (4 + len(earlier)), o...]
    dot_general x6 -> x25, matrix products: 36.7 us -> 13.5 us  [the longest x9 7.03 us: on_device(): jnp.dot(columns, block, preferred_element_type=jnp.float32)]
    all_to_all x4 -> x0, starting transfers between devices: 15.1 us -> none  [the longest x1 5.05 us: on_device(): lax.all_to_all(block_value, 'seq', split_axis=1, concat_axis=1, tiled=True)]
  transfers between devices with their start and end apart: 6 -> 57, of which waited for: 5 -> 29; matrix products, arithmetic and copies ran while one was open for 4% -> 8% of each run, Pallas kernels for 0% -> 19%
where the time goes in v1:
time: 218 us; the launch traced here: 217 us
  waiting for transfers between devices  104 us (48%)
  starting transfers between devices  49.1 us (23%)
  Pallas kernels  40.7 us (19%)
  matrix products  13.5 us (6%)
  local copies, waits for them, and re-layouts  6.39 us (3%)
  other arithmetic  2.54 us (1%)
    ppermute x13, waiting for transfers between devices, around(): return lax.ppermute(block, 'expert', ring_pairs[hop])  53 us
    pallas_call x4, Pallas kernels, expert_half(): pl.pallas_call(expert_kernel, in_specs=[anywhere] * (4 + len(earlier)), o...  34.6 us
    ppermute x24, waiting for transfers between devices, exchange(): parts[i] = lax.ppermute(parts[i], 'seq', swap_pairs(seq_count, i))  21.8 us
    ppermute x12, waiting for transfers between devices, other_half(): return lax.ppermute(block, 'expert', half_pairs)  20 us
    ppermute x13, starting transfers between devices, around(): return lax.ppermute(block, 'expert', ring_pairs[hop])  16.3 us
    ppermute x24, starting transfers between devices, exchange(): parts[i] = lax.ppermute(parts[i], 'seq', swap_pairs(seq_count, i))  14.7 us
    ppermute x12, starting transfers between devices, other_half(): return lax.ppermute(block, 'expert', half_pairs)  14.5 us
    ppermute x2, waiting for transfers between devices, on_device(): lax.ppermute(sources[which], 'seq', swap_pairs(seq_count, across))  8.38 us
  transfers between devices with their start and end apart: 57, of which 29 were waited for; matrix products, arithmetic and copies ran while one was open for 8% of the time, Pallas kernels for 19%

profile of v1, /device:TPU:0, one launch (start us, length us, event | category | flops | bytes accessed | tf_op | source)
XLA Modules:
  0.0 217.3 jit_solution(3488099306681618537)
XLA Ops:
  0.0 1.2 copy-done
  1.3 3.1 %collective-permute-start.2 = (bf16[256,1024]{1,0:T(8,128)(2,1)S(1)}, bf16[256,1024]{1,0:T(8,128)(2,1)}, u32[]{:S(2)}, u32[]{:S(2)}) collective-permute-start(bf16[256,1024]{1,0:T(8,128)(2,1)S(1)} %constant_dynamic-slice_fusion), channel_id=1, source_target_pairs={{0,2},{1,3},{2,6},{3,7},{6,4},{7,5},{4,0},{5,1},{8,10},{9,11},{10,... | collective-permute-start | bytes 1572872 | tf_op jit(solution)/shard_map/gather_0/ring/ppermute | solution.py:194
  4.3 1.5 collective-permute-start.1
  5.9 1.5 collective-permute-start.3
  9.6 7.8 %collective-permute-done.2 = bf16[256,1024]{1,0:T(8,128)(2,1)} collective-permute-done((bf16[256,1024]{1,0:T(8,128)(2,1)S(1)}, bf16[256,1024]{1,0:T(8,128)(2,1)}, u32[]{:S(2)}, u32[]{:S(2)}) %collective-permute-start.2) | collective-permute-done | bytes 524320 | tf_op jit(solution)/shard_map/gather_0/ring/ppermute | solution.py:194
  17.7 1.4 collective-permute-done.3.refs_3_
  19.2 1.5 collective-permute-start.8
  20.7 2.6 %collective-permute-start.7 = (bf16[256,1024]{1,0:T(8,128)(2,1)}, bf16[256,1024]{1,0:T(8,128)(2,1)}, u32[]{:S(2)}, u32[]{:S(2)}) collective-permute-start(bf16[256,1024]{1,0:T(8,128)(2,1)} %collective-permute-done.2), channel_id=1, source_target_pairs={{0,2},{1,3},{2,6},{3,7},{6,4},{7,5},{4,0},{5,1},{8,10},{9,11},{10,... | collective-permute-start | bytes 1572872 | tf_op jit(solution)/shard_map/gather_1/ring/ppermute | solution.py:194
  24.7 6.9 %collective-permute-done.8.refs_7_ = bf16[128,2048]{1,0:T(8,128)(2,1)S(1)} collective-permute-done((bf16[128,2048]{1,0:T(8,128)(2,1)}, bf16[128,2048]{1,0:T(8,128)(2,1)S(1)}, u32[]{:S(2)}, u32[]{:S(2)}) %collective-permute-start.8) | collective-permute-done | bytes 524320 | tf_op jit(solution)/shard_map/gather_1/ppermute | solution.py:225
  31.6 2.2 %collective-permute-done.7 = bf16[256,1024]{1,0:T(8,128)(2,1)} collective-permute-done((bf16[256,1024]{1,0:T(8,128)(2,1)}, bf16[256,1024]{1,0:T(8,128)(2,1)}, u32[]{:S(2)}, u32[]{:S(2)}) %collective-permute-start.7) | collective-permute-done | bytes 524320 | tf_op jit(solution)/shard_map/gather_1/ring/ppermute | solution.py:194
  33.8 1.4 collective-permute-done.6
  35.4 1.3 collective-permute-start.12
  36.7 1.5 collective-permute-start.11
  38.3 6.1 %shard_map.100 = bf16[128,2048]{1,0:T(8,128)(2,1)} custom-call(bf16[128,2048]{1,0:T(8,128)(2,1)} %bitcast.94, bf16[128,2048]{1,0:T(8,128)(2,1)} %bitcast.97, bf16[128,2048]{1,0:T(8,128)(2,1)} %copy-done.12, bf16[128,2048]{1,0:T(8,128)(2,1)} %copy-done.10, bf16[128,2048]{1,0:T(8,128)(2,1)} %collective-permute-done.4.refs_4_, bf16[128,2048]{1,0:T(8,128)(2,1)} %bitcast.100, ...), custom_call_target="tpu_custom_call" | custom-call | flops 1000 | bytes 1000 | tf_op jit(solution)/shard_map/pallas_call | solution.py:76
  44.5 1.4 collective-permute-start.32
  45.9 2.3 %collective-permute-start.26 = (s32[2,128]{0,1:T(8,128)S(1)}, s32[2,128]{0,1:T(8,128)S(1)}, u32[]{:S(2)}, u32[]{:S(2)}) collective-permute-start(s32[2,128]{0,1:T(8,128)S(1)} %bitcast.92), channel_id=1, source_target_pairs={{0,6},{1,7},{2,4},{3,5},{6,0},{7,1},{4,2},{5,3},{8,14},{9,15},{10,... | collective-permute-start | bytes 3080 | tf_op jit(solution)/shard_map/gather_0/ring/ppermute | solution.py:194
  48.2 3.5 %collective-permute-done.32 = s32[2,128]{0,1:T(8,128)S(1)} collective-permute-done((s32[2,128]{0,1:T(8,128)S(1)}, s32[2,128]{0,1:T(8,128)S(1)}, u32[]{:S(2)}, u32[]{:S(2)}) %collective-permute-start.32) | collective-permute-done | bytes 1056 | tf_op jit(solution)/shard_map/gather_0/ring/ppermute | solution.py:194
  53.1 1.0 collective-permute-done.12
  54.2 1.2 collective-permute-start.13
  55.4 1.7 collective-permute-start.14
  57.1 1.4 fusion.26
  58.5 1.4 fusion.30
  59.9 1.2 fusion.32
  62.1 1.4 fusion.28
  65.5 1.2 collective-permute-done.15
  67.6 1.8 collective-permute-start.21
  69.9 1.5 collective-permute-start.17
  72.0 3.6 %collective-permute-done.18 = bf16[32,2048]{1,0:T(8,128)(2,1)S(1)} collective-permute-done((bf16[32,2048]{1,0:T(8,128)(2,1)S(1)}, bf16[32,2048]{1,0:T(8,128)(2,1)S(1)}, u32[]{:S(2)}, u32[]{:S(2)}) %collective-permute-start.18) | collective-permute-done | bytes 131104 | tf_op jit(solution)/shard_map/out_0/ppermute | solution.py:283
  75.7 2.8 %collective-permute-done.17 = bf16[32,2048]{1,0:T(8,128)(2,1)S(1)} collective-permute-done((bf16[32,2048]{1,0:T(8,128)(2,1)S(1)}, bf16[32,2048]{1,0:T(8,128)(2,1)S(1)}, u32[]{:S(2)}, u32[]{:S(2)}) %collective-permute-start.17) | collective-permute-done | bytes 131104 | tf_op jit(solution)/shard_map/out_0/ppermute | solution.py:283
  78.6 1.2 collective-permute-start.19
  79.8 2.7 %collective-permute-done.21 = bf16[128,2048]{1,0:T(8,128)(2,1)S(1)} collective-permute-done((bf16[128,2048]{1,0:T(8,128)(2,1)S(1)}, bf16[128,2048]{1,0:T(8,128)(2,1)S(1)}, u32[]{:S(2)}, u32[]{:S(2)}) %collective-permute-start.21) | collective-permute-done | bytes 524320 | tf_op jit(solution)/shard_map/tokens/ring/ppermute | solution.py:194
  83.0 0.9 collective-permute-start.23
  86.0 2.7 %collective-permute-done.24 = bf16[32,2048]{1,0:T(8,128)(2,1)S(1)} collective-permute-done((bf16[32,2048]{1,0:T(8,128)(2,1)S(1)}, bf16[32,2048]{1,0:T(8,128)(2,1)S(1)}, u32[]{:S(2)}, u32[]{:S(2)}) %collective-permute-start.24) | collective-permute-done | bytes 131104 | tf_op jit(solution)/shard_map/out_1/ppermute | solution.py:283
  88.7 1.9 collective-permute-done.23
  90.7 1.7 collective-permute-start.25
  92.4 7.5 %collective-permute-done.27 = bf16[128,2048]{1,0:T(8,128)(2,1)S(1)} collective-permute-done((bf16[128,2048]{1,0:T(8,128)(2,1)S(1)}, bf16[128,2048]{1,0:T(8,128)(2,1)S(1)}, u32[]{:S(2)}, u32[]{:S(2)}) %collective-permute-start.27) | collective-permute-done | bytes 524320 | tf_op jit(solution)/shard_map/tokens/ring/ppermute | solution.py:194
  101.5 15.3 %collective-permute-done.33 = bf16[128,2048]{1,0:T(8,128)(2,1)S(1)} collective-permute-done((bf16[128,2048]{1,0:T(8,128)(2,1)S(1)}, bf16[128,2048]{1,0:T(8,128)(2,1)S(1)}, u32[]{:S(2)}, u32[]{:S(2)}) %collective-permute-start.33) | collective-permute-done | bytes 524320 | tf_op jit(solution)/shard_map/tokens/ring/ppermute | solution.py:194
  117.4 0.9 collective-permute-start.36
  118.4 1.2 collective-permute-start.35
  119.6 1.1 collective-permute-start.31
  121.5 8.6 %expert_1.1 = (bf16[128,2048]{1,0:T(8,128)(2,1)}, bf16[128,2048]{1,0:T(8,128)(2,1)}) custom-call(bf16[128,2048]{1,0:T(8,128)(2,1)} %copy-done.8, bf16[128,2048]{1,0:T(8,128)(2,1)} %copy-done.13, bf16[2048,2048]{1,0:T(8,128)(2,1)} %bitcast.80, bf16[2048,2048]{1,0:T(8,128)(2,1)} %bitcast.84, bf16[128,2048]{1,0:T(8,128)(2,1)} %copy-done.5, ...), custom_call_target="tpu_custom_call" | custom-call | flops 1000 | bytes 1000 | tf_op jit(solution)/shard_map/expert_1/pallas_call | solution.py:141
  130.1 1.1 collective-permute-start.38
  131.3 1.1 collective-permute-start.37
  132.6 1.8 collective-permute-done.31.other_ref
  135.2 8.6 %expert_2.1 = (bf16[128,2048]{1,0:T(8,128)(2,1)}, bf16[128,2048]{1,0:T(8,128)(2,1)}) custom-call(bf16[128,2048]{1,0:T(8,128)(2,1)} %copy-done.5, bf16[128,2048]{1,0:T(8,128)(2,1)} %copy-done.19, bf16[2048,2048]{1,0:T(8,128)(2,1)} %bitcast.81, bf16[2048,2048]{1,0:T(8,128)(2,1)} %bitcast.85, bf16[128,2048]{1,0:T(8,128)(2,1)} %copy-done.4), custom_call_target="tpu_custom_call" | custom-call | flops 1000 | bytes 1000 | tf_op jit(solution)/shard_map/expert_2/pallas_call | solution.py:141
  143.9 1.1 collective-permute-start.50
  144.9 12.0 %collective-permute-done.37.other_ref = bf16[128,2048]{1,0:T(8,128)(2,1)S(1)} collective-permute-done((bf16[128,2048]{1,0:T(8,128)(2,1)S(1)}, bf16[128,2048]{1,0:T(8,128)(2,1)S(1)}, u32[]{:S(2)}, u32[]{:S(2)}) %collective-permute-start.37) | collective-permute-done | bytes 524320 | tf_op jit(solution)/shard_map/out_3/half/ppermute | solution.py:198
  157.2 1.0 collective-permute-start.40
  159.0 8.8 %expert_3.1 = (bf16[128,2048]{1,0:T(8,128)(2,1)}, bf16[128,2048]{1,0:T(8,128)(2,1)}) custom-call(bf16[128,2048]{1,0:T(8,128)(2,1)} %copy-done.4, bf16[128,2048]{1,0:T(8,128)(2,1)} %copy-done.18, bf16[2048,2048]{1,0:T(8,128)(2,1)} %bitcast.82, bf16[2048,2048]{1,0:T(8,128)(2,1)} %bitcast.86), custom_call_target="tpu_custom_call" | custom-call | flops 1000 | bytes 1000 | tf_op jit(solution)/shard_map/expert_3/pallas_call | solution.py:141
  168.6 1.2 collective-permute-start.52
  170.0 1.0 collective-permute-start.46
  172.6 8.6 %expert_0.1 = (bf16[128,2048]{1,0:T(8,128)(2,1)}, bf16[128,2048]{1,0:T(8,128)(2,1)}) custom-call(bf16[128,2048]{1,0:T(8,128)(2,1)} %copy-done.7, bf16[128,2048]{1,0:T(8,128)(2,1)} %copy-done.6, bf16[2048,2048]{1,0:T(8,128)(2,1)} %bitcast.83, bf16[2048,2048]{1,0:T(8,128)(2,1)} %bitcast.87, bf16[128,2048]{1,0:T(8,128)(2,1)} %copy-done.16, ...), custom_call_target="tpu_custom_call" | custom-call | flops 1000 | bytes 1000 | tf_op jit(solution)/shard_map/expert_0/pallas_call | solution.py:141
  181.2 1.1 collective-permute-start.42
  182.7 1.8 collective-permute-done.46
  184.8 1.0 collective-permute-start.48
  187.5 3.0 %collective-permute-done.49 = bf16[32,2048]{1,0:T(8,128)(2,1)S(1)} collective-permute-done((bf16[32,2048]{1,0:T(8,128)(2,1)S(1)}, bf16[32,2048]{1,0:T(8,128)(2,1)S(1)}, u32[]{:S(2)}, u32[]{:S(2)}) %collective-permute-start.49) | collective-permute-done | bytes 131104 | tf_op jit(solution)/shard_map/back_3/ppermute | solution.py:283
  190.5 2.1 collective-permute-done.48
  193.0 2.6 %collective-permute-done.42 = bf16[128,2048]{1,0:T(8,128)(2,1)S(1)} collective-permute-done((bf16[128,2048]{1,0:T(8,128)(2,1)}, bf16[128,2048]{1,0:T(8,128)(2,1)S(1)}, u32[]{:S(2)}, u32[]{:S(2)}) %collective-permute-start.42) | collective-permute-done | bytes 524320 | tf_op jit(solution)/shard_map/back_0/half/ppermute | solution.py:198
  195.7 6.1 %collective-permute-done.55 = bf16[128,2048]{1,0:T(8,128)(2,1)S(1)} collective-permute-done((bf16[128,2048]{1,0:T(8,128)(2,1)S(1)}, bf16[128,2048]{1,0:T(8,128)(2,1)S(1)}, u32[]{:S(2)}, u32[]{:S(2)}) %collective-permute-start.55) | collective-permute-done | bytes 524320 | tf_op jit(solution)/shard_map/back_home/ring/ppermute | solution.py:194
  203.3 1.0 collective-permute-start.43
  204.2 3.9 %collective-permute-done.45 = bf16[32,2048]{1,0:T(8,128)(2,1)S(1)} collective-permute-done((bf16[32,2048]{1,0:T(8,128)(2,1)S(1)}, bf16[32,2048]{1,0:T(8,128)(2,1)S(1)}, u32[]{:S(2)}, u32[]{:S(2)}) %collective-permute-start.45) | collective-permute-done | bytes 131104 | tf_op jit(solution)/shard_map/back_0/ppermute | solution.py:283
  208.1 1.7 collective-permute-done.44
  210.1 6.0 %collective-permute-done.56 = bf16[128,2048]{1,0:T(8,128)(2,1)S(1)} collective-permute-done((bf16[128,2048]{1,0:T(8,128)(2,1)S(1)}, bf16[128,2048]{1,0:T(8,128)(2,1)S(1)}, u32[]{:S(2)}, u32[]{:S(2)}) %collective-permute-start.56) | collective-permute-done | bytes 524320 | tf_op jit(solution)/shard_map/ring/ppermute | solution.py:194
  216.1 1.2 fusion.8
  (186 shorter events, 25.8 us)
Async XLA Ops:
  1.3 16.1 %collective-permute-start.2 = (bf16[256,1024]{1,0:T(8,128)(2,1)S(1)}, bf16[256,1024]{1,0:T(8,128)(2,1)}, u32[]{:S(2)}, u32[]{:S(2)}) collective-permute-start(bf16[256,1024]{1,0:T(8,128)(2,1)S(1)} %constant_dynamic-slice_fusion), channel_id=1, source_target_pairs={{0,2},{1,3},{2,6},{3,7},{6,4},{7,5},{4,0},{5,1},{8,10},{9,11},{10,... | collective-permute-start | bytes 1572872 | tf_op jit(solution)/shard_map/gather_0/ring/ppermute | solution.py:194
  4.3 13.4 %collective-permute-start.1 = (bf16[256,1024]{1,0:T(8,128)(2,1)S(1)}, bf16[256,1024]{1,0:T(8,128)(2,1)S(1)}, u32[]{:S(2)}, u32[]{:S(2)}) collective-permute-start(bf16[256,1024]{1,0:T(8,128)(2,1)S(1)} %constant_dynamic-slice_fusion), channel_id=1, source_target_pairs={{0,1},{1,0},{2,3},{3,2},{4,5},{5,4},{6,7},{7,6},{8,9},{9,8},{10,11... | collective-permute-start | bytes 1572872 | tf_op jit(solution)/shard_map/gather_0/half/ppermute | solution.py:198
  5.9 13.3 %collective-permute-start.3 = (bf16[128,2048]{1,0:T(8,128)(2,1)}, bf16[128,2048]{1,0:T(8,128)(2,1)S(1)}, u32[]{:S(2)}, u32[]{:S(2)}) collective-permute-start(bf16[128,2048]{1,0:T(8,128)(2,1)} %bitcast.95), channel_id=1, source_target_pairs={{0,16},{8,24},{16,0},{24,8},{1,17},{9,25},{17,1},{25,9},{2,18},{10... | collective-permute-start | bytes 1572872 | tf_op jit(solution)/shard_map/gather_0/ppermute | solution.py:225
  19.2 19.0 %copy-start.10 = (bf16[128,2048]{1,0:T(8,128)(2,1)}, bf16[128,2048]{1,0:T(8,128)(2,1)S(1)}, u32[]{:S(2)}) copy-start(bf16[128,2048]{1,0:T(8,128)(2,1)S(1)} %collective-permute-done.3.refs_3_) | copy-start | bytes 1572868
  19.2 12.4 %collective-permute-start.8 = (bf16[128,2048]{1,0:T(8,128)(2,1)}, bf16[128,2048]{1,0:T(8,128)(2,1)S(1)}, u32[]{:S(2)}, u32[]{:S(2)}) collective-permute-start(bf16[128,2048]{1,0:T(8,128)(2,1)} %bitcast.98), channel_id=1, source_target_pairs={{0,16},{8,24},{16,0},{24,8},{1,17},{9,25},{17,1},{25,9},{2,18},{10... | collective-permute-start | bytes 1572872 | tf_op jit(solution)/shard_map/gather_1/ppermute | solution.py:225
  20.7 13.1 %collective-permute-start.7 = (bf16[256,1024]{1,0:T(8,128)(2,1)}, bf16[256,1024]{1,0:T(8,128)(2,1)}, u32[]{:S(2)}, u32[]{:S(2)}) collective-permute-start(bf16[256,1024]{1,0:T(8,128)(2,1)} %collective-permute-done.2), channel_id=1, source_target_pairs={{0,2},{1,3},{2,6},{3,7},{6,4},{7,5},{4,0},{5,1},{8,10},{9,11},{10,... | collective-permute-start | bytes 1572872 | tf_op jit(solution)/shard_map/gather_1/ring/ppermute | solution.py:194
  23.3 11.9 %collective-permute-start.6 = (bf16[256,1024]{1,0:T(8,128)(2,1)}, bf16[256,1024]{1,0:T(8,128)(2,1)}, u32[]{:S(2)}, u32[]{:S(2)}) collective-permute-start(bf16[256,1024]{1,0:T(8,128)(2,1)} %collective-permute-done.2), channel_id=1, source_target_pairs={{0,1},{1,0},{2,3},{3,2},{4,5},{5,4},{6,7},{7,6},{8,9},{9,8},{10,11... | collective-permute-start | bytes 1572872 | tf_op jit(solution)/shard_map/gather_1/half/ppermute | solution.py:198
  24.1 12.6 %collective-permute-start = (bf16[128,2048]{1,0:T(8,128)(2,1)}, bf16[128,2048]{1,0:T(8,128)(2,1)S(1)}, u32[]{:S(2)}, u32[]{:S(2)}) collective-permute-start(bf16[128,2048]{1,0:T(8,128)(2,1)} %bitcast.96), channel_id=1, source_target_pairs={{0,8},{8,0},{16,24},{24,16},{1,9},{9,1},{17,25},{25,17},{2,10},{10... | collective-permute-start | bytes 1572872 | tf_op jit(solution)/shard_map/core/ppermute | solution.py:202
  24.1 14.1 %collective-permute-start.5 = (bf16[128,2048]{1,0:T(8,128)(2,1)}, bf16[128,2048]{1,0:T(8,128)(2,1)}, u32[]{:S(2)}, u32[]{:S(2)}) collective-permute-start(bf16[128,2048]{1,0:T(8,128)(2,1)} %bitcast.99), channel_id=1, source_target_pairs={{0,8},{8,0},{16,24},{24,16},{1,9},{9,1},{17,25},{25,17},{2,10},{10... | collective-permute-start | bytes 1572872 | tf_op jit(solution)/shard_map/core/ppermute | solution.py:202
  31.6 6.6 %collective-permute-start.4 = (bf16[128,2048]{1,0:T(8,128)(2,1)S(1)}, bf16[128,2048]{1,0:T(8,128)(2,1)}, u32[]{:S(2)}, u32[]{:S(2)}) collective-permute-start(bf16[128,2048]{1,0:T(8,128)(2,1)S(1)} %collective-permute-done.3.refs_3_), channel_id=1, source_target_pairs={{0,8},{8,0},{16,24},{24,16},{1,9},{9,1},{17,25},{25,17},{2,10},{10... | collective-permute-start | bytes 1572872 | tf_op jit(solution)/shard_map/core/ppermute | solution.py:202
  35.2 3.0 %collective-permute-start.9 = (bf16[128,2048]{1,0:T(8,128)(2,1)S(1)}, bf16[128,2048]{1,0:T(8,128)(2,1)}, u32[]{:S(2)}, u32[]{:S(2)}) collective-permute-start(bf16[128,2048]{1,0:T(8,128)(2,1)S(1)} %collective-permute-done.8.refs_7_), channel_id=1, source_target_pairs={{0,8},{8,0},{16,24},{24,16},{1,9},{9,1},{17,25},{25,17},{2,10},{10... | collective-permute-start | bytes 1572872 | tf_op jit(solution)/shard_map/core/ppermute | solution.py:202
  35.4 18.7 %collective-permute-start.12 = (bf16[256,1024]{1,0:T(8,128)(2,1)}, bf16[256,1024]{1,0:T(8,128)(2,1)S(1)}, u32[]{:S(2)}, u32[]{:S(2)}) collective-permute-start(bf16[256,1024]{1,0:T(8,128)(2,1)} %collective-permute-done.7), channel_id=1, source_target_pairs={{0,2},{1,3},{2,6},{3,7},{6,4},{7,5},{4,0},{5,1},{8,10},{9,11},{10,... | collective-permute-start | bytes 1572872 | tf_op jit(solution)/shard_map/gather_2/ring/ppermute | solution.py:194
  36.7 17.4 %collective-permute-start.11 = (bf16[256,1024]{1,0:T(8,128)(2,1)}, bf16[256,1024]{1,0:T(8,128)(2,1)S(1)}, u32[]{:S(2)}, u32[]{:S(2)}) collective-permute-start(bf16[256,1024]{1,0:T(8,128)(2,1)} %collective-permute-done.7), channel_id=1, source_target_pairs={{0,1},{1,0},{2,3},{3,2},{4,5},{5,4},{6,7},{7,6},{8,9},{9,8},{10,11... | collective-permute-start | bytes 1572872 | tf_op jit(solution)/shard_map/gather_2/half/ppermute | solution.py:198
  44.4 16.7 %copy-start.2 = (bf16[128,2048]{1,0:T(8,128)(2,1)S(1)}, bf16[128,2048]{1,0:T(8,128)(2,1)}, u32[]{:S(2)}) copy-start(bf16[128,2048]{1,0:T(8,128)(2,1)} %shard_map.100) | copy-start | bytes 1572868
  44.4 17.0 %copy-start.22 = (bf16[256,1024]{1,0:T(8,128)(2,1)S(1)}, bf16[256,1024]{1,0:T(8,128)(2,1)}, u32[]{:S(2)}) copy-start(bf16[256,1024]{1,0:T(8,128)(2,1)} %copy-done.21) | copy-start | bytes 1572868
  44.4 12.7 %collective-permute-start.10 = (bf16[128,2048]{1,0:T(8,128)(2,1)}, bf16[128,2048]{1,0:T(8,128)(2,1)S(1)}, u32[]{:S(2)}, u32[]{:S(2)}) collective-permute-start(bf16[128,2048]{1,0:T(8,128)(2,1)} %shard_map.100), channel_id=1, source_target_pairs={{0,8},{8,0},{16,24},{24,16},{1,9},{9,1},{17,25},{25,17},{2,10},{10... | collective-permute-start | bytes 1572872 | tf_op jit(solution)/shard_map/core/ppermute | solution.py:202
  44.5 7.2 %collective-permute-start.32 = (s32[2,128]{0,1:T(8,128)S(1)}, s32[2,128]{0,1:T(8,128)S(1)}, u32[]{:S(2)}, u32[]{:S(2)}) collective-permute-start(s32[2,128]{0,1:T(8,128)S(1)} %bitcast.91), channel_id=1, source_target_pairs={{0,4},{1,5},{2,0},{3,1},{6,2},{7,3},{4,6},{5,7},{8,12},{9,13},{10,... | collective-permute-start | bytes 3080 | tf_op jit(solution)/shard_map/gather_0/ring/ppermute | solution.py:194
  45.9 7.1 %collective-permute-start.26 = (s32[2,128]{0,1:T(8,128)S(1)}, s32[2,128]{0,1:T(8,128)S(1)}, u32[]{:S(2)}, u32[]{:S(2)}) collective-permute-start(s32[2,128]{0,1:T(8,128)S(1)} %bitcast.92), channel_id=1, source_target_pairs={{0,6},{1,7},{2,4},{3,5},{6,0},{7,1},{4,2},{5,3},{8,14},{9,15},{10,... | collective-permute-start | bytes 3080 | tf_op jit(solution)/shard_map/gather_0/ring/ppermute | solution.py:194
  51.7 13.1 %collective-permute-start.20 = (s32[2,128]{0,1:T(8,128)S(1)}, s32[2,128]{0,1:T(8,128)S(1)}, u32[]{:S(2)}, u32[]{:S(2)}) collective-permute-start(s32[2,128]{0,1:T(8,128)S(1)} %bitcast.93), channel_id=1, source_target_pairs={{0,2},{1,3},{2,6},{3,7},{6,4},{7,5},{4,0},{5,1},{8,10},{9,11},{10,... | collective-permute-start | bytes 3080 | tf_op jit(solution)/shard_map/gather_0/ring/ppermute | solution.py:194
  54.2 7.6 %collective-permute-start.13 = (bf16[128,1024]{1,0:T(8,128)(2,1)S(1)}, bf16[128,1024]{1,0:T(8,128)(2,1)S(1)}, u32[]{:S(2)}, u32[]{:S(2)}) collective-permute-start(bf16[128,1024]{1,0:T(8,128)(2,1)S(1)} %slice.172), channel_id=1, source_target_pairs={{0,1},{1,0},{2,3},{3,2},{4,5},{5,4},{6,7},{7,6},{8,9},{9,8},{10,11... | collective-permute-start | bytes 786440 | tf_op jit(solution)/shard_map/half/ppermute | solution.py:198
  55.4 8.4 %collective-permute-start.14 = (bf16[128,1024]{1,0:T(8,128)(2,1)S(1)}, bf16[128,1024]{1,0:T(8,128)(2,1)S(1)}, u32[]{:S(2)}, u32[]{:S(2)}) collective-permute-start(bf16[128,1024]{1,0:T(8,128)(2,1)S(1)} %slice.173), channel_id=1, source_target_pairs={{0,2},{1,3},{2,6},{3,7},{6,4},{7,5},{4,0},{5,1},{8,10},{9,11},{10,... | collective-permute-start | bytes 786440 | tf_op jit(solution)/shard_map/ring/ppermute | solution.py:194
  64.7 2.0 collective-permute-start.15
  67.6 14.9 %collective-permute-start.21 = (bf16[128,2048]{1,0:T(8,128)(2,1)S(1)}, bf16[128,2048]{1,0:T(8,128)(2,1)S(1)}, u32[]{:S(2)}, u32[]{:S(2)}) collective-permute-start(bf16[128,2048]{1,0:T(8,128)(2,1)S(1)} %multiply_convert_fusion), channel_id=1, source_target_pairs={{0,2},{1,3},{2,6},{3,7},{6,4},{7,5},{4,0},{5,1},{8,10},{9,11},{10,... | collective-permute-start | bytes 1572872 | tf_op jit(solution)/shard_map/tokens/ring/ppermute | solution.py:194
  69.8 5.8 %collective-permute-start.18 = (bf16[32,2048]{1,0:T(8,128)(2,1)S(1)}, bf16[32,2048]{1,0:T(8,128)(2,1)S(1)}, u32[]{:S(2)}, u32[]{:S(2)}) collective-permute-start(bf16[32,2048]{1,0:T(8,128)(2,1)S(1)} %get-tuple-element.88), channel_id=1, source_target_pairs={{0,24},{8,16},{16,8},{24,0},{1,25},{9,17},{17,9},{25,1},{2,26},{10... | collective-permute-start | bytes 393224 | tf_op jit(solution)/shard_map/out_0/ppermute | solution.py:283
  69.9 8.6 %collective-permute-start.17 = (bf16[32,2048]{1,0:T(8,128)(2,1)S(1)}, bf16[32,2048]{1,0:T(8,128)(2,1)S(1)}, u32[]{:S(2)}, u32[]{:S(2)}) collective-permute-start(bf16[32,2048]{1,0:T(8,128)(2,1)S(1)} %get-tuple-element.89), channel_id=1, source_target_pairs={{0,16},{8,24},{16,0},{24,8},{1,17},{9,25},{17,1},{25,9},{2,18},{10... | collective-permute-start | bytes 393224 | tf_op jit(solution)/shard_map/out_0/ppermute | solution.py:283
  71.4 7.1 %collective-permute-start.16 = (bf16[32,2048]{1,0:T(8,128)(2,1)S(1)}, bf16[32,2048]{1,0:T(8,128)(2,1)S(1)}, u32[]{:S(2)}, u32[]{:S(2)}) collective-permute-start(bf16[32,2048]{1,0:T(8,128)(2,1)S(1)} %get-tuple-element.90), channel_id=1, source_target_pairs={{0,8},{8,0},{16,24},{24,16},{1,9},{9,1},{17,25},{25,17},{2,10},{10... | collective-permute-start | bytes 393224 | tf_op jit(solution)/shard_map/out_0/ppermute | solution.py:283
  78.6 51.5 %copy-start.7 = (bf16[128,2048]{1,0:T(8,128)(2,1)}, bf16[128,2048]{1,0:T(8,128)(2,1)S(1)}, u32[]{:S(2)}) copy-start(bf16[128,2048]{1,0:T(8,128)(2,1)S(1)} %pad_maximum_fusion.own_ref) | copy-start | bytes 1572868
  78.6 41.0 %collective-permute-start.19 = (bf16[128,2048]{1,0:T(8,128)(2,1)S(1)}, bf16[128,2048]{1,0:T(8,128)(2,1)S(1)}, u32[]{:S(2)}, u32[]{:S(2)}) collective-permute-start(bf16[128,2048]{1,0:T(8,128)(2,1)S(1)} %pad_maximum_fusion.own_ref), channel_id=1, source_target_pairs={{0,1},{1,0},{2,3},{3,2},{4,5},{5,4},{6,7},{7,6},{8,9},{9,8},{10,11... | collective-permute-start | bytes 1572872 | tf_op jit(solution)/shard_map/out_0/half/ppermute | solution.py:198
  82.9 5.8 %collective-permute-start.24 = (bf16[32,2048]{1,0:T(8,128)(2,1)S(1)}, bf16[32,2048]{1,0:T(8,128)(2,1)S(1)}, u32[]{:S(2)}, u32[]{:S(2)}) collective-permute-start(bf16[32,2048]{1,0:T(8,128)(2,1)S(1)} %get-tuple-element.84), channel_id=1, source_target_pairs={{0,24},{8,16},{16,8},{24,0},{1,25},{9,17},{17,9},{25,1},{2,26},{10... | collective-permute-start | bytes 393224 | tf_op jit(solution)/shard_map/out_1/ppermute | solution.py:283
  83.0 7.6 %collective-permute-start.23 = (bf16[32,2048]{1,0:T(8,128)(2,1)S(1)}, bf16[32,2048]{1,0:T(8,128)(2,1)S(1)}, u32[]{:S(2)}, u32[]{:S(2)}) collective-permute-start(bf16[32,2048]{1,0:T(8,128)(2,1)S(1)} %get-tuple-element.85), channel_id=1, source_target_pairs={{0,16},{8,24},{16,0},{24,8},{1,17},{9,25},{17,1},{25,9},{2,18},{10... | collective-permute-start | bytes 393224 | tf_op jit(solution)/shard_map/out_1/ppermute | solution.py:283
  84.0 6.7 %collective-permute-start.22 = (bf16[32,2048]{1,0:T(8,128)(2,1)S(1)}, bf16[32,2048]{1,0:T(8,128)(2,1)S(1)}, u32[]{:S(2)}, u32[]{:S(2)}) collective-permute-start(bf16[32,2048]{1,0:T(8,128)(2,1)S(1)} %get-tuple-element.86), channel_id=1, source_target_pairs={{0,8},{8,0},{16,24},{24,16},{1,9},{9,1},{17,25},{25,17},{2,10},{10... | collective-permute-start | bytes 393224 | tf_op jit(solution)/shard_map/out_1/ppermute | solution.py:283
  85.1 14.7 %collective-permute-start.27 = (bf16[128,2048]{1,0:T(8,128)(2,1)S(1)}, bf16[128,2048]{1,0:T(8,128)(2,1)S(1)}, u32[]{:S(2)}, u32[]{:S(2)}) collective-permute-start(bf16[128,2048]{1,0:T(8,128)(2,1)S(1)} %collective-permute-done.21), channel_id=1, source_target_pairs={{0,2},{1,3},{2,6},{3,7},{6,4},{7,5},{4,0},{5,1},{8,10},{9,11},{10,... | collective-permute-start | bytes 1572872 | tf_op jit(solution)/shard_map/tokens/ring/ppermute | solution.py:194
  90.7 30.0 %copy-start.8 = (bf16[128,2048]{1,0:T(8,128)(2,1)}, bf16[128,2048]{1,0:T(8,128)(2,1)S(1)}, u32[]{:S(2)}) copy-start(bf16[128,2048]{1,0:T(8,128)(2,1)S(1)} %pad_maximum_fusion.1.own_ref) | copy-start | bytes 1572868
  90.7 30.0 %collective-permute-start.25 = (bf16[128,2048]{1,0:T(8,128)(2,1)S(1)}, bf16[128,2048]{1,0:T(8,128)(2,1)S(1)}, u32[]{:S(2)}, u32[]{:S(2)}) collective-permute-start(bf16[128,2048]{1,0:T(8,128)(2,1)S(1)} %pad_maximum_fusion.1.own_ref), channel_id=1, source_target_pairs={{0,1},{1,0},{2,3},{3,2},{4,5},{5,4},{6,7},{7,6},{8,9},{9,8},{10,11... | collective-permute-start | bytes 1572872 | tf_op jit(solution)/shard_map/out_1/half/ppermute | solution.py:198
  100.3 17.1 %collective-permute-start.30 = (bf16[32,2048]{1,0:T(8,128)(2,1)S(1)}, bf16[32,2048]{1,0:T(8,128)(2,1)S(1)}, u32[]{:S(2)}, u32[]{:S(2)}) collective-permute-start(bf16[32,2048]{1,0:T(8,128)(2,1)S(1)} %get-tuple-element.80), channel_id=1, source_target_pairs={{0,24},{8,16},{16,8},{24,0},{1,25},{9,17},{17,9},{25,1},{2,26},{10... | collective-permute-start | bytes 393224 | tf_op jit(solution)/shard_map/out_2/ppermute | solution.py:283
  100.4 18.0 %collective-permute-start.29 = (bf16[32,2048]{1,0:T(8,128)(2,1)S(1)}, bf16[32,2048]{1,0:T(8,128)(2,1)S(1)}, u32[]{:S(2)}, u32[]{:S(2)}) collective-permute-start(bf16[32,2048]{1,0:T(8,128)(2,1)S(1)} %get-tuple-element.81), channel_id=1, source_target_pairs={{0,16},{8,24},{16,0},{24,8},{1,17},{9,25},{17,1},{25,9},{2,18},{10... | collective-permute-start | bytes 393224 | tf_op jit(solution)/shard_map/out_2/ppermute | solution.py:283
  101.2 15.6 %collective-permute-start.33 = (bf16[128,2048]{1,0:T(8,128)(2,1)S(1)}, bf16[128,2048]{1,0:T(8,128)(2,1)S(1)}, u32[]{:S(2)}, u32[]{:S(2)}) collective-permute-start(bf16[128,2048]{1,0:T(8,128)(2,1)S(1)} %collective-permute-done.27), channel_id=1, source_target_pairs={{0,2},{1,3},{2,6},{3,7},{6,4},{7,5},{4,0},{5,1},{8,10},{9,11},{10,... | collective-permute-start | bytes 1572872 | tf_op jit(solution)/shard_map/tokens/ring/ppermute | solution.py:194
  116.8 2.7 %collective-permute-start.28 = (bf16[32,2048]{1,0:T(8,128)(2,1)S(1)}, bf16[32,2048]{1,0:T(8,128)(2,1)S(1)}, u32[]{:S(2)}, u32[]{:S(2)}) collective-permute-start(bf16[32,2048]{1,0:T(8,128)(2,1)S(1)} %get-tuple-element.82), channel_id=1, source_target_pairs={{0,8},{8,0},{16,24},{24,16},{1,9},{9,1},{17,25},{25,17},{2,10},{10... | collective-permute-start | bytes 393224 | tf_op jit(solution)/shard_map/out_2/ppermute | solution.py:283
  117.4 13.8 %collective-permute-start.36 = (bf16[32,2048]{1,0:T(8,128)(2,1)S(1)}, bf16[32,2048]{1,0:T(8,128)(2,1)S(1)}, u32[]{:S(2)}, u32[]{:S(2)}) collective-permute-start(bf16[32,2048]{1,0:T(8,128)(2,1)S(1)} %get-tuple-element.76), channel_id=1, source_target_pairs={{0,24},{8,16},{16,8},{24,0},{1,25},{9,17},{17,9},{25,1},{2,26},{10... | collective-permute-start | bytes 393224 | tf_op jit(solution)/shard_map/out_3/ppermute | solution.py:283
  118.4 12.8 %collective-permute-start.35 = (bf16[32,2048]{1,0:T(8,128)(2,1)S(1)}, bf16[32,2048]{1,0:T(8,128)(2,1)S(1)}, u32[]{:S(2)}, u32[]{:S(2)}) collective-permute-start(bf16[32,2048]{1,0:T(8,128)(2,1)S(1)} %get-tuple-element.77), channel_id=1, source_target_pairs={{0,16},{8,24},{16,0},{24,8},{1,17},{9,25},{17,1},{25,9},{2,18},{10... | collective-permute-start | bytes 393224 | tf_op jit(solution)/shard_map/out_3/ppermute | solution.py:283
  119.6 11.6 %collective-permute-start.34 = (bf16[32,2048]{1,0:T(8,128)(2,1)S(1)}, bf16[32,2048]{1,0:T(8,128)(2,1)S(1)}, u32[]{:S(2)}, u32[]{:S(2)}) collective-permute-start(bf16[32,2048]{1,0:T(8,128)(2,1)S(1)} %get-tuple-element.78), channel_id=1, source_target_pairs={{0,8},{8,0},{16,24},{24,16},{1,9},{9,1},{17,25},{25,17},{2,10},{10... | collective-permute-start | bytes 393224 | tf_op jit(solution)/shard_map/out_3/ppermute | solution.py:283
  119.6 14.8 %collective-permute-start.31 = (bf16[128,2048]{1,0:T(8,128)(2,1)S(1)}, bf16[128,2048]{1,0:T(8,128)(2,1)S(1)}, u32[]{:S(2)}, u32[]{:S(2)}) collective-permute-start(bf16[128,2048]{1,0:T(8,128)(2,1)S(1)} %pad_maximum_fusion.2.refs_0_.own_ref), channel_id=1, source_target_pairs={{0,1},{1,0},{2,3},{3,2},{4,5},{5,4},{6,7},{7,6},{8,9},{9,8},{10,11... | collective-permute-start | bytes 1572872 | tf_op jit(solution)/shard_map/out_2/half/ppermute | solution.py:198
  130.1 26.8 %collective-permute-start.38 = (bf16[128,2048]{1,0:T(8,128)(2,1)}, bf16[128,2048]{1,0:T(8,128)(2,1)S(1)}, u32[]{:S(2)}, u32[]{:S(2)}) collective-permute-start(bf16[128,2048]{1,0:T(8,128)(2,1)} %get-tuple-element.39), channel_id=1, source_target_pairs={{0,1},{1,0},{2,3},{3,2},{4,5},{5,4},{6,7},{7,6},{8,9},{9,8},{10,11... | collective-permute-start | bytes 1572872 | tf_op jit(solution)/shard_map/back_1/half/ppermute | solution.py:198
  131.3 25.6 %collective-permute-start.37 = (bf16[128,2048]{1,0:T(8,128)(2,1)S(1)}, bf16[128,2048]{1,0:T(8,128)(2,1)S(1)}, u32[]{:S(2)}, u32[]{:S(2)}) collective-permute-start(bf16[128,2048]{1,0:T(8,128)(2,1)S(1)} %pad_maximum_fusion.3.refs_0_.own_ref), channel_id=1, source_target_pairs={{0,1},{1,0},{2,3},{3,2},{4,5},{5,4},{6,7},{7,6},{8,9},{9,8},{10,11... | collective-permute-start | bytes 1572872 | tf_op jit(solution)/shard_map/out_3/half/ppermute | solution.py:198
  132.6 24.3 %copy-start.17 = (bf16[128,2048]{1,0:T(8,128)(2,1)S(1)}, bf16[128,2048]{1,0:T(8,128)(2,1)}, u32[]{:S(2)}) copy-start(bf16[128,2048]{1,0:T(8,128)(2,1)} %get-tuple-element.38) | copy-start | bytes 1572868
  143.9 24.0 %collective-permute-start.50 = (bf16[128,2048]{1,0:T(8,128)(2,1)}, bf16[128,2048]{1,0:T(8,128)(2,1)S(1)}, u32[]{:S(2)}, u32[]{:S(2)}) collective-permute-start(bf16[128,2048]{1,0:T(8,128)(2,1)} %get-tuple-element.46), channel_id=1, source_target_pairs={{0,1},{1,0},{2,3},{3,2},{4,5},{5,4},{6,7},{7,6},{8,9},{9,8},{10,11... | collective-permute-start | bytes 1572872 | tf_op jit(solution)/shard_map/back_2/half/ppermute | solution.py:198
  157.1 12.7 %collective-permute-start.41 = (bf16[32,2048]{1,0:T(8,128)(2,1)S(1)}, bf16[32,2048]{1,0:T(8,128)(2,1)S(1)}, u32[]{:S(2)}, u32[]{:S(2)}) collective-permute-start(bf16[32,2048]{1,0:T(8,128)(2,1)S(1)} %get-tuple-element.72), channel_id=1, source_target_pairs={{0,24},{8,16},{16,8},{24,0},{1,25},{9,17},{17,9},{25,1},{2,26},{10... | collective-permute-start | bytes 393224 | tf_op jit(solution)/shard_map/back_1/ppermute | solution.py:283
  157.2 12.8 %collective-permute-start.40 = (bf16[32,2048]{1,0:T(8,128)(2,1)S(1)}, bf16[32,2048]{1,0:T(8,128)(2,1)S(1)}, u32[]{:S(2)}, u32[]{:S(2)}) collective-permute-start(bf16[32,2048]{1,0:T(8,128)(2,1)S(1)} %get-tuple-element.73), channel_id=1, source_target_pairs={{0,16},{8,24},{16,0},{24,8},{1,17},{9,25},{17,1},{25,9},{2,18},{10... | collective-permute-start | bytes 393224 | tf_op jit(solution)/shard_map/back_1/ppermute | solution.py:283
  158.1 12.9 %collective-permute-start.39 = (bf16[32,2048]{1,0:T(8,128)(2,1)S(1)}, bf16[32,2048]{1,0:T(8,128)(2,1)S(1)}, u32[]{:S(2)}, u32[]{:S(2)}) collective-permute-start(bf16[32,2048]{1,0:T(8,128)(2,1)S(1)} %get-tuple-element.74), channel_id=1, source_target_pairs={{0,8},{8,0},{16,24},{24,16},{1,9},{9,1},{17,25},{25,17},{2,10},{10... | collective-permute-start | bytes 393224 | tf_op jit(solution)/shard_map/back_1/ppermute | solution.py:283
  168.0 13.2 %collective-permute-start.53 = (bf16[32,2048]{1,0:T(8,128)(2,1)S(1)}, bf16[32,2048]{1,0:T(8,128)(2,1)S(1)}, u32[]{:S(2)}, u32[]{:S(2)}) collective-permute-start(bf16[32,2048]{1,0:T(8,128)(2,1)S(1)} %get-tuple-element.60), channel_id=1, source_target_pairs={{0,24},{8,16},{16,8},{24,0},{1,25},{9,17},{17,9},{25,1},{2,26},{10... | collective-permute-start | bytes 393224 | tf_op jit(solution)/shard_map/back_2/ppermute | solution.py:283
  168.6 13.7 %collective-permute-start.52 = (bf16[32,2048]{1,0:T(8,128)(2,1)S(1)}, bf16[32,2048]{1,0:T(8,128)(2,1)S(1)}, u32[]{:S(2)}, u32[]{:S(2)}) collective-permute-start(bf16[32,2048]{1,0:T(8,128)(2,1)S(1)} %get-tuple-element.61), channel_id=1, source_target_pairs={{0,16},{8,24},{16,0},{24,8},{1,17},{9,25},{17,1},{25,9},{2,18},{10... | collective-permute-start | bytes 393224 | tf_op jit(solution)/shard_map/back_2/ppermute | solution.py:283
  169.8 12.5 %collective-permute-start.51 = (bf16[32,2048]{1,0:T(8,128)(2,1)S(1)}, bf16[32,2048]{1,0:T(8,128)(2,1)S(1)}, u32[]{:S(2)}, u32[]{:S(2)}) collective-permute-start(bf16[32,2048]{1,0:T(8,128)(2,1)S(1)} %get-tuple-element.62), channel_id=1, source_target_pairs={{0,8},{8,0},{16,24},{24,16},{1,9},{9,1},{17,25},{25,17},{2,10},{10... | collective-permute-start | bytes 393224 | tf_op jit(solution)/shard_map/back_2/ppermute | solution.py:283
  170.0 14.5 %collective-permute-start.46 = (bf16[128,2048]{1,0:T(8,128)(2,1)}, bf16[128,2048]{1,0:T(8,128)(2,1)S(1)}, u32[]{:S(2)}, u32[]{:S(2)}) collective-permute-start(bf16[128,2048]{1,0:T(8,128)(2,1)} %get-tuple-element.40.refs_1_), channel_id=1, source_target_pairs={{0,1},{1,0},{2,3},{3,2},{4,5},{5,4},{6,7},{7,6},{8,9},{9,8},{10,11... | collective-permute-start | bytes 1572872 | tf_op jit(solution)/shard_map/back_3/half/ppermute | solution.py:198
  171.8 14.8 %collective-permute-start.54 = (bf16[128,2048]{1,0:T(8,128)(2,1)S(1)}, bf16[128,2048]{1,0:T(8,128)(2,1)S(1)}, u32[]{:S(2)}, u32[]{:S(2)}) collective-permute-start(bf16[128,2048]{1,0:T(8,128)(2,1)S(1)} %fusion.5.refs_0_), channel_id=1, source_target_pairs={{0,2},{1,3},{2,6},{3,7},{6,4},{7,5},{4,0},{5,1},{8,10},{9,11},{10,... | collective-permute-start | bytes 1572872 | tf_op jit(solution)/shard_map/back_home/ring/ppermute | solution.py:194
  181.2 14.4 %collective-permute-start.42 = (bf16[128,2048]{1,0:T(8,128)(2,1)}, bf16[128,2048]{1,0:T(8,128)(2,1)S(1)}, u32[]{:S(2)}, u32[]{:S(2)}) collective-permute-start(bf16[128,2048]{1,0:T(8,128)(2,1)} %get-tuple-element.42), channel_id=1, source_target_pairs={{0,1},{1,0},{2,3},{3,2},{4,5},{5,4},{6,7},{7,6},{8,9},{9,8},{10,11... | collective-permute-start | bytes 1572872 | tf_op jit(solution)/shard_map/back_0/half/ppermute | solution.py:198
  184.6 32.7 %copy-start.1 = (bf16[256,2048]{1,0:T(8,128)(2,1)S(1)}, bf16[256,2048]{1,0:T(8,128)(2,1)}, u32[]{:S(2)}) copy-start(bf16[256,2048]{1,0:T(8,128)(2,1)} %param.14) | copy-start | bytes 3145732
  184.7 5.8 %collective-permute-start.49 = (bf16[32,2048]{1,0:T(8,128)(2,1)S(1)}, bf16[32,2048]{1,0:T(8,128)(2,1)S(1)}, u32[]{:S(2)}, u32[]{:S(2)}) collective-permute-start(bf16[32,2048]{1,0:T(8,128)(2,1)S(1)} %get-tuple-element.64), channel_id=1, source_target_pairs={{0,24},{8,16},{16,8},{24,0},{1,25},{9,17},{17,9},{25,1},{2,26},{10... | collective-permute-start | bytes 393224 | tf_op jit(solution)/shard_map/back_3/ppermute | solution.py:283
  184.8 7.8 %collective-permute-start.48 = (bf16[32,2048]{1,0:T(8,128)(2,1)S(1)}, bf16[32,2048]{1,0:T(8,128)(2,1)S(1)}, u32[]{:S(2)}, u32[]{:S(2)}) collective-permute-start(bf16[32,2048]{1,0:T(8,128)(2,1)S(1)} %get-tuple-element.65), channel_id=1, source_target_pairs={{0,16},{8,24},{16,0},{24,8},{1,17},{9,25},{17,1},{25,9},{2,18},{10... | collective-permute-start | bytes 393224 | tf_op jit(solution)/shard_map/back_3/ppermute | solution.py:283
  185.8 6.8 %collective-permute-start.47 = (bf16[32,2048]{1,0:T(8,128)(2,1)S(1)}, bf16[32,2048]{1,0:T(8,128)(2,1)S(1)}, u32[]{:S(2)}, u32[]{:S(2)}) collective-permute-start(bf16[32,2048]{1,0:T(8,128)(2,1)S(1)} %get-tuple-element.66), channel_id=1, source_target_pairs={{0,8},{8,0},{16,24},{24,16},{1,9},{9,1},{17,25},{25,17},{2,10},{10... | collective-permute-start | bytes 393224 | tf_op jit(solution)/shard_map/back_3/ppermute | solution.py:283
  187.0 14.8 %collective-permute-start.55 = (bf16[128,2048]{1,0:T(8,128)(2,1)S(1)}, bf16[128,2048]{1,0:T(8,128)(2,1)S(1)}, u32[]{:S(2)}, u32[]{:S(2)}) collective-permute-start(bf16[128,2048]{1,0:T(8,128)(2,1)S(1)} %fusion.7), channel_id=1, source_target_pairs={{0,2},{1,3},{2,6},{3,7},{6,4},{7,5},{4,0},{5,1},{8,10},{9,11},{10,... | collective-permute-start | bytes 1572872 | tf_op jit(solution)/shard_map/back_home/ring/ppermute | solution.py:194
  202.2 13.9 %collective-permute-start.56 = (bf16[128,2048]{1,0:T(8,128)(2,1)S(1)}, bf16[128,2048]{1,0:T(8,128)(2,1)S(1)}, u32[]{:S(2)}, u32[]{:S(2)}) collective-permute-start(bf16[128,2048]{1,0:T(8,128)(2,1)S(1)} %fusion.6), channel_id=1, source_target_pairs={{0,2},{1,3},{2,6},{3,7},{6,4},{7,5},{4,0},{5,1},{8,10},{9,11},{10,... | collective-permute-start | bytes 1572872 | tf_op jit(solution)/shard_map/ring/ppermute | solution.py:194
  202.3 5.8 %collective-permute-start.45 = (bf16[32,2048]{1,0:T(8,128)(2,1)S(1)}, bf16[32,2048]{1,0:T(8,128)(2,1)S(1)}, u32[]{:S(2)}, u32[]{:S(2)}) collective-permute-start(bf16[32,2048]{1,0:T(8,128)(2,1)S(1)} %get-tuple-element.68), channel_id=1, source_target_pairs={{0,24},{8,16},{16,8},{24,0},{1,25},{9,17},{17,9},{25,1},{2,26},{10... | collective-permute-start | bytes 393224 | tf_op jit(solution)/shard_map/back_0/ppermute | solution.py:283
  202.4 7.4 %collective-permute-start.44 = (bf16[32,2048]{1,0:T(8,128)(2,1)S(1)}, bf16[32,2048]{1,0:T(8,128)(2,1)S(1)}, u32[]{:S(2)}, u32[]{:S(2)}) collective-permute-start(bf16[32,2048]{1,0:T(8,128)(2,1)S(1)} %get-tuple-element.69), channel_id=1, source_target_pairs={{0,16},{8,24},{16,0},{24,8},{1,17},{9,25},{17,1},{25,9},{2,18},{10... | collective-permute-start | bytes 393224 | tf_op jit(solution)/shard_map/back_0/ppermute | solution.py:283
  203.3 6.5 %collective-permute-start.43 = (bf16[32,2048]{1,0:T(8,128)(2,1)S(1)}, bf16[32,2048]{1,0:T(8,128)(2,1)S(1)}, u32[]{:S(2)}, u32[]{:S(2)}) collective-permute-start(bf16[32,2048]{1,0:T(8,128)(2,1)S(1)} %get-tuple-element.70), channel_id=1, source_target_pairs={{0,8},{8,0},{16,24},{24,16},{1,9},{9,1},{17,25},{25,17},{2,10},{10... | collective-permute-start | bytes 393224 | tf_op jit(solution)/shard_map/back_0/ppermute | solution.py:283
  (17 other events, 71.9 us)

commit v2 on v1

--- a/solution.py
+++ b/solution.py
@@ -9,6 +9,9 @@
 
 HEADS = 16
 HALVES = 2
+TIES = {"E1": ["D0", "W2"], "E2": ["W3"], "H1": ["E2"], "H2": ["E3"], "H3": ["E0"], "E0": ["D1", "E3", "P1"], "X3": ["E0", "P2"], "S1": ["W0"], "Z2": ["W0"], "Z3": ["D0"]}
+ECOST = 4000000000
+ACOST = 1000
 
 
 NORM_EPS = 1e-05
@@ -81,7 +84,7 @@
         out_specs=pl.BlockSpec((row_count, width), lambda i: (0, i)),
         out_shape=jax.ShapeDtypeStruct((row_count, model_width), jnp.bfloat16),
         compiler_params=pltpu.CompilerParams(vmem_limit_bytes=VMEM_BYTES),
-        cost_estimate=pl.CostEstimate(flops=1000, bytes_accessed=1000, transcendentals=0),
+        cost_estimate=pl.CostEstimate(flops=ACOST, bytes_accessed=1000, transcendentals=0),
     )(*operands, *earlier)
 
 
@@ -154,7 +157,7 @@
             pltpu.SemaphoreType.DMA((4,)),
         ],
         compiler_params=pltpu.CompilerParams(vmem_limit_bytes=VMEM_BYTES),
-        cost_estimate=pl.CostEstimate(flops=1000, bytes_accessed=1000, transcendentals=0),
+        cost_estimate=pl.CostEstimate(flops=ECOST, bytes_accessed=1000, transcendentals=0),
     )(own_rows, other_rows, first, second, *earlier)
 
 
@@ -283,68 +286,92 @@
             parts[i] = lax.ppermute(parts[i], "seq", swap_pairs(seq_count, i))
         return jnp.concatenate(parts, axis=0)
 
-    with jax.named_scope("tokens"):
-        blocks = [normed]
-        for _ in range(1, planes):
-            blocks.append(around(blocks[-1]))
-
-    def around_add(passing, part):
-        with jax.named_scope("back_home"):
-            if passing is not None:
-                part = part + around(passing).astype(jnp.float32)
-            return part.astype(jnp.bfloat16)
-
-    matches, slot_rows, other_rows = [], [], []
-    for step in range(planes):
-        with jax.named_scope(f"out_{step}"):
-            target = targets[step].T
-            matches.append([target[:, k : k + 1] == served_target[None, :] for k in range(2)])
-            place_map = (matches[step][0] | matches[step][1]).astype(jnp.bfloat16)
-            slots = jnp.einsum(
-                "ts,td->sd", place_map, blocks[step], preferred_element_type=jnp.float32
-            ).astype(jnp.bfloat16)
-            slot_rows.append(exchange(slots))
-            other_rows.append(other_half(slot_rows[step]))
-
-    def expert_step(step, earlier):
-        with jax.named_scope(f"expert_{step}"):
-            return expert_half(slot_rows[step], other_rows[step], w_in[0], w_out[0], earlier)
-
-    def combine(step, outs, later):
-        with jax.named_scope(f"back_{step}"):
-            own_out, other_out = outs
-            own_out = after(own_out, later)
-            out_sum = own_out.astype(jnp.float32) + other_half(other_out).astype(jnp.float32)
-            returned = exchange(out_sum.astype(jnp.bfloat16))
-            logits = jnp.dot(blocks[step], w_router, preferred_element_type=jnp.float32)
-            named = (targets[step].T // slot_count)[:, :, None] == expert_ids[None, None, :]
-            picked = jnp.sum(jnp.where(named, logits[:, None, :], 0.0), axis=2)
-            gate_first = 1.0 / (1.0 + jnp.exp(picked[:, 1:2] - picked[:, 0:1]))
-            gate_second = 1.0 / (1.0 + jnp.exp(picked[:, 0:1] - picked[:, 1:2]))
-            gate_map = jnp.where(matches[step][0], gate_first, 0.0) + jnp.where(
-                matches[step][1], gate_second, 0.0
-            )
-            gate_high = gate_map.astype(jnp.bfloat16)
-            gate_low = (gate_map - gate_high.astype(jnp.float32)).astype(jnp.bfloat16)
-            return jnp.dot(gate_high, returned, preferred_element_type=jnp.float32) + jnp.dot(
-                gate_low, returned, preferred_element_type=jnp.float32
-            )
-
-    outs = [None] * planes
-    passing, waiting = None, []
-    for step in range(1, planes):
-        ahead = slot_rows[step + 1 : step + 2]
-        outs[step] = expert_step(step, ahead + other_rows[:1] if step == 1 else ahead)
+    made = {}
+
+    def get(name):
+        if name not in made:
+            made[name] = MAKE[name[0]](int(name[1:]), [get(other) for other in TIES.get(name, []) if int(other[1:]) < planes])
+        return made[name]
+
+    def tied(value, others):
+        return after(value, [other[0] if isinstance(other, tuple) else other for other in others])
+
+    def token_block(step, ties):
+        return around(tied(get(f"Z{step - 1}"), ties)) if step else normed
+
+    def matches(step):
+        target = targets[step].T
+        return [target[:, k : k + 1] == served_target[None, :] for k in range(2)]
+
+    def slot_block(step, ties):
+        match = matches(step)
+        return jnp.einsum(
+            "ts,td->sd",
+            (match[0] | match[1]).astype(jnp.bfloat16),
+            tied(get(f"Z{step}"), ties),
+            preferred_element_type=jnp.float32,
+        ).astype(jnp.bfloat16)
+
+    def expert_rows(step, ties):
+        return exchange(tied(get(f"S{step}"), ties))
+
+    def other_rows(step, ties):
+        return other_half(tied(get(f"W{step}"), ties))
+
+    def expert_out(step, ties):
+        own, other = get(f"W{step}"), get(f"D{step}")
+        ties = [tie[0] if isinstance(tie, tuple) else tie for tie in ties]
+        return tuple(expert_half(own, other, w_in[0], w_out[0], ties))
+
+    def other_out(step, ties):
+        return other_half(tied(get(f"E{step}")[1], ties))
+
+    def both_halves(step, ties):
+        own = tied(get(f"E{step}")[0], ties)
+        both = own.astype(jnp.float32) + get(f"R{step}").astype(jnp.float32)
+        return both.astype(jnp.bfloat16)
+
+    def returned_rows(step, ties):
+        return exchange(tied(get(f"H{step}"), ties))
+
+    def gated_part(step, ties):
+        returned = tied(get(f"X{step}"), ties)
+        match = matches(step)
+        logits = jnp.dot(get(f"Z{step}"), w_router, preferred_element_type=jnp.float32)
+        named = (targets[step].T // slot_count)[:, :, None] == expert_ids[None, None, :]
+        picked = jnp.sum(jnp.where(named, logits[:, None, :], 0.0), axis=2)
+        gate_first = 1.0 / (1.0 + jnp.exp(picked[:, 1:2] - picked[:, 0:1]))
+        gate_second = 1.0 / (1.0 + jnp.exp(picked[:, 0:1] - picked[:, 1:2]))
+        gate_map = jnp.where(match[0], gate_first, 0.0) + jnp.where(match[1], gate_second, 0.0)
+        gate_high = gate_map.astype(jnp.bfloat16)
+        gate_low = (gate_map - gate_high.astype(jnp.float32)).astype(jnp.bfloat16)
+        return jnp.dot(gate_high, returned, preferred_element_type=jnp.float32) + jnp.dot(
+            gate_low, returned, preferred_element_type=jnp.float32
+        )
+
+    def passed_sum(step, ties):
+        part = get(f"G{step}")
         if step > 1:
-            later = [outs[step][0], *other_rows[step + 1 : step + 2]]
-            passing = around_add(passing, combine(step - 1, outs[step - 1], later))
-            waiting = waiting or [passing]
-    outs[0] = expert_step(0, waiting + [outs[-1][1]])
+            part = part + around(get(f"P{step - 1}")).astype(jnp.float32)
+        return tied(part.astype(jnp.bfloat16), ties)
+
+    MAKE = {
+        "Z": token_block,
+        "S": slot_block,
+        "W": expert_rows,
+        "D": other_rows,
+        "E": expert_out,
+        "R": other_out,
+        "H": both_halves,
+        "X": returned_rows,
+        "G": gated_part,
+        "P": passed_sum,
+    }
+    layer_out = residual + get("G0")
     if planes > 1:
-        passing = around_add(passing, combine(planes - 1, outs[-1], outs[0][:1]))
-    layer_out = residual + combine(0, outs[0], [])
-    if planes > 1:
-        layer_out = layer_out + around(passing).astype(jnp.float32)
+        last = get(f"P{planes - 1}")
+        with jax.named_scope("home"):
+            layer_out = layer_out + around(last).astype(jnp.float32)
     return layer_out.astype(jnp.bfloat16)[None]
 
 

time: 218 us -> 204 us (0.936)
  waiting for transfers between devices: 104 us -> 87.7 us
    ppermute x13, waiting for transfers between devices: 53 us -> 28.4 us  [around(): return lax.ppermute(block, 'expert', ring_pairs[hop])]
    ppermute x24, waiting for transfers between devices: 21.8 us -> 34.7 us  [exchange(): parts[i] = lax.ppermute(parts[i], 'seq', swap_pairs(seq_count, i))]
    ppermute x12, waiting for transfers between devices: 20 us -> 15 us  [other_half(): return lax.ppermute(block, 'expert', half_pairs)]
    unnamed x49 -> x47, local copies, waits for them, and re-layouts: 4.38 us -> 4.51 us
  transfers between devices with their start and end apart: 57 -> 57, of which waited for: 29 -> 28; matrix products, arithmetic and copies ran while one was open for 8% -> 9% of each run, Pallas kernels for 19% -> 20%
where the time goes in v2:
time: 204 us
  waiting for transfers between devices  87.7 us (43%)
  starting transfers between devices  51.2 us (25%)
  Pallas kernels  40.5 us (20%)
  matrix products  13.5 us (7%)
  local copies, waits for them, and re-layouts  6.55 us (3%)
  other arithmetic  3.61 us (2%)
    ppermute x24, waiting for transfers between devices, exchange(): parts[i] = lax.ppermute(parts[i], 'seq', swap_pairs(seq_count, i))  34.7 us
    pallas_call x4, Pallas kernels, expert_half(): pl.pallas_call(expert_kernel, in_specs=[anywhere] * (4 + len(earlier)), o...  34.4 us
    ppermute x13, waiting for transfers between devices, around(): return lax.ppermute(block, 'expert', ring_pairs[hop])  28.4 us
    ppermute x13, starting transfers between devices, around(): return lax.ppermute(block, 'expert', ring_pairs[hop])  18.5 us
    ppermute x24, starting transfers between devices, exchange(): parts[i] = lax.ppermute(parts[i], 'seq', swap_pairs(seq_count, i))  15.8 us
    ppermute x12, waiting for transfers between devices, other_half(): return lax.ppermute(block, 'expert', half_pairs)  15 us
    ppermute x12, starting transfers between devices, other_half(): return lax.ppermute(block, 'expert', half_pairs)  13.3 us
    ppermute x2, waiting for transfers between devices, on_device(): lax.ppermute(sources[which], 'seq', swap_pairs(seq_count, across))  8.38 us
  transfers between devices with their start and end apart: 57, of which 28 were waited for; matrix products, arithmetic and copies ran while one was open for 9% of the time, Pallas kernels for 20%

profile of v2, /device:TPU:0, one launch (start us, length us, event | category | flops | bytes accessed | tf_op | source)
XLA Modules:
  0.0 203.9 jit_solution(14053614811259423410)
XLA Ops:
  0.0 1.2 copy-done
  1.3 3.1 %collective-permute-start.2 = (bf16[256,1024]{1,0:T(8,128)(2,1)S(1)}, bf16[256,1024]{1,0:T(8,128)(2,1)}, u32[]{:S(2)}, u32[]{:S(2)}) collective-permute-start(bf16[256,1024]{1,0:T(8,128)(2,1)S(1)} %constant_dynamic-slice_fusion), channel_id=1, source_target_pairs={{0,2},{1,3},{2,6},{3,7},{6,4},{7,5},{4,0},{5,1},{8,10},{9,11},{10,... | collective-permute-start | bytes 1572872 | tf_op jit(solution)/shard_map/gather_0/ring/ppermute | solution.py:197
  4.3 1.5 collective-permute-start.1
  5.9 1.5 collective-permute-start.3
  9.6 7.8 %collective-permute-done.2 = bf16[256,1024]{1,0:T(8,128)(2,1)} collective-permute-done((bf16[256,1024]{1,0:T(8,128)(2,1)S(1)}, bf16[256,1024]{1,0:T(8,128)(2,1)}, u32[]{:S(2)}, u32[]{:S(2)}) %collective-permute-start.2) | collective-permute-done | bytes 524320 | tf_op jit(solution)/shard_map/gather_0/ring/ppermute | solution.py:197
  17.7 1.4 collective-permute-done.3.refs_3_
  19.2 1.5 collective-permute-start.8
  20.7 2.6 %collective-permute-start.7 = (bf16[256,1024]{1,0:T(8,128)(2,1)}, bf16[256,1024]{1,0:T(8,128)(2,1)}, u32[]{:S(2)}, u32[]{:S(2)}) collective-permute-start(bf16[256,1024]{1,0:T(8,128)(2,1)} %collective-permute-done.2), channel_id=1, source_target_pairs={{0,2},{1,3},{2,6},{3,7},{6,4},{7,5},{4,0},{5,1},{8,10},{9,11},{10,... | collective-permute-start | bytes 1572872 | tf_op jit(solution)/shard_map/gather_1/ring/ppermute | solution.py:197
  24.6 6.9 %collective-permute-done.8.refs_7_ = bf16[128,2048]{1,0:T(8,128)(2,1)S(1)} collective-permute-done((bf16[128,2048]{1,0:T(8,128)(2,1)}, bf16[128,2048]{1,0:T(8,128)(2,1)S(1)}, u32[]{:S(2)}, u32[]{:S(2)}) %collective-permute-start.8) | collective-permute-done | bytes 524320 | tf_op jit(solution)/shard_map/gather_1/ppermute | solution.py:228
  31.6 2.2 %collective-permute-done.7 = bf16[256,1024]{1,0:T(8,128)(2,1)} collective-permute-done((bf16[256,1024]{1,0:T(8,128)(2,1)}, bf16[256,1024]{1,0:T(8,128)(2,1)}, u32[]{:S(2)}, u32[]{:S(2)}) %collective-permute-start.7) | collective-permute-done | bytes 524320 | tf_op jit(solution)/shard_map/gather_1/ring/ppermute | solution.py:197
  33.8 1.4 collective-permute-done.6
  35.4 1.3 collective-permute-start.12
  36.7 1.5 collective-permute-start.11
  38.3 6.1 %shard_map.100 = bf16[128,2048]{1,0:T(8,128)(2,1)} custom-call(bf16[128,2048]{1,0:T(8,128)(2,1)} %bitcast.94, bf16[128,2048]{1,0:T(8,128)(2,1)} %bitcast.97, bf16[128,2048]{1,0:T(8,128)(2,1)} %copy-done.14, bf16[128,2048]{1,0:T(8,128)(2,1)} %copy-done.12, bf16[128,2048]{1,0:T(8,128)(2,1)} %collective-permute-done.4.refs_4_, bf16[128,2048]{1,0:T(8,128)(2,1)} %bitcast.100, ...), custom_call_target="tpu_custom_call" | custom-call | flops 1000 | bytes 1000 | tf_op jit(solution)/shard_map/pallas_call | solution.py:79
  44.5 1.0 collective-permute-start.33
  45.5 1.8 collective-permute-start.26
  47.3 4.4 %collective-permute-done.33 = s32[2,128]{0,1:T(8,128)S(1)} collective-permute-done((s32[2,128]{0,1:T(8,128)S(1)}, s32[2,128]{0,1:T(8,128)S(1)}, u32[]{:S(2)}, u32[]{:S(2)}) %collective-permute-start.33) | collective-permute-done | bytes 1056 | tf_op jit(solution)/shard_map/gather_0/ring/ppermute | solution.py:197
  51.7 4.0 %collective-permute-start.20 = (s32[2,128]{0,1:T(8,128)S(1)}, s32[2,128]{0,1:T(8,128)S(1)}, u32[]{:S(2)}, u32[]{:S(2)}) collective-permute-start(s32[2,128]{0,1:T(8,128)S(1)} %bitcast.93), channel_id=1, source_target_pairs={{0,2},{1,3},{2,6},{3,7},{6,4},{7,5},{4,0},{5,1},{8,10},{9,11},{10,... | collective-permute-start | bytes 3080 | tf_op jit(solution)/shard_map/gather_0/ring/ppermute | solution.py:197
  56.0 1.2 collective-permute-start.13
  57.4 1.4 fusion.26
  58.8 1.4 fusion.30
  60.2 1.2 fusion.32
  62.0 1.8 collective-permute-done.13
  64.0 1.3 fusion.28
  67.2 1.2 collective-permute-done.15
  70.7 1.5 collective-permute-start.17
  72.8 3.6 %collective-permute-done.18 = bf16[32,2048]{1,0:T(8,128)(2,1)S(1)} collective-permute-done((bf16[32,2048]{1,0:T(8,128)(2,1)S(1)}, bf16[32,2048]{1,0:T(8,128)(2,1)S(1)}, u32[]{:S(2)}, u32[]{:S(2)}) %collective-permute-start.18) | collective-permute-done | bytes 131104 | tf_op jit(solution)/shard_map/ppermute | solution.py:286
  76.4 2.8 %collective-permute-done.17 = bf16[32,2048]{1,0:T(8,128)(2,1)S(1)} collective-permute-done((bf16[32,2048]{1,0:T(8,128)(2,1)S(1)}, bf16[32,2048]{1,0:T(8,128)(2,1)S(1)}, u32[]{:S(2)}, u32[]{:S(2)}) %collective-permute-start.17) | collective-permute-done | bytes 131104 | tf_op jit(solution)/shard_map/ppermute | solution.py:286
  79.9 4.3 %collective-permute-done.21 = bf16[128,2048]{1,0:T(8,128)(2,1)S(1)} collective-permute-done((bf16[128,2048]{1,0:T(8,128)(2,1)S(1)}, bf16[128,2048]{1,0:T(8,128)(2,1)S(1)}, u32[]{:S(2)}, u32[]{:S(2)}) %collective-permute-start.21) | collective-permute-done | bytes 524320 | tf_op jit(solution)/shard_map/ring/ppermute | solution.py:197
  86.9 3.6 %collective-permute-done.24 = bf16[32,2048]{1,0:T(8,128)(2,1)S(1)} collective-permute-done((bf16[32,2048]{1,0:T(8,128)(2,1)S(1)}, bf16[32,2048]{1,0:T(8,128)(2,1)S(1)}, u32[]{:S(2)}, u32[]{:S(2)}) %collective-permute-start.24) | collective-permute-done | bytes 131104 | tf_op jit(solution)/shard_map/ppermute | solution.py:286
  90.5 1.9 collective-permute-done.23
  92.4 1.1 collective-permute-start.25
  93.6 4.7 %collective-permute-done.27 = bf16[128,2048]{1,0:T(8,128)(2,1)S(1)} collective-permute-done((bf16[128,2048]{1,0:T(8,128)(2,1)S(1)}, bf16[128,2048]{1,0:T(8,128)(2,1)S(1)}, u32[]{:S(2)}, u32[]{:S(2)}) %collective-permute-start.27) | collective-permute-done | bytes 524320 | tf_op jit(solution)/shard_map/ring/ppermute | solution.py:197
  99.4 1.3 collective-permute-start.34
  100.9 3.6 %collective-permute-done.36 = bf16[32,2048]{1,0:T(8,128)(2,1)S(1)} collective-permute-done((bf16[32,2048]{1,0:T(8,128)(2,1)S(1)}, bf16[32,2048]{1,0:T(8,128)(2,1)S(1)}, u32[]{:S(2)}, u32[]{:S(2)}) %collective-permute-start.36) | collective-permute-done | bytes 131104 | tf_op jit(solution)/shard_map/ppermute | solution.py:286
  104.6 1.0 collective-permute-done.35
  105.6 1.1 collective-permute-start.37
  107.7 8.6 %shard_map.102 = (bf16[128,2048]{1,0:T(8,128)(2,1)}, bf16[128,2048]{1,0:T(8,128)(2,1)}) custom-call(bf16[128,2048]{1,0:T(8,128)(2,1)} %copy-done.10, bf16[128,2048]{1,0:T(8,128)(2,1)} %copy-done.7, bf16[2048,2048]{1,0:T(8,128)(2,1)} %bitcast.80, bf16[2048,2048]{1,0:T(8,128)(2,1)} %bitcast.84, bf16[128,2048]{1,0:T(8,128)(2,1)} %copy-done.6, ...), custom_call_target="tpu_custom_call" | custom-call | flops 4000000000 | bytes 1000 | tf_op jit(solution)/shard_map/pallas_call | solution.py:144
  116.3 1.1 collective-permute-start.38
  117.9 1.3 collective-permute-start.31
  119.2 1.0 collective-permute-start.30
  120.5 2.6 %collective-permute-done.31 = bf16[32,2048]{1,0:T(8,128)(2,1)S(1)} collective-permute-done((bf16[32,2048]{1,0:T(8,128)(2,1)S(1)}, bf16[32,2048]{1,0:T(8,128)(2,1)S(1)}, u32[]{:S(2)}, u32[]{:S(2)}) %collective-permute-start.31) | collective-permute-done | bytes 131104 | tf_op jit(solution)/shard_map/ppermute | solution.py:286
  123.1 3.5 %collective-permute-done.30 = bf16[32,2048]{1,0:T(8,128)(2,1)S(1)} collective-permute-done((bf16[32,2048]{1,0:T(8,128)(2,1)S(1)}, bf16[32,2048]{1,0:T(8,128)(2,1)S(1)}, u32[]{:S(2)}, u32[]{:S(2)}) %collective-permute-start.30) | collective-permute-done | bytes 131104 | tf_op jit(solution)/shard_map/ppermute | solution.py:286
  126.7 1.1 collective-permute-start.32
  128.5 8.6 %shard_map.103 = (bf16[128,2048]{1,0:T(8,128)(2,1)}, bf16[128,2048]{1,0:T(8,128)(2,1)}) custom-call(bf16[128,2048]{1,0:T(8,128)(2,1)} %copy-done.5, bf16[128,2048]{1,0:T(8,128)(2,1)} %copy-done.19, bf16[2048,2048]{1,0:T(8,128)(2,1)} %bitcast.81, bf16[2048,2048]{1,0:T(8,128)(2,1)} %bitcast.85, bf16[128,2048]{1,0:T(8,128)(2,1)} %copy-done.4), custom_call_target="tpu_custom_call" | custom-call | flops 4000000000 | bytes 1000 | tf_op jit(solution)/shard_map/pallas_call | solution.py:144
  137.3 1.4 collective-permute-start.41
  139.3 1.1 collective-permute-start.47
  140.4 2.7 %collective-permute-done.41 = bf16[32,2048]{1,0:T(8,128)(2,1)S(1)} collective-permute-done((bf16[32,2048]{1,0:T(8,128)(2,1)S(1)}, bf16[32,2048]{1,0:T(8,128)(2,1)S(1)}, u32[]{:S(2)}, u32[]{:S(2)}) %collective-permute-start.41) | collective-permute-done | bytes 131104 | tf_op jit(solution)/shard_map/ppermute | solution.py:286
  143.0 2.9 %collective-permute-done.40 = bf16[32,2048]{1,0:T(8,128)(2,1)S(1)} collective-permute-done((bf16[32,2048]{1,0:T(8,128)(2,1)S(1)}, bf16[32,2048]{1,0:T(8,128)(2,1)S(1)}, u32[]{:S(2)}, u32[]{:S(2)}) %collective-permute-start.40) | collective-permute-done | bytes 131104 | tf_op jit(solution)/shard_map/ppermute | solution.py:286
  146.8 2.5 %collective-permute-start.51 = (bf16[128,2048]{1,0:T(8,128)(2,1)S(1)}, bf16[128,2048]{1,0:T(8,128)(2,1)S(1)}, u32[]{:S(2)}, u32[]{:S(2)}) collective-permute-start(bf16[128,2048]{1,0:T(8,128)(2,1)S(1)} %fusion.5.refs_2_), channel_id=1, source_target_pairs={{0,2},{1,3},{2,6},{3,7},{6,4},{7,5},{4,0},{5,1},{8,10},{9,11},{10,... | collective-permute-start | bytes 1572872 | tf_op jit(solution)/shard_map/ring/ppermute | solution.py:197
  150.0 8.6 %shard_map.101 = (bf16[128,2048]{1,0:T(8,128)(2,1)}, bf16[128,2048]{1,0:T(8,128)(2,1)}) custom-call(bf16[128,2048]{1,0:T(8,128)(2,1)} %copy-done.4, bf16[128,2048]{1,0:T(8,128)(2,1)} %copy-done.15, bf16[2048,2048]{1,0:T(8,128)(2,1)} %bitcast.82, bf16[2048,2048]{1,0:T(8,128)(2,1)} %bitcast.86), custom_call_target="tpu_custom_call" | custom-call | flops 4000000000 | bytes 1000 | tf_op jit(solution)/shard_map/pallas_call | solution.py:144
  158.9 1.7 collective-permute-start.49
  160.8 1.0 collective-permute-start.46
  161.8 8.6 %shard_map.104 = (bf16[128,2048]{1,0:T(8,128)(2,1)}, bf16[128,2048]{1,0:T(8,128)(2,1)}) custom-call(bf16[128,2048]{1,0:T(8,128)(2,1)} %copy-done.9, bf16[128,2048]{1,0:T(8,128)(2,1)} %copy-done.6, bf16[2048,2048]{1,0:T(8,128)(2,1)} %bitcast.83, bf16[2048,2048]{1,0:T(8,128)(2,1)} %bitcast.87, bf16[128,2048]{1,0:T(8,128)(2,1)} %copy-done.7, ...), custom_call_target="tpu_custom_call" | custom-call | flops 4000000000 | bytes 1000 | tf_op jit(solution)/shard_map/pallas_call | solution.py:144
  170.4 1.1 collective-permute-start.42
  172.9 2.8 %collective-permute-done.46 = bf16[128,2048]{1,0:T(8,128)(2,1)S(1)} collective-permute-done((bf16[128,2048]{1,0:T(8,128)(2,1)}, bf16[128,2048]{1,0:T(8,128)(2,1)S(1)}, u32[]{:S(2)}, u32[]{:S(2)}) %collective-permute-start.46) | collective-permute-done | bytes 524320 | tf_op jit(solution)/shard_map/half/ppermute | solution.py:201
  176.5 1.3 collective-permute-start.52
  177.9 8.5 %collective-permute-done.42 = bf16[128,2048]{1,0:T(8,128)(2,1)S(1)} collective-permute-done((bf16[128,2048]{1,0:T(8,128)(2,1)}, bf16[128,2048]{1,0:T(8,128)(2,1)S(1)}, u32[]{:S(2)}, u32[]{:S(2)}) %collective-permute-start.42) | collective-permute-done | bytes 524320 | tf_op jit(solution)/shard_map/half/ppermute | solution.py:201
  186.4 1.2 add_convert_fusion.2
  189.1 1.3 collective-permute-start.44
  191.0 3.9 %collective-permute-done.45 = bf16[32,2048]{1,0:T(8,128)(2,1)S(1)} collective-permute-done((bf16[32,2048]{1,0:T(8,128)(2,1)S(1)}, bf16[32,2048]{1,0:T(8,128)(2,1)S(1)}, u32[]{:S(2)}, u32[]{:S(2)}) %collective-permute-start.45) | collective-permute-done | bytes 131104 | tf_op jit(solution)/shard_map/ppermute | solution.py:286
  194.9 2.5 %collective-permute-done.44 = bf16[32,2048]{1,0:T(8,128)(2,1)S(1)} collective-permute-done((bf16[32,2048]{1,0:T(8,128)(2,1)S(1)}, bf16[32,2048]{1,0:T(8,128)(2,1)S(1)}, u32[]{:S(2)}, u32[]{:S(2)}) %collective-permute-start.44) | collective-permute-done | bytes 131104 | tf_op jit(solution)/shard_map/ppermute | solution.py:286
  197.8 4.9 %collective-permute-done.56 = bf16[128,2048]{1,0:T(8,128)(2,1)S(1)} collective-permute-done((bf16[128,2048]{1,0:T(8,128)(2,1)S(1)}, bf16[128,2048]{1,0:T(8,128)(2,1)S(1)}, u32[]{:S(2)}, u32[]{:S(2)}) %collective-permute-start.56) | collective-permute-done | bytes 524320 | tf_op jit(solution)/shard_map/home/ring/ppermute | solution.py:197
  202.7 1.2 fusion.8
  (184 shorter events, 24.9 us)
Async XLA Ops:
  1.3 16.1 %collective-permute-start.2 = (bf16[256,1024]{1,0:T(8,128)(2,1)S(1)}, bf16[256,1024]{1,0:T(8,128)(2,1)}, u32[]{:S(2)}, u32[]{:S(2)}) collective-permute-start(bf16[256,1024]{1,0:T(8,128)(2,1)S(1)} %constant_dynamic-slice_fusion), channel_id=1, source_target_pairs={{0,2},{1,3},{2,6},{3,7},{6,4},{7,5},{4,0},{5,1},{8,10},{9,11},{10,... | collective-permute-start | bytes 1572872 | tf_op jit(solution)/shard_map/gather_0/ring/ppermute | solution.py:197
  4.3 13.4 %collective-permute-start.1 = (bf16[256,1024]{1,0:T(8,128)(2,1)S(1)}, bf16[256,1024]{1,0:T(8,128)(2,1)S(1)}, u32[]{:S(2)}, u32[]{:S(2)}) collective-permute-start(bf16[256,1024]{1,0:T(8,128)(2,1)S(1)} %constant_dynamic-slice_fusion), channel_id=1, source_target_pairs={{0,1},{1,0},{2,3},{3,2},{4,5},{5,4},{6,7},{7,6},{8,9},{9,8},{10,11... | collective-permute-start | bytes 1572872 | tf_op jit(solution)/shard_map/gather_0/half/ppermute | solution.py:201
  5.9 13.3 %collective-permute-start.3 = (bf16[128,2048]{1,0:T(8,128)(2,1)}, bf16[128,2048]{1,0:T(8,128)(2,1)S(1)}, u32[]{:S(2)}, u32[]{:S(2)}) collective-permute-start(bf16[128,2048]{1,0:T(8,128)(2,1)} %bitcast.95), channel_id=1, source_target_pairs={{0,16},{8,24},{16,0},{24,8},{1,17},{9,25},{17,1},{25,9},{2,18},{10... | collective-permute-start | bytes 1572872 | tf_op jit(solution)/shard_map/gather_0/ppermute | solution.py:228
  19.2 19.0 %copy-start.12 = (bf16[128,2048]{1,0:T(8,128)(2,1)}, bf16[128,2048]{1,0:T(8,128)(2,1)S(1)}, u32[]{:S(2)}) copy-start(bf16[128,2048]{1,0:T(8,128)(2,1)S(1)} %collective-permute-done.3.refs_3_) | copy-start | bytes 1572868
  19.2 12.4 %collective-permute-start.8 = (bf16[128,2048]{1,0:T(8,128)(2,1)}, bf16[128,2048]{1,0:T(8,128)(2,1)S(1)}, u32[]{:S(2)}, u32[]{:S(2)}) collective-permute-start(bf16[128,2048]{1,0:T(8,128)(2,1)} %bitcast.98), channel_id=1, source_target_pairs={{0,16},{8,24},{16,0},{24,8},{1,17},{9,25},{17,1},{25,9},{2,18},{10... | collective-permute-start | bytes 1572872 | tf_op jit(solution)/shard_map/gather_1/ppermute | solution.py:228
  20.7 13.1 %collective-permute-start.7 = (bf16[256,1024]{1,0:T(8,128)(2,1)}, bf16[256,1024]{1,0:T(8,128)(2,1)}, u32[]{:S(2)}, u32[]{:S(2)}) collective-permute-start(bf16[256,1024]{1,0:T(8,128)(2,1)} %collective-permute-done.2), channel_id=1, source_target_pairs={{0,2},{1,3},{2,6},{3,7},{6,4},{7,5},{4,0},{5,1},{8,10},{9,11},{10,... | collective-permute-start | bytes 1572872 | tf_op jit(solution)/shard_map/gather_1/ring/ppermute | solution.py:197
  23.3 11.9 %collective-permute-start.6 = (bf16[256,1024]{1,0:T(8,128)(2,1)}, bf16[256,1024]{1,0:T(8,128)(2,1)}, u32[]{:S(2)}, u32[]{:S(2)}) collective-permute-start(bf16[256,1024]{1,0:T(8,128)(2,1)} %collective-permute-done.2), channel_id=1, source_target_pairs={{0,1},{1,0},{2,3},{3,2},{4,5},{5,4},{6,7},{7,6},{8,9},{9,8},{10,11... | collective-permute-start | bytes 1572872 | tf_op jit(solution)/shard_map/gather_1/half/ppermute | solution.py:201
  24.1 12.6 %collective-permute-start = (bf16[128,2048]{1,0:T(8,128)(2,1)}, bf16[128,2048]{1,0:T(8,128)(2,1)S(1)}, u32[]{:S(2)}, u32[]{:S(2)}) collective-permute-start(bf16[128,2048]{1,0:T(8,128)(2,1)} %bitcast.96), channel_id=1, source_target_pairs={{0,8},{8,0},{16,24},{24,16},{1,9},{9,1},{17,25},{25,17},{2,10},{10... | collective-permute-start | bytes 1572872 | tf_op jit(solution)/shard_map/core/ppermute | solution.py:205
  24.1 14.1 %collective-permute-start.5 = (bf16[128,2048]{1,0:T(8,128)(2,1)}, bf16[128,2048]{1,0:T(8,128)(2,1)}, u32[]{:S(2)}, u32[]{:S(2)}) collective-permute-start(bf16[128,2048]{1,0:T(8,128)(2,1)} %bitcast.99), channel_id=1, source_target_pairs={{0,8},{8,0},{16,24},{24,16},{1,9},{9,1},{17,25},{25,17},{2,10},{10... | collective-permute-start | bytes 1572872 | tf_op jit(solution)/shard_map/core/ppermute | solution.py:205
  31.6 6.6 %collective-permute-start.4 = (bf16[128,2048]{1,0:T(8,128)(2,1)S(1)}, bf16[128,2048]{1,0:T(8,128)(2,1)}, u32[]{:S(2)}, u32[]{:S(2)}) collective-permute-start(bf16[128,2048]{1,0:T(8,128)(2,1)S(1)} %collective-permute-done.3.refs_3_), channel_id=1, source_target_pairs={{0,8},{8,0},{16,24},{24,16},{1,9},{9,1},{17,25},{25,17},{2,10},{10... | collective-permute-start | bytes 1572872 | tf_op jit(solution)/shard_map/core/ppermute | solution.py:205
  35.2 3.0 %collective-permute-start.9 = (bf16[128,2048]{1,0:T(8,128)(2,1)S(1)}, bf16[128,2048]{1,0:T(8,128)(2,1)}, u32[]{:S(2)}, u32[]{:S(2)}) collective-permute-start(bf16[128,2048]{1,0:T(8,128)(2,1)S(1)} %collective-permute-done.8.refs_7_), channel_id=1, source_target_pairs={{0,8},{8,0},{16,24},{24,16},{1,9},{9,1},{17,25},{25,17},{2,10},{10... | collective-permute-start | bytes 1572872 | tf_op jit(solution)/shard_map/core/ppermute | solution.py:205
  35.4 20.6 %collective-permute-start.12 = (bf16[256,1024]{1,0:T(8,128)(2,1)}, bf16[256,1024]{1,0:T(8,128)(2,1)S(1)}, u32[]{:S(2)}, u32[]{:S(2)}) collective-permute-start(bf16[256,1024]{1,0:T(8,128)(2,1)} %collective-permute-done.7), channel_id=1, source_target_pairs={{0,2},{1,3},{2,6},{3,7},{6,4},{7,5},{4,0},{5,1},{8,10},{9,11},{10,... | collective-permute-start | bytes 1572872 | tf_op jit(solution)/shard_map/gather_2/ring/ppermute | solution.py:197
  36.7 19.3 %collective-permute-start.11 = (bf16[256,1024]{1,0:T(8,128)(2,1)}, bf16[256,1024]{1,0:T(8,128)(2,1)S(1)}, u32[]{:S(2)}, u32[]{:S(2)}) collective-permute-start(bf16[256,1024]{1,0:T(8,128)(2,1)} %collective-permute-done.7), channel_id=1, source_target_pairs={{0,1},{1,0},{2,3},{3,2},{4,5},{5,4},{6,7},{7,6},{8,9},{9,8},{10,11... | collective-permute-start | bytes 1572872 | tf_op jit(solution)/shard_map/gather_2/half/ppermute | solution.py:201
  44.4 17.0 %copy-start.2 = (bf16[128,2048]{1,0:T(8,128)(2,1)S(1)}, bf16[128,2048]{1,0:T(8,128)(2,1)}, u32[]{:S(2)}) copy-start(bf16[128,2048]{1,0:T(8,128)(2,1)} %shard_map.100) | copy-start | bytes 1572868
  44.4 17.3 %copy-start.21 = (bf16[256,1024]{1,0:T(8,128)(2,1)S(1)}, bf16[256,1024]{1,0:T(8,128)(2,1)}, u32[]{:S(2)}) copy-start(bf16[256,1024]{1,0:T(8,128)(2,1)} %copy-done.20) | copy-start | bytes 1572868
  44.4 13.0 %collective-permute-start.10 = (bf16[128,2048]{1,0:T(8,128)(2,1)}, bf16[128,2048]{1,0:T(8,128)(2,1)S(1)}, u32[]{:S(2)}, u32[]{:S(2)}) collective-permute-start(bf16[128,2048]{1,0:T(8,128)(2,1)} %shard_map.100), channel_id=1, source_target_pairs={{0,8},{8,0},{16,24},{24,16},{1,9},{9,1},{17,25},{25,17},{2,10},{10... | collective-permute-start | bytes 1572872 | tf_op jit(solution)/shard_map/core/ppermute | solution.py:205
  44.5 7.2 %collective-permute-start.33 = (s32[2,128]{0,1:T(8,128)S(1)}, s32[2,128]{0,1:T(8,128)S(1)}, u32[]{:S(2)}, u32[]{:S(2)}) collective-permute-start(s32[2,128]{0,1:T(8,128)S(1)} %bitcast.91), channel_id=1, source_target_pairs={{0,6},{1,7},{2,4},{3,5},{6,0},{7,1},{4,2},{5,3},{8,14},{9,15},{10,... | collective-permute-start | bytes 3080 | tf_op jit(solution)/shard_map/gather_0/ring/ppermute | solution.py:197
  45.5 10.3 %collective-permute-start.26 = (s32[2,128]{0,1:T(8,128)S(1)}, s32[2,128]{0,1:T(8,128)S(1)}, u32[]{:S(2)}, u32[]{:S(2)}) collective-permute-start(s32[2,128]{0,1:T(8,128)S(1)} %bitcast.92), channel_id=1, source_target_pairs={{0,4},{1,5},{2,0},{3,1},{6,2},{7,3},{4,6},{5,7},{8,12},{9,13},{10,... | collective-permute-start | bytes 3080 | tf_op jit(solution)/shard_map/gather_0/ring/ppermute | solution.py:197
  51.7 14.8 %collective-permute-start.20 = (s32[2,128]{0,1:T(8,128)S(1)}, s32[2,128]{0,1:T(8,128)S(1)}, u32[]{:S(2)}, u32[]{:S(2)}) collective-permute-start(s32[2,128]{0,1:T(8,128)S(1)} %bitcast.93), channel_id=1, source_target_pairs={{0,2},{1,3},{2,6},{3,7},{6,4},{7,5},{4,0},{5,1},{8,10},{9,11},{10,... | collective-permute-start | bytes 3080 | tf_op jit(solution)/shard_map/gather_0/ring/ppermute | solution.py:197
  56.0 7.7 %collective-permute-start.13 = (bf16[128,1024]{1,0:T(8,128)(2,1)S(1)}, bf16[128,1024]{1,0:T(8,128)(2,1)S(1)}, u32[]{:S(2)}, u32[]{:S(2)}) collective-permute-start(bf16[128,1024]{1,0:T(8,128)(2,1)S(1)} %slice.180), channel_id=1, source_target_pairs={{0,1},{1,0},{2,3},{3,2},{4,5},{5,4},{6,7},{7,6},{8,9},{9,8},{10,11... | collective-permute-start | bytes 786440 | tf_op jit(solution)/shard_map/half/ppermute | solution.py:201
  57.2 8.3 %collective-permute-start.14 = (bf16[128,1024]{1,0:T(8,128)(2,1)S(1)}, bf16[128,1024]{1,0:T(8,128)(2,1)S(1)}, u32[]{:S(2)}, u32[]{:S(2)}) collective-permute-start(bf16[128,1024]{1,0:T(8,128)(2,1)S(1)} %slice.181), channel_id=1, source_target_pairs={{0,2},{1,3},{2,6},{3,7},{6,4},{7,5},{4,0},{5,1},{8,10},{9,11},{10,... | collective-permute-start | bytes 786440 | tf_op jit(solution)/shard_map/ring/ppermute | solution.py:197
  66.5 2.0 collective-permute-start.15
  69.3 14.9 %collective-permute-start.21 = (bf16[128,2048]{1,0:T(8,128)(2,1)S(1)}, bf16[128,2048]{1,0:T(8,128)(2,1)S(1)}, u32[]{:S(2)}, u32[]{:S(2)}) collective-permute-start(bf16[128,2048]{1,0:T(8,128)(2,1)S(1)} %multiply_convert_fusion), channel_id=1, source_target_pairs={{0,2},{1,3},{2,6},{3,7},{6,4},{7,5},{4,0},{5,1},{8,10},{9,11},{10,... | collective-permute-start | bytes 1572872 | tf_op jit(solution)/shard_map/ring/ppermute | solution.py:197
  70.6 5.8 %collective-permute-start.18 = (bf16[32,2048]{1,0:T(8,128)(2,1)S(1)}, bf16[32,2048]{1,0:T(8,128)(2,1)S(1)}, u32[]{:S(2)}, u32[]{:S(2)}) collective-permute-start(bf16[32,2048]{1,0:T(8,128)(2,1)S(1)} %get-tuple-element.94), channel_id=1, source_target_pairs={{0,24},{8,16},{16,8},{24,0},{1,25},{9,17},{17,9},{25,1},{2,26},{10... | collective-permute-start | bytes 393224 | tf_op jit(solution)/shard_map/ppermute | solution.py:286
  70.7 8.6 %collective-permute-start.17 = (bf16[32,2048]{1,0:T(8,128)(2,1)S(1)}, bf16[32,2048]{1,0:T(8,128)(2,1)S(1)}, u32[]{:S(2)}, u32[]{:S(2)}) collective-permute-start(bf16[32,2048]{1,0:T(8,128)(2,1)S(1)} %get-tuple-element.95), channel_id=1, source_target_pairs={{0,16},{8,24},{16,0},{24,8},{1,17},{9,25},{17,1},{25,9},{2,18},{10... | collective-permute-start | bytes 393224 | tf_op jit(solution)/shard_map/ppermute | solution.py:286
  72.1 7.1 %collective-permute-start.16 = (bf16[32,2048]{1,0:T(8,128)(2,1)S(1)}, bf16[32,2048]{1,0:T(8,128)(2,1)S(1)}, u32[]{:S(2)}, u32[]{:S(2)}) collective-permute-start(bf16[32,2048]{1,0:T(8,128)(2,1)S(1)} %get-tuple-element.96), channel_id=1, source_target_pairs={{0,8},{8,0},{16,24},{24,16},{1,9},{9,1},{17,25},{25,17},{2,10},{10... | collective-permute-start | bytes 393224 | tf_op jit(solution)/shard_map/ppermute | solution.py:286
  79.3 37.0 %copy-start.9 = (bf16[128,2048]{1,0:T(8,128)(2,1)}, bf16[128,2048]{1,0:T(8,128)(2,1)S(1)}, u32[]{:S(2)}) copy-start(bf16[128,2048]{1,0:T(8,128)(2,1)S(1)} %pad_maximum_fusion.own_ref) | copy-start | bytes 1572868
  79.3 14.2 %collective-permute-start.19 = (bf16[128,2048]{1,0:T(8,128)(2,1)S(1)}, bf16[128,2048]{1,0:T(8,128)(2,1)S(1)}, u32[]{:S(2)}, u32[]{:S(2)}) collective-permute-start(bf16[128,2048]{1,0:T(8,128)(2,1)S(1)} %pad_maximum_fusion.own_ref), channel_id=1, source_target_pairs={{0,1},{1,0},{2,3},{3,2},{4,5},{5,4},{6,7},{7,6},{8,9},{9,8},{10,11... | collective-permute-start | bytes 1572872 | tf_op jit(solution)/shard_map/half/ppermute | solution.py:201
  84.2 14.0 %collective-permute-start.27 = (bf16[128,2048]{1,0:T(8,128)(2,1)S(1)}, bf16[128,2048]{1,0:T(8,128)(2,1)S(1)}, u32[]{:S(2)}, u32[]{:S(2)}) collective-permute-start(bf16[128,2048]{1,0:T(8,128)(2,1)S(1)} %collective-permute-done.21), channel_id=1, source_target_pairs={{0,2},{1,3},{2,6},{3,7},{6,4},{7,5},{4,0},{5,1},{8,10},{9,11},{10,... | collective-permute-start | bytes 1572872 | tf_op jit(solution)/shard_map/ring/ppermute | solution.py:197
  84.7 5.8 %collective-permute-start.24 = (bf16[32,2048]{1,0:T(8,128)(2,1)S(1)}, bf16[32,2048]{1,0:T(8,128)(2,1)S(1)}, u32[]{:S(2)}, u32[]{:S(2)}) collective-permute-start(bf16[32,2048]{1,0:T(8,128)(2,1)S(1)} %get-tuple-element.90), channel_id=1, source_target_pairs={{0,24},{8,16},{16,8},{24,0},{1,25},{9,17},{17,9},{25,1},{2,26},{10... | collective-permute-start | bytes 393224 | tf_op jit(solution)/shard_map/ppermute | solution.py:286
  84.8 7.6 %collective-permute-start.23 = (bf16[32,2048]{1,0:T(8,128)(2,1)S(1)}, bf16[32,2048]{1,0:T(8,128)(2,1)S(1)}, u32[]{:S(2)}, u32[]{:S(2)}) collective-permute-start(bf16[32,2048]{1,0:T(8,128)(2,1)S(1)} %get-tuple-element.91), channel_id=1, source_target_pairs={{0,16},{8,24},{16,0},{24,8},{1,17},{9,25},{17,1},{25,9},{2,18},{10... | collective-permute-start | bytes 393224 | tf_op jit(solution)/shard_map/ppermute | solution.py:286
  85.7 6.7 %collective-permute-start.22 = (bf16[32,2048]{1,0:T(8,128)(2,1)S(1)}, bf16[32,2048]{1,0:T(8,128)(2,1)S(1)}, u32[]{:S(2)}, u32[]{:S(2)}) collective-permute-start(bf16[32,2048]{1,0:T(8,128)(2,1)S(1)} %get-tuple-element.92), channel_id=1, source_target_pairs={{0,8},{8,0},{16,24},{24,16},{1,9},{9,1},{17,25},{25,17},{2,10},{10... | collective-permute-start | bytes 393224 | tf_op jit(solution)/shard_map/ppermute | solution.py:286
  92.4 14.5 %collective-permute-start.25 = (bf16[128,2048]{1,0:T(8,128)(2,1)S(1)}, bf16[128,2048]{1,0:T(8,128)(2,1)S(1)}, u32[]{:S(2)}, u32[]{:S(2)}) collective-permute-start(bf16[128,2048]{1,0:T(8,128)(2,1)S(1)} %pad_maximum_fusion.1.own_ref), channel_id=1, source_target_pairs={{0,1},{1,0},{2,3},{3,2},{4,5},{5,4},{6,7},{7,6},{8,9},{9,8},{10,11... | collective-permute-start | bytes 1572872 | tf_op jit(solution)/shard_map/half/ppermute | solution.py:201
  98.7 5.8 %collective-permute-start.36 = (bf16[32,2048]{1,0:T(8,128)(2,1)S(1)}, bf16[32,2048]{1,0:T(8,128)(2,1)S(1)}, u32[]{:S(2)}, u32[]{:S(2)}) collective-permute-start(bf16[32,2048]{1,0:T(8,128)(2,1)S(1)} %get-tuple-element.82), channel_id=1, source_target_pairs={{0,24},{8,16},{16,8},{24,0},{1,25},{9,17},{17,9},{25,1},{2,26},{10... | collective-permute-start | bytes 393224 | tf_op jit(solution)/shard_map/ppermute | solution.py:286
  98.8 6.8 %collective-permute-start.35 = (bf16[32,2048]{1,0:T(8,128)(2,1)S(1)}, bf16[32,2048]{1,0:T(8,128)(2,1)S(1)}, u32[]{:S(2)}, u32[]{:S(2)}) collective-permute-start(bf16[32,2048]{1,0:T(8,128)(2,1)S(1)} %get-tuple-element.83), channel_id=1, source_target_pairs={{0,16},{8,24},{16,0},{24,8},{1,17},{9,25},{17,1},{25,9},{2,18},{10... | collective-permute-start | bytes 393224 | tf_op jit(solution)/shard_map/ppermute | solution.py:286
  99.4 6.2 %collective-permute-start.34 = (bf16[32,2048]{1,0:T(8,128)(2,1)S(1)}, bf16[32,2048]{1,0:T(8,128)(2,1)S(1)}, u32[]{:S(2)}, u32[]{:S(2)}) collective-permute-start(bf16[32,2048]{1,0:T(8,128)(2,1)S(1)} %get-tuple-element.84), channel_id=1, source_target_pairs={{0,8},{8,0},{16,24},{24,16},{1,9},{9,1},{17,25},{25,17},{2,10},{10... | collective-permute-start | bytes 393224 | tf_op jit(solution)/shard_map/ppermute | solution.py:286
  100.6 16.8 %collective-permute-start.28 = (bf16[128,2048]{1,0:T(8,128)(2,1)S(1)}, bf16[128,2048]{1,0:T(8,128)(2,1)S(1)}, u32[]{:S(2)}, u32[]{:S(2)}) collective-permute-start(bf16[128,2048]{1,0:T(8,128)(2,1)S(1)} %collective-permute-done.27), channel_id=1, source_target_pairs={{0,2},{1,3},{2,6},{3,7},{6,4},{7,5},{4,0},{5,1},{8,10},{9,11},{10,... | collective-permute-start | bytes 1572872 | tf_op jit(solution)/shard_map/ring/ppermute | solution.py:197
  105.6 22.1 %collective-permute-start.37 = (bf16[128,2048]{1,0:T(8,128)(2,1)S(1)}, bf16[128,2048]{1,0:T(8,128)(2,1)S(1)}, u32[]{:S(2)}, u32[]{:S(2)}) collective-permute-start(bf16[128,2048]{1,0:T(8,128)(2,1)S(1)} %pad_maximum_fusion.3.refs_1_.own_ref), channel_id=1, source_target_pairs={{0,1},{1,0},{2,3},{3,2},{4,5},{5,4},{6,7},{7,6},{8,9},{9,8},{10,11... | collective-permute-start | bytes 1572872 | tf_op jit(solution)/shard_map/half/ppermute | solution.py:201
  116.3 20.8 %collective-permute-start.38 = (bf16[128,2048]{1,0:T(8,128)(2,1)}, bf16[128,2048]{1,0:T(8,128)(2,1)S(1)}, u32[]{:S(2)}, u32[]{:S(2)}) collective-permute-start(bf16[128,2048]{1,0:T(8,128)(2,1)} %get-tuple-element.45), channel_id=1, source_target_pairs={{0,1},{1,0},{2,3},{3,2},{4,5},{5,4},{6,7},{7,6},{8,9},{9,8},{10,11... | collective-permute-start | bytes 1572872 | tf_op jit(solution)/shard_map/half/ppermute | solution.py:201
  117.9 5.2 %collective-permute-start.31 = (bf16[32,2048]{1,0:T(8,128)(2,1)S(1)}, bf16[32,2048]{1,0:T(8,128)(2,1)S(1)}, u32[]{:S(2)}, u32[]{:S(2)}) collective-permute-start(bf16[32,2048]{1,0:T(8,128)(2,1)S(1)} %get-tuple-element.86), channel_id=1, source_target_pairs={{0,24},{8,16},{16,8},{24,0},{1,25},{9,17},{17,9},{25,1},{2,26},{10... | collective-permute-start | bytes 393224 | tf_op jit(solution)/shard_map/ppermute | solution.py:286
  119.2 7.4 %collective-permute-start.30 = (bf16[32,2048]{1,0:T(8,128)(2,1)S(1)}, bf16[32,2048]{1,0:T(8,128)(2,1)S(1)}, u32[]{:S(2)}, u32[]{:S(2)}) collective-permute-start(bf16[32,2048]{1,0:T(8,128)(2,1)S(1)} %get-tuple-element.87), channel_id=1, source_target_pairs={{0,16},{8,24},{16,0},{24,8},{1,17},{9,25},{17,1},{25,9},{2,18},{10... | collective-permute-start | bytes 393224 | tf_op jit(solution)/shard_map/ppermute | solution.py:286
  120.2 6.4 %collective-permute-start.29 = (bf16[32,2048]{1,0:T(8,128)(2,1)S(1)}, bf16[32,2048]{1,0:T(8,128)(2,1)S(1)}, u32[]{:S(2)}, u32[]{:S(2)}) collective-permute-start(bf16[32,2048]{1,0:T(8,128)(2,1)S(1)} %get-tuple-element.88), channel_id=1, source_target_pairs={{0,8},{8,0},{16,24},{24,16},{1,9},{9,1},{17,25},{25,17},{2,10},{10... | collective-permute-start | bytes 393224 | tf_op jit(solution)/shard_map/ppermute | solution.py:286
  126.7 22.6 %collective-permute-start.32 = (bf16[128,2048]{1,0:T(8,128)(2,1)S(1)}, bf16[128,2048]{1,0:T(8,128)(2,1)S(1)}, u32[]{:S(2)}, u32[]{:S(2)}) collective-permute-start(bf16[128,2048]{1,0:T(8,128)(2,1)S(1)} %pad_maximum_fusion.2.own_ref.refs_0_), channel_id=1, source_target_pairs={{0,1},{1,0},{2,3},{3,2},{4,5},{5,4},{6,7},{7,6},{8,9},{9,8},{10,11... | collective-permute-start | bytes 1572872 | tf_op jit(solution)/shard_map/half/ppermute | solution.py:201
  137.3 5.7 %collective-permute-start.41 = (bf16[32,2048]{1,0:T(8,128)(2,1)S(1)}, bf16[32,2048]{1,0:T(8,128)(2,1)S(1)}, u32[]{:S(2)}, u32[]{:S(2)}) collective-permute-start(bf16[32,2048]{1,0:T(8,128)(2,1)S(1)} %get-tuple-element.78), channel_id=1, source_target_pairs={{0,24},{8,16},{16,8},{24,0},{1,25},{9,17},{17,9},{25,1},{2,26},{10... | collective-permute-start | bytes 393224 | tf_op jit(solution)/shard_map/ppermute | solution.py:286
  138.7 7.3 %collective-permute-start.40 = (bf16[32,2048]{1,0:T(8,128)(2,1)S(1)}, bf16[32,2048]{1,0:T(8,128)(2,1)S(1)}, u32[]{:S(2)}, u32[]{:S(2)}) collective-permute-start(bf16[32,2048]{1,0:T(8,128)(2,1)S(1)} %get-tuple-element.79), channel_id=1, source_target_pairs={{0,16},{8,24},{16,0},{24,8},{1,17},{9,25},{17,1},{25,9},{2,18},{10... | collective-permute-start | bytes 393224 | tf_op jit(solution)/shard_map/ppermute | solution.py:286
  139.0 7.0 %collective-permute-start.39 = (bf16[32,2048]{1,0:T(8,128)(2,1)S(1)}, bf16[32,2048]{1,0:T(8,128)(2,1)S(1)}, u32[]{:S(2)}, u32[]{:S(2)}) collective-permute-start(bf16[32,2048]{1,0:T(8,128)(2,1)S(1)} %get-tuple-element.80), channel_id=1, source_target_pairs={{0,8},{8,0},{16,24},{24,16},{1,9},{9,1},{17,25},{25,17},{2,10},{10... | collective-permute-start | bytes 393224 | tf_op jit(solution)/shard_map/ppermute | solution.py:286
  139.3 19.4 %collective-permute-start.47 = (bf16[128,2048]{1,0:T(8,128)(2,1)}, bf16[128,2048]{1,0:T(8,128)(2,1)S(1)}, u32[]{:S(2)}, u32[]{:S(2)}) collective-permute-start(bf16[128,2048]{1,0:T(8,128)(2,1)} %get-tuple-element.51), channel_id=1, source_target_pairs={{0,1},{1,0},{2,3},{3,2},{4,5},{5,4},{6,7},{7,6},{8,9},{9,8},{10,11... | collective-permute-start | bytes 1572872 | tf_op jit(solution)/shard_map/half/ppermute | solution.py:201
  146.8 15.0 %copy-start.17 = (bf16[128,2048]{1,0:T(8,128)(2,1)}, bf16[128,2048]{1,0:T(8,128)(2,1)S(1)}, u32[]{:S(2)}) copy-start(bf16[128,2048]{1,0:T(8,128)(2,1)S(1)} %fusion.5.refs_2_) | copy-start | bytes 1572868
  146.8 25.1 %collective-permute-start.51 = (bf16[128,2048]{1,0:T(8,128)(2,1)S(1)}, bf16[128,2048]{1,0:T(8,128)(2,1)S(1)}, u32[]{:S(2)}, u32[]{:S(2)}) collective-permute-start(bf16[128,2048]{1,0:T(8,128)(2,1)S(1)} %fusion.5.refs_2_), channel_id=1, source_target_pairs={{0,2},{1,3},{2,6},{3,7},{6,4},{7,5},{4,0},{5,1},{8,10},{9,11},{10,... | collective-permute-start | bytes 1572872 | tf_op jit(solution)/shard_map/ring/ppermute | solution.py:197
  158.9 11.5 %collective-permute-start.50 = (bf16[32,2048]{1,0:T(8,128)(2,1)S(1)}, bf16[32,2048]{1,0:T(8,128)(2,1)S(1)}, u32[]{:S(2)}, u32[]{:S(2)}) collective-permute-start(bf16[32,2048]{1,0:T(8,128)(2,1)S(1)} %get-tuple-element.70), channel_id=1, source_target_pairs={{0,24},{8,16},{16,8},{24,0},{1,25},{9,17},{17,9},{25,1},{2,26},{10... | collective-permute-start | bytes 393224 | tf_op jit(solution)/shard_map/ppermute | solution.py:286
  158.9 12.6 %collective-permute-start.49 = (bf16[32,2048]{1,0:T(8,128)(2,1)S(1)}, bf16[32,2048]{1,0:T(8,128)(2,1)S(1)}, u32[]{:S(2)}, u32[]{:S(2)}) collective-permute-start(bf16[32,2048]{1,0:T(8,128)(2,1)S(1)} %get-tuple-element.71), channel_id=1, source_target_pairs={{0,16},{8,24},{16,0},{24,8},{1,17},{9,25},{17,1},{25,9},{2,18},{10... | collective-permute-start | bytes 393224 | tf_op jit(solution)/shard_map/ppermute | solution.py:286
  160.6 10.9 %collective-permute-start.48 = (bf16[32,2048]{1,0:T(8,128)(2,1)S(1)}, bf16[32,2048]{1,0:T(8,128)(2,1)S(1)}, u32[]{:S(2)}, u32[]{:S(2)}) collective-permute-start(bf16[32,2048]{1,0:T(8,128)(2,1)S(1)} %get-tuple-element.72), channel_id=1, source_target_pairs={{0,8},{8,0},{16,24},{24,16},{1,9},{9,1},{17,25},{25,17},{2,10},{10... | collective-permute-start | bytes 393224 | tf_op jit(solution)/shard_map/ppermute | solution.py:286
  160.8 15.0 %copy-start.8 = (bf16[128,2048]{1,0:T(8,128)(2,1)S(1)}, bf16[128,2048]{1,0:T(8,128)(2,1)}, u32[]{:S(2)}) copy-start(bf16[128,2048]{1,0:T(8,128)(2,1)} %get-tuple-element.48.refs_1_) | copy-start | bytes 1572868
  160.8 15.0 %collective-permute-start.46 = (bf16[128,2048]{1,0:T(8,128)(2,1)}, bf16[128,2048]{1,0:T(8,128)(2,1)S(1)}, u32[]{:S(2)}, u32[]{:S(2)}) collective-permute-start(bf16[128,2048]{1,0:T(8,128)(2,1)} %get-tuple-element.49), channel_id=1, source_target_pairs={{0,1},{1,0},{2,3},{3,2},{4,5},{5,4},{6,7},{7,6},{8,9},{9,8},{10,11... | collective-permute-start | bytes 1572872 | tf_op jit(solution)/shard_map/half/ppermute | solution.py:201
  170.4 16.0 %collective-permute-start.42 = (bf16[128,2048]{1,0:T(8,128)(2,1)}, bf16[128,2048]{1,0:T(8,128)(2,1)S(1)}, u32[]{:S(2)}, u32[]{:S(2)}) collective-permute-start(bf16[128,2048]{1,0:T(8,128)(2,1)} %get-tuple-element.47), channel_id=1, source_target_pairs={{0,1},{1,0},{2,3},{3,2},{4,5},{5,4},{6,7},{7,6},{8,9},{9,8},{10,11... | collective-permute-start | bytes 1572872 | tf_op jit(solution)/shard_map/half/ppermute | solution.py:201
  171.9 32.0 %copy-start.1 = (bf16[256,2048]{1,0:T(8,128)(2,1)S(1)}, bf16[256,2048]{1,0:T(8,128)(2,1)}, u32[]{:S(2)}) copy-start(bf16[256,2048]{1,0:T(8,128)(2,1)} %param.14) | copy-start | bytes 3145732
  172.3 15.7 %collective-permute-start.55 = (bf16[128,2048]{1,0:T(8,128)(2,1)S(1)}, bf16[128,2048]{1,0:T(8,128)(2,1)S(1)}, u32[]{:S(2)}, u32[]{:S(2)}) collective-permute-start(bf16[128,2048]{1,0:T(8,128)(2,1)S(1)} %fusion.6), channel_id=1, source_target_pairs={{0,2},{1,3},{2,6},{3,7},{6,4},{7,5},{4,0},{5,1},{8,10},{9,11},{10,... | collective-permute-start | bytes 1572872 | tf_op jit(solution)/shard_map/ring/ppermute | solution.py:197
  175.9 11.6 %collective-permute-start.54 = (bf16[32,2048]{1,0:T(8,128)(2,1)S(1)}, bf16[32,2048]{1,0:T(8,128)(2,1)S(1)}, u32[]{:S(2)}, u32[]{:S(2)}) collective-permute-start(bf16[32,2048]{1,0:T(8,128)(2,1)S(1)} %get-tuple-element.66), channel_id=1, source_target_pairs={{0,24},{8,16},{16,8},{24,0},{1,25},{9,17},{17,9},{25,1},{2,26},{10... | collective-permute-start | bytes 393224 | tf_op jit(solution)/shard_map/ppermute | solution.py:286
  176.0 11.6 %collective-permute-start.53 = (bf16[32,2048]{1,0:T(8,128)(2,1)S(1)}, bf16[32,2048]{1,0:T(8,128)(2,1)S(1)}, u32[]{:S(2)}, u32[]{:S(2)}) collective-permute-start(bf16[32,2048]{1,0:T(8,128)(2,1)S(1)} %get-tuple-element.67), channel_id=1, source_target_pairs={{0,16},{8,24},{16,0},{24,8},{1,17},{9,25},{17,1},{25,9},{2,18},{10... | collective-permute-start | bytes 393224 | tf_op jit(solution)/shard_map/ppermute | solution.py:286
  176.5 11.0 %collective-permute-start.52 = (bf16[32,2048]{1,0:T(8,128)(2,1)S(1)}, bf16[32,2048]{1,0:T(8,128)(2,1)S(1)}, u32[]{:S(2)}, u32[]{:S(2)}) collective-permute-start(bf16[32,2048]{1,0:T(8,128)(2,1)S(1)} %get-tuple-element.68), channel_id=1, source_target_pairs={{0,8},{8,0},{16,24},{24,16},{1,9},{9,1},{17,25},{25,17},{2,10},{10... | collective-permute-start | bytes 393224 | tf_op jit(solution)/shard_map/ppermute | solution.py:286
  188.4 14.3 %collective-permute-start.56 = (bf16[128,2048]{1,0:T(8,128)(2,1)S(1)}, bf16[128,2048]{1,0:T(8,128)(2,1)S(1)}, u32[]{:S(2)}, u32[]{:S(2)}) collective-permute-start(bf16[128,2048]{1,0:T(8,128)(2,1)S(1)} %fusion.7), channel_id=1, source_target_pairs={{0,2},{1,3},{2,6},{3,7},{6,4},{7,5},{4,0},{5,1},{8,10},{9,11},{10,... | collective-permute-start | bytes 1572872 | tf_op jit(solution)/shard_map/home/ring/ppermute | solution.py:197
  189.1 5.9 %collective-permute-start.45 = (bf16[32,2048]{1,0:T(8,128)(2,1)S(1)}, bf16[32,2048]{1,0:T(8,128)(2,1)S(1)}, u32[]{:S(2)}, u32[]{:S(2)}) collective-permute-start(bf16[32,2048]{1,0:T(8,128)(2,1)S(1)} %get-tuple-element.74), channel_id=1, source_target_pairs={{0,24},{8,16},{16,8},{24,0},{1,25},{9,17},{17,9},{25,1},{2,26},{10... | collective-permute-start | bytes 393224 | tf_op jit(solution)/shard_map/ppermute | solution.py:286
  189.1 8.2 %collective-permute-start.44 = (bf16[32,2048]{1,0:T(8,128)(2,1)S(1)}, bf16[32,2048]{1,0:T(8,128)(2,1)S(1)}, u32[]{:S(2)}, u32[]{:S(2)}) collective-permute-start(bf16[32,2048]{1,0:T(8,128)(2,1)S(1)} %get-tuple-element.75), channel_id=1, source_target_pairs={{0,16},{8,24},{16,0},{24,8},{1,17},{9,25},{17,1},{25,9},{2,18},{10... | collective-permute-start | bytes 393224 | tf_op jit(solution)/shard_map/ppermute | solution.py:286
  190.5 6.9 %collective-permute-start.43 = (bf16[32,2048]{1,0:T(8,128)(2,1)S(1)}, bf16[32,2048]{1,0:T(8,128)(2,1)S(1)}, u32[]{:S(2)}, u32[]{:S(2)}) collective-permute-start(bf16[32,2048]{1,0:T(8,128)(2,1)S(1)} %get-tuple-element.76), channel_id=1, source_target_pairs={{0,8},{8,0},{16,24},{24,16},{1,9},{9,1},{17,25},{25,17},{2,10},{10... | collective-permute-start | bytes 393224 | tf_op jit(solution)/shard_map/ppermute | solution.py:286
  (16 other events, 78.9 us)

commit v3 on v2

--- a/solution.py
+++ b/solution.py
@@ -9,7 +9,7 @@
 
 HEADS = 16
 HALVES = 2
-TIES = {"E1": ["D0", "W2"], "E2": ["W3"], "H1": ["E2"], "H2": ["E3"], "H3": ["E0"], "E0": ["D1", "E3", "P1"], "X3": ["E0", "P2"], "S1": ["W0"], "Z2": ["W0"], "Z3": ["D0"]}
+TIES = {"E1": ["D0", "W2"], "E2": ["W3"], "H1": ["E2"], "H2": ["P1"], "H3": ["E0"], "E0": ["D1", "E3", "P1"], "X3": ["E0", "P2"], "S1": ["W0"], "Z2": ["W0"], "Z3": ["D0"], "G1": ["E3"], "E3": ["H1"]}
 ECOST = 4000000000
 ACOST = 1000
 
@@ -69,6 +69,7 @@
 
 
 VMEM_BYTES = 56 * 1024 * 1024
+EXPERT_BYTES = 48 * 1024 * 1024
 
 
 def attention(query_rows, key_blocks, value_blocks, head_count, earlier):
@@ -156,7 +157,7 @@
             pltpu.SemaphoreType.DMA((2,)),
             pltpu.SemaphoreType.DMA((4,)),
         ],
-        compiler_params=pltpu.CompilerParams(vmem_limit_bytes=VMEM_BYTES),
+        compiler_params=pltpu.CompilerParams(vmem_limit_bytes=EXPERT_BYTES),
         cost_estimate=pl.CostEstimate(flops=ECOST, bytes_accessed=1000, transcendentals=0),
     )(own_rows, other_rows, first, second, *earlier)
 
@@ -284,7 +285,7 @@
         parts = [rows[i * slot_count : (i + 1) * slot_count] for i in range(seq_count)]
         for i in range(1, seq_count):
             parts[i] = lax.ppermute(parts[i], "seq", swap_pairs(seq_count, i))
-        return jnp.concatenate(parts, axis=0)
+        return tuple(parts)
 
     made = {}
 
@@ -313,7 +314,7 @@
         ).astype(jnp.bfloat16)
 
     def expert_rows(step, ties):
-        return exchange(tied(get(f"S{step}"), ties))
+        return jnp.concatenate(exchange(tied(get(f"S{step}"), ties)), axis=0)
 
     def other_rows(step, ties):
         return other_half(tied(get(f"W{step}"), ties))
@@ -335,7 +336,11 @@
         return exchange(tied(get(f"H{step}"), ties))
 
     def gated_part(step, ties):
-        returned = tied(get(f"X{step}"), ties)
+        parts = get(f"X{step}")
+        if ties:
+            ties = [tie[0] if isinstance(tie, tuple) else tie for tie in ties]
+            parts = lax.optimization_barrier((*parts, *ties))[: len(parts)]
+        returned = jnp.concatenate(parts, axis=0)
         match = matches(step)
         logits = jnp.dot(get(f"Z{step}"), w_router, preferred_element_type=jnp.float32)
         named = (targets[step].T // slot_count)[:, :, None] == expert_ids[None, None, :]

time: 204 us -> 196 us (0.961)
  Pallas kernels: 40.5 us -> 36.4 us
  local copies, waits for them, and re-layouts: 6.55 us -> 4.13 us
    ppermute x24, waiting for transfers between devices: 34.7 us -> 29.1 us  [exchange(): parts[i] = lax.ppermute(parts[i], 'seq', swap_pairs(seq_count, i))]
    ppermute x12, waiting for transfers between devices: 15 us -> 20.2 us  [other_half(): return lax.ppermute(block, 'expert', half_pairs)]
    pallas_call x4, Pallas kernels: 34.4 us -> 30.3 us  [expert_half(): pl.pallas_call(expert_kernel, in_specs=[anywhere] * (4 + len(earlier)), o...]
    unnamed x47 -> x26, local copies, waits for them, and re-layouts: 4.51 us -> 2.09 us
    ppermute x13, starting transfers between devices: 18.5 us -> 16.3 us  [around(): return lax.ppermute(block, 'expert', ring_pairs[hop])]
  transfers between devices with their start and end apart: 57 -> 57, of which waited for: 28 -> 29; matrix products, arithmetic and copies ran while one was open for 9% -> 8% of each run, Pallas kernels for 20% -> 19%
where the time goes in v3:
time: 196 us
  waiting for transfers between devices  89.2 us (46%)
  starting transfers between devices  49.4 us (25%)
  Pallas kernels  36.4 us (19%)
  matrix products  13.5 us (7%)
  local copies, waits for them, and re-layouts  4.13 us (2%)
  other arithmetic  2.57 us (1%)
    ppermute x13, waiting for transfers between devices, around(): return lax.ppermute(block, 'expert', ring_pairs[hop])  30.3 us
    pallas_call x4, Pallas kernels, expert_half(): pl.pallas_call(expert_kernel, in_specs=[anywhere] * (4 + len(earlier)), o...  30.3 us
    ppermute x24, waiting for transfers between devices, exchange(): parts[i] = lax.ppermute(parts[i], 'seq', swap_pairs(seq_count, i))  29.1 us
    ppermute x12, waiting for transfers between devices, other_half(): return lax.ppermute(block, 'expert', half_pairs)  20.2 us
    ppermute x13, starting transfers between devices, around(): return lax.ppermute(block, 'expert', ring_pairs[hop])  16.3 us
    ppermute x24, starting transfers between devices, exchange(): parts[i] = lax.ppermute(parts[i], 'seq', swap_pairs(seq_count, i))  16.1 us
    ppermute x12, starting transfers between devices, other_half(): return lax.ppermute(block, 'expert', half_pairs)  13.3 us
    ppermute x2, waiting for transfers between devices, on_device(): lax.ppermute(sources[which], 'seq', swap_pairs(seq_count, across))  8.39 us
  transfers between devices with their start and end apart: 57, of which 29 were waited for; matrix products, arithmetic and copies ran while one was open for 8% of the time, Pallas kernels for 19%

profile of v3, /device:TPU:0, one launch (start us, length us, event | category | flops | bytes accessed | tf_op | source)
XLA Modules:
  0.0 195.9 jit_solution(5461809977040708287)
XLA Ops:
  0.0 1.2 copy-done
  1.3 3.1 %collective-permute-start.2 = (bf16[256,1024]{1,0:T(8,128)(2,1)S(1)}, bf16[256,1024]{1,0:T(8,128)(2,1)}, u32[]{:S(2)}, u32[]{:S(2)}) collective-permute-start(bf16[256,1024]{1,0:T(8,128)(2,1)S(1)} %constant_dynamic-slice_fusion), channel_id=1, source_target_pairs={{0,2},{1,3},{2,6},{3,7},{6,4},{7,5},{4,0},{5,1},{8,10},{9,11},{10,... | collective-permute-start | bytes 1572872 | tf_op jit(solution)/shard_map/gather_0/ring/ppermute | solution.py:198
  4.3 1.5 collective-permute-start.1
  5.9 1.5 collective-permute-start.3
  9.6 7.8 %collective-permute-done.2 = bf16[256,1024]{1,0:T(8,128)(2,1)} collective-permute-done((bf16[256,1024]{1,0:T(8,128)(2,1)S(1)}, bf16[256,1024]{1,0:T(8,128)(2,1)}, u32[]{:S(2)}, u32[]{:S(2)}) %collective-permute-start.2) | collective-permute-done | bytes 524320 | tf_op jit(solution)/shard_map/gather_0/ring/ppermute | solution.py:198
  17.7 1.4 collective-permute-done.3.refs_3_
  19.2 1.5 collective-permute-start.8
  20.7 2.6 %collective-permute-start.7 = (bf16[256,1024]{1,0:T(8,128)(2,1)}, bf16[256,1024]{1,0:T(8,128)(2,1)}, u32[]{:S(2)}, u32[]{:S(2)}) collective-permute-start(bf16[256,1024]{1,0:T(8,128)(2,1)} %collective-permute-done.2), channel_id=1, source_target_pairs={{0,2},{1,3},{2,6},{3,7},{6,4},{7,5},{4,0},{5,1},{8,10},{9,11},{10,... | collective-permute-start | bytes 1572872 | tf_op jit(solution)/shard_map/gather_1/ring/ppermute | solution.py:198
  24.6 6.9 %collective-permute-done.8.refs_7_ = bf16[128,2048]{1,0:T(8,128)(2,1)S(1)} collective-permute-done((bf16[128,2048]{1,0:T(8,128)(2,1)}, bf16[128,2048]{1,0:T(8,128)(2,1)S(1)}, u32[]{:S(2)}, u32[]{:S(2)}) %collective-permute-start.8) | collective-permute-done | bytes 524320 | tf_op jit(solution)/shard_map/gather_1/ppermute | solution.py:229
  31.6 2.2 %collective-permute-done.7 = bf16[256,1024]{1,0:T(8,128)(2,1)} collective-permute-done((bf16[256,1024]{1,0:T(8,128)(2,1)}, bf16[256,1024]{1,0:T(8,128)(2,1)}, u32[]{:S(2)}, u32[]{:S(2)}) %collective-permute-start.7) | collective-permute-done | bytes 524320 | tf_op jit(solution)/shard_map/gather_1/ring/ppermute | solution.py:198
  33.8 1.4 collective-permute-done.6
  35.4 1.3 collective-permute-start.12
  36.7 1.5 collective-permute-start.11
  38.2 6.1 %shard_map.100 = bf16[128,2048]{1,0:T(8,128)(2,1)} custom-call(bf16[128,2048]{1,0:T(8,128)(2,1)} %bitcast.96, bf16[128,2048]{1,0:T(8,128)(2,1)} %bitcast.99, bf16[128,2048]{1,0:T(8,128)(2,1)} %copy-done.7, bf16[128,2048]{1,0:T(8,128)(2,1)} %copy-done.5, bf16[128,2048]{1,0:T(8,128)(2,1)} %collective-permute-done.4.refs_4_, bf16[128,2048]{1,0:T(8,128)(2,1)} %bitcast.102, ...), custom_call_target="tpu_custom_call" | custom-call | flops 1000 | bytes 1000 | tf_op jit(solution)/shard_map/pallas_call | solution.py:80
  44.5 1.0 collective-permute-start.33
  45.5 1.8 collective-permute-start.26
  47.3 4.4 %collective-permute-done.33 = s32[2,128]{0,1:T(8,128)S(1)} collective-permute-done((s32[2,128]{0,1:T(8,128)S(1)}, s32[2,128]{0,1:T(8,128)S(1)}, u32[]{:S(2)}, u32[]{:S(2)}) %collective-permute-start.33) | collective-permute-done | bytes 1056 | tf_op jit(solution)/shard_map/gather_0/ring/ppermute | solution.py:198
  51.7 4.0 %collective-permute-start.20 = (s32[2,128]{0,1:T(8,128)S(1)}, s32[2,128]{0,1:T(8,128)S(1)}, u32[]{:S(2)}, u32[]{:S(2)}) collective-permute-start(s32[2,128]{0,1:T(8,128)S(1)} %bitcast.95), channel_id=1, source_target_pairs={{0,2},{1,3},{2,6},{3,7},{6,4},{7,5},{4,0},{5,1},{8,10},{9,11},{10,... | collective-permute-start | bytes 3080 | tf_op jit(solution)/shard_map/gather_0/ring/ppermute | solution.py:198
  56.0 1.2 collective-permute-start.13
  57.4 1.4 fusion.26
  58.8 1.4 fusion.30
  60.2 1.2 fusion.32
  62.0 1.8 collective-permute-done.13
  64.0 1.3 fusion.28
  67.2 1.2 collective-permute-done.15
  70.7 1.5 collective-permute-start.17
  72.8 3.6 %collective-permute-done.18 = bf16[32,2048]{1,0:T(8,128)(2,1)S(1)} collective-permute-done((bf16[32,2048]{1,0:T(8,128)(2,1)S(1)}, bf16[32,2048]{1,0:T(8,128)(2,1)S(1)}, u32[]{:S(2)}, u32[]{:S(2)}) %collective-permute-start.18) | collective-permute-done | bytes 131104 | tf_op jit(solution)/shard_map/ppermute | solution.py:287
  76.4 2.9 %collective-permute-done.17 = bf16[32,2048]{1,0:T(8,128)(2,1)S(1)} collective-permute-done((bf16[32,2048]{1,0:T(8,128)(2,1)S(1)}, bf16[32,2048]{1,0:T(8,128)(2,1)S(1)}, u32[]{:S(2)}, u32[]{:S(2)}) %collective-permute-start.17) | collective-permute-done | bytes 131104 | tf_op jit(solution)/shard_map/ppermute | solution.py:287
  79.9 4.3 %collective-permute-done.21 = bf16[128,2048]{1,0:T(8,128)(2,1)S(1)} collective-permute-done((bf16[128,2048]{1,0:T(8,128)(2,1)S(1)}, bf16[128,2048]{1,0:T(8,128)(2,1)S(1)}, u32[]{:S(2)}, u32[]{:S(2)}) %collective-permute-start.21) | collective-permute-done | bytes 524320 | tf_op jit(solution)/shard_map/ring/ppermute | solution.py:198
  84.7 0.9 collective-permute-start.23
  85.7 0.9 collective-permute-start.22
  86.9 3.6 %collective-permute-done.24 = bf16[32,2048]{1,0:T(8,128)(2,1)S(1)} collective-permute-done((bf16[32,2048]{1,0:T(8,128)(2,1)S(1)}, bf16[32,2048]{1,0:T(8,128)(2,1)S(1)}, u32[]{:S(2)}, u32[]{:S(2)}) %collective-permute-start.24) | collective-permute-done | bytes 131104 | tf_op jit(solution)/shard_map/ppermute | solution.py:287
  90.5 1.9 collective-permute-done.23
  92.4 1.1 collective-permute-start.25
  93.6 4.7 %collective-permute-done.27 = bf16[128,2048]{1,0:T(8,128)(2,1)S(1)} collective-permute-done((bf16[128,2048]{1,0:T(8,128)(2,1)S(1)}, bf16[128,2048]{1,0:T(8,128)(2,1)S(1)}, u32[]{:S(2)}, u32[]{:S(2)}) %collective-permute-start.27) | collective-permute-done | bytes 524320 | tf_op jit(solution)/shard_map/ring/ppermute | solution.py:198
  99.4 1.2 collective-permute-start.34
  100.9 3.6 %collective-permute-done.36 = bf16[32,2048]{1,0:T(8,128)(2,1)S(1)} collective-permute-done((bf16[32,2048]{1,0:T(8,128)(2,1)S(1)}, bf16[32,2048]{1,0:T(8,128)(2,1)S(1)}, u32[]{:S(2)}, u32[]{:S(2)}) %collective-permute-start.36) | collective-permute-done | bytes 131104 | tf_op jit(solution)/shard_map/ppermute | solution.py:287
  104.5 1.0 collective-permute-done.35
  105.6 1.1 collective-permute-start.37
  106.9 7.5 %shard_map.101 = (bf16[128,2048]{1,0:T(8,128)(2,1)S(1)}, bf16[128,2048]{1,0:T(8,128)(2,1)S(1)}) custom-call(bf16[128,2048]{1,0:T(8,128)(2,1)S(1)} %pad_maximum_fusion.1.own_ref, bf16[128,2048]{1,0:T(8,128)(2,1)S(1)} %collective-permute-done.25.other_ref.refs_0_, bf16[2048,2048]{1,0:T(8,128)(2,1)} %bitcast.82, bf16[2048,2048]{1,0:T(8,128)(2,1)} %bitcast.86, ...), custom_call_target="tpu_custom_call" | custom-call | flops 4000000000 | bytes 1000 | tf_op jit(solution)/shard_map/pallas_call | solution.py:145
  114.4 1.1 collective-permute-start.38
  116.0 1.3 collective-permute-start.31
  117.3 1.0 collective-permute-start.30
  118.6 2.6 %collective-permute-done.31 = bf16[32,2048]{1,0:T(8,128)(2,1)S(1)} collective-permute-done((bf16[32,2048]{1,0:T(8,128)(2,1)S(1)}, bf16[32,2048]{1,0:T(8,128)(2,1)S(1)}, u32[]{:S(2)}, u32[]{:S(2)}) %collective-permute-start.31) | collective-permute-done | bytes 131104 | tf_op jit(solution)/shard_map/ppermute | solution.py:287
  121.2 3.4 %collective-permute-done.30 = bf16[32,2048]{1,0:T(8,128)(2,1)S(1)} collective-permute-done((bf16[32,2048]{1,0:T(8,128)(2,1)S(1)}, bf16[32,2048]{1,0:T(8,128)(2,1)S(1)}, u32[]{:S(2)}, u32[]{:S(2)}) %collective-permute-start.30) | collective-permute-done | bytes 131104 | tf_op jit(solution)/shard_map/ppermute | solution.py:287
  124.7 1.0 collective-permute-start.32
  125.8 7.5 %shard_map.102 = (bf16[128,2048]{1,0:T(8,128)(2,1)S(1)}, bf16[128,2048]{1,0:T(8,128)(2,1)S(1)}) custom-call(bf16[128,2048]{1,0:T(8,128)(2,1)S(1)} %pad_maximum_fusion.3.refs_1_.own_ref, bf16[128,2048]{1,0:T(8,128)(2,1)S(1)} %collective-permute-done.37.other_ref, bf16[2048,2048]{1,0:T(8,128)(2,1)} %bitcast.83, bf16[2048,2048]{1,0:T(8,128)(2,1)} %bitcast.87, ...), custom_call_target="tpu_custom_call" | custom-call | flops 4000000000 | bytes 1000 | tf_op jit(solution)/shard_map/pallas_call | solution.py:145
  133.5 1.4 collective-permute-start.41
  135.4 1.0 collective-permute-start.47
  136.5 6.5 %collective-permute-done.32.other_ref = bf16[128,2048]{1,0:T(8,128)(2,1)S(1)} collective-permute-done((bf16[128,2048]{1,0:T(8,128)(2,1)S(1)}, bf16[128,2048]{1,0:T(8,128)(2,1)S(1)}, u32[]{:S(2)}, u32[]{:S(2)}) %collective-permute-start.32) | collective-permute-done | bytes 524320 | tf_op jit(solution)/shard_map/half/ppermute | solution.py:202
  142.9 7.7 %shard_map.103 = (bf16[128,2048]{1,0:T(8,128)(2,1)S(1)}, bf16[128,2048]{1,0:T(8,128)(2,1)S(1)}) custom-call(bf16[128,2048]{1,0:T(8,128)(2,1)S(1)} %pad_maximum_fusion.2.refs_0_.own_ref, bf16[128,2048]{1,0:T(8,128)(2,1)S(1)} %collective-permute-done.32.other_ref, bf16[2048,2048]{1,0:T(8,128)(2,1)} %bitcast.84, bf16[2048,2048]{1,0:T(8,128)(2,1)} %bitcast.88, ...), custom_call_target="tpu_custom_call" | custom-call | flops 4000000000 | bytes 1000 | tf_op jit(solution)/shard_map/pallas_call | solution.py:145
  151.8 1.1 collective-permute-start.46
  152.9 1.2 collective-permute-done.47
  154.7 1.9 collective-permute-start.49
  156.6 7.5 %shard_map.104 = (bf16[128,2048]{1,0:T(8,128)(2,1)S(1)}, bf16[128,2048]{1,0:T(8,128)(2,1)S(1)}) custom-call(bf16[128,2048]{1,0:T(8,128)(2,1)S(1)} %pad_maximum_fusion.own_ref, bf16[128,2048]{1,0:T(8,128)(2,1)S(1)} %collective-permute-done.19.refs_0_.other_ref, bf16[2048,2048]{1,0:T(8,128)(2,1)} %bitcast.85, bf16[2048,2048]{1,0:T(8,128)(2,1)} %bitcast.89, ...), custom_call_target="tpu_custom_call" | custom-call | flops 4000000000 | bytes 1000 | tf_op jit(solution)/shard_map/pallas_call | solution.py:145
  164.1 1.1 collective-permute-start.42
  168.6 1.0 collective-permute-start.53
  169.7 8.8 %collective-permute-done.42 = bf16[128,2048]{1,0:T(8,128)(2,1)S(1)} collective-permute-done((bf16[128,2048]{1,0:T(8,128)(2,1)S(1)}, bf16[128,2048]{1,0:T(8,128)(2,1)S(1)}, u32[]{:S(2)}, u32[]{:S(2)}) %collective-permute-start.42) | collective-permute-done | bytes 524320 | tf_op jit(solution)/shard_map/half/ppermute | solution.py:202
  179.0 2.0 %collective-permute-done.55 = bf16[128,2048]{1,0:T(8,128)(2,1)S(1)} collective-permute-done((bf16[128,2048]{1,0:T(8,128)(2,1)S(1)}, bf16[128,2048]{1,0:T(8,128)(2,1)S(1)}, u32[]{:S(2)}, u32[]{:S(2)}) %collective-permute-start.55) | collective-permute-done | bytes 524320 | tf_op jit(solution)/shard_map/ring/ppermute | solution.py:198
  182.2 1.3 collective-permute-start.44
  184.0 3.9 %collective-permute-done.45 = bf16[32,2048]{1,0:T(8,128)(2,1)S(1)} collective-permute-done((bf16[32,2048]{1,0:T(8,128)(2,1)S(1)}, bf16[32,2048]{1,0:T(8,128)(2,1)S(1)}, u32[]{:S(2)}, u32[]{:S(2)}) %collective-permute-start.45) | collective-permute-done | bytes 131104 | tf_op jit(solution)/shard_map/ppermute | solution.py:287
  187.9 2.5 %collective-permute-done.44 = bf16[32,2048]{1,0:T(8,128)(2,1)S(1)} collective-permute-done((bf16[32,2048]{1,0:T(8,128)(2,1)S(1)}, bf16[32,2048]{1,0:T(8,128)(2,1)S(1)}, u32[]{:S(2)}, u32[]{:S(2)}) %collective-permute-start.44) | collective-permute-done | bytes 131104 | tf_op jit(solution)/shard_map/ppermute | solution.py:287
  190.8 3.9 %collective-permute-done.56 = bf16[128,2048]{1,0:T(8,128)(2,1)S(1)} collective-permute-done((bf16[128,2048]{1,0:T(8,128)(2,1)S(1)}, bf16[128,2048]{1,0:T(8,128)(2,1)S(1)}, u32[]{:S(2)}, u32[]{:S(2)}) %collective-permute-start.56) | collective-permute-done | bytes 524320 | tf_op jit(solution)/shard_map/home/ring/ppermute | solution.py:198
  194.7 1.2 fusion.8
  (164 shorter events, 22.4 us)
Async XLA Ops:
  1.3 16.1 %collective-permute-start.2 = (bf16[256,1024]{1,0:T(8,128)(2,1)S(1)}, bf16[256,1024]{1,0:T(8,128)(2,1)}, u32[]{:S(2)}, u32[]{:S(2)}) collective-permute-start(bf16[256,1024]{1,0:T(8,128)(2,1)S(1)} %constant_dynamic-slice_fusion), channel_id=1, source_target_pairs={{0,2},{1,3},{2,6},{3,7},{6,4},{7,5},{4,0},{5,1},{8,10},{9,11},{10,... | collective-permute-start | bytes 1572872 | tf_op jit(solution)/shard_map/gather_0/ring/ppermute | solution.py:198
  4.3 13.4 %collective-permute-start.1 = (bf16[256,1024]{1,0:T(8,128)(2,1)S(1)}, bf16[256,1024]{1,0:T(8,128)(2,1)S(1)}, u32[]{:S(2)}, u32[]{:S(2)}) collective-permute-start(bf16[256,1024]{1,0:T(8,128)(2,1)S(1)} %constant_dynamic-slice_fusion), channel_id=1, source_target_pairs={{0,1},{1,0},{2,3},{3,2},{4,5},{5,4},{6,7},{7,6},{8,9},{9,8},{10,11... | collective-permute-start | bytes 1572872 | tf_op jit(solution)/shard_map/gather_0/half/ppermute | solution.py:202
  5.9 13.3 %collective-permute-start.3 = (bf16[128,2048]{1,0:T(8,128)(2,1)}, bf16[128,2048]{1,0:T(8,128)(2,1)S(1)}, u32[]{:S(2)}, u32[]{:S(2)}) collective-permute-start(bf16[128,2048]{1,0:T(8,128)(2,1)} %bitcast.97), channel_id=1, source_target_pairs={{0,16},{8,24},{16,0},{24,8},{1,17},{9,25},{17,1},{25,9},{2,18},{10... | collective-permute-start | bytes 1572872 | tf_op jit(solution)/shard_map/gather_0/ppermute | solution.py:229
  19.2 19.0 %copy-start.5 = (bf16[128,2048]{1,0:T(8,128)(2,1)}, bf16[128,2048]{1,0:T(8,128)(2,1)S(1)}, u32[]{:S(2)}) copy-start(bf16[128,2048]{1,0:T(8,128)(2,1)S(1)} %collective-permute-done.3.refs_3_) | copy-start | bytes 1572868
  19.2 12.4 %collective-permute-start.8 = (bf16[128,2048]{1,0:T(8,128)(2,1)}, bf16[128,2048]{1,0:T(8,128)(2,1)S(1)}, u32[]{:S(2)}, u32[]{:S(2)}) collective-permute-start(bf16[128,2048]{1,0:T(8,128)(2,1)} %bitcast.100), channel_id=1, source_target_pairs={{0,16},{8,24},{16,0},{24,8},{1,17},{9,25},{17,1},{25,9},{2,18},{10... | collective-permute-start | bytes 1572872 | tf_op jit(solution)/shard_map/gather_1/ppermute | solution.py:229
  20.7 13.1 %collective-permute-start.7 = (bf16[256,1024]{1,0:T(8,128)(2,1)}, bf16[256,1024]{1,0:T(8,128)(2,1)}, u32[]{:S(2)}, u32[]{:S(2)}) collective-permute-start(bf16[256,1024]{1,0:T(8,128)(2,1)} %collective-permute-done.2), channel_id=1, source_target_pairs={{0,2},{1,3},{2,6},{3,7},{6,4},{7,5},{4,0},{5,1},{8,10},{9,11},{10,... | collective-permute-start | bytes 1572872 | tf_op jit(solution)/shard_map/gather_1/ring/ppermute | solution.py:198
  23.3 11.9 %collective-permute-start.6 = (bf16[256,1024]{1,0:T(8,128)(2,1)}, bf16[256,1024]{1,0:T(8,128)(2,1)}, u32[]{:S(2)}, u32[]{:S(2)}) collective-permute-start(bf16[256,1024]{1,0:T(8,128)(2,1)} %collective-permute-done.2), channel_id=1, source_target_pairs={{0,1},{1,0},{2,3},{3,2},{4,5},{5,4},{6,7},{7,6},{8,9},{9,8},{10,11... | collective-permute-start | bytes 1572872 | tf_op jit(solution)/shard_map/gather_1/half/ppermute | solution.py:202
  24.1 12.6 %collective-permute-start = (bf16[128,2048]{1,0:T(8,128)(2,1)}, bf16[128,2048]{1,0:T(8,128)(2,1)S(1)}, u32[]{:S(2)}, u32[]{:S(2)}) collective-permute-start(bf16[128,2048]{1,0:T(8,128)(2,1)} %bitcast.98), channel_id=1, source_target_pairs={{0,8},{8,0},{16,24},{24,16},{1,9},{9,1},{17,25},{25,17},{2,10},{10... | collective-permute-start | bytes 1572872 | tf_op jit(solution)/shard_map/core/ppermute | solution.py:206
  24.1 14.1 %collective-permute-start.5 = (bf16[128,2048]{1,0:T(8,128)(2,1)}, bf16[128,2048]{1,0:T(8,128)(2,1)}, u32[]{:S(2)}, u32[]{:S(2)}) collective-permute-start(bf16[128,2048]{1,0:T(8,128)(2,1)} %bitcast.101), channel_id=1, source_target_pairs={{0,8},{8,0},{16,24},{24,16},{1,9},{9,1},{17,25},{25,17},{2,10},{10... | collective-permute-start | bytes 1572872 | tf_op jit(solution)/shard_map/core/ppermute | solution.py:206
  31.6 6.6 %copy-start.6 = (bf16[128,2048]{1,0:T(8,128)(2,1)}, bf16[128,2048]{1,0:T(8,128)(2,1)S(1)}, u32[]{:S(2)}) copy-start(bf16[128,2048]{1,0:T(8,128)(2,1)S(1)} %collective-permute-done.8.refs_7_) | copy-start | bytes 1572868
  31.6 6.6 %collective-permute-start.4 = (bf16[128,2048]{1,0:T(8,128)(2,1)S(1)}, bf16[128,2048]{1,0:T(8,128)(2,1)}, u32[]{:S(2)}, u32[]{:S(2)}) collective-permute-start(bf16[128,2048]{1,0:T(8,128)(2,1)S(1)} %collective-permute-done.3.refs_3_), channel_id=1, source_target_pairs={{0,8},{8,0},{16,24},{24,16},{1,9},{9,1},{17,25},{25,17},{2,10},{10... | collective-permute-start | bytes 1572872 | tf_op jit(solution)/shard_map/core/ppermute | solution.py:206
  35.2 3.0 %collective-permute-start.9 = (bf16[128,2048]{1,0:T(8,128)(2,1)S(1)}, bf16[128,2048]{1,0:T(8,128)(2,1)}, u32[]{:S(2)}, u32[]{:S(2)}) collective-permute-start(bf16[128,2048]{1,0:T(8,128)(2,1)S(1)} %collective-permute-done.8.refs_7_), channel_id=1, source_target_pairs={{0,8},{8,0},{16,24},{24,16},{1,9},{9,1},{17,25},{25,17},{2,10},{10... | collective-permute-start | bytes 1572872 | tf_op jit(solution)/shard_map/core/ppermute | solution.py:206
  35.4 20.6 %collective-permute-start.12 = (bf16[256,1024]{1,0:T(8,128)(2,1)}, bf16[256,1024]{1,0:T(8,128)(2,1)S(1)}, u32[]{:S(2)}, u32[]{:S(2)}) collective-permute-start(bf16[256,1024]{1,0:T(8,128)(2,1)} %collective-permute-done.7), channel_id=1, source_target_pairs={{0,2},{1,3},{2,6},{3,7},{6,4},{7,5},{4,0},{5,1},{8,10},{9,11},{10,... | collective-permute-start | bytes 1572872 | tf_op jit(solution)/shard_map/gather_2/ring/ppermute | solution.py:198
  36.7 19.3 %collective-permute-start.11 = (bf16[256,1024]{1,0:T(8,128)(2,1)}, bf16[256,1024]{1,0:T(8,128)(2,1)S(1)}, u32[]{:S(2)}, u32[]{:S(2)}) collective-permute-start(bf16[256,1024]{1,0:T(8,128)(2,1)} %collective-permute-done.7), channel_id=1, source_target_pairs={{0,1},{1,0},{2,3},{3,2},{4,5},{5,4},{6,7},{7,6},{8,9},{9,8},{10,11... | collective-permute-start | bytes 1572872 | tf_op jit(solution)/shard_map/gather_2/half/ppermute | solution.py:202
  44.4 17.0 %copy-start.2 = (bf16[128,2048]{1,0:T(8,128)(2,1)S(1)}, bf16[128,2048]{1,0:T(8,128)(2,1)}, u32[]{:S(2)}) copy-start(bf16[128,2048]{1,0:T(8,128)(2,1)} %shard_map.100) | copy-start | bytes 1572868
  44.4 17.3 %copy-start.9 = (bf16[256,1024]{1,0:T(8,128)(2,1)S(1)}, bf16[256,1024]{1,0:T(8,128)(2,1)}, u32[]{:S(2)}) copy-start(bf16[256,1024]{1,0:T(8,128)(2,1)} %copy-done.8) | copy-start | bytes 1572868
  44.4 13.0 %collective-permute-start.10 = (bf16[128,2048]{1,0:T(8,128)(2,1)}, bf16[128,2048]{1,0:T(8,128)(2,1)S(1)}, u32[]{:S(2)}, u32[]{:S(2)}) collective-permute-start(bf16[128,2048]{1,0:T(8,128)(2,1)} %shard_map.100), channel_id=1, source_target_pairs={{0,8},{8,0},{16,24},{24,16},{1,9},{9,1},{17,25},{25,17},{2,10},{10... | collective-permute-start | bytes 1572872 | tf_op jit(solution)/shard_map/core/ppermute | solution.py:206
  44.5 7.2 %collective-permute-start.33 = (s32[2,128]{0,1:T(8,128)S(1)}, s32[2,128]{0,1:T(8,128)S(1)}, u32[]{:S(2)}, u32[]{:S(2)}) collective-permute-start(s32[2,128]{0,1:T(8,128)S(1)} %bitcast.93), channel_id=1, source_target_pairs={{0,6},{1,7},{2,4},{3,5},{6,0},{7,1},{4,2},{5,3},{8,14},{9,15},{10,... | collective-permute-start | bytes 3080 | tf_op jit(solution)/shard_map/gather_0/ring/ppermute | solution.py:198
  45.5 10.3 %collective-permute-start.26 = (s32[2,128]{0,1:T(8,128)S(1)}, s32[2,128]{0,1:T(8,128)S(1)}, u32[]{:S(2)}, u32[]{:S(2)}) collective-permute-start(s32[2,128]{0,1:T(8,128)S(1)} %bitcast.94), channel_id=1, source_target_pairs={{0,4},{1,5},{2,0},{3,1},{6,2},{7,3},{4,6},{5,7},{8,12},{9,13},{10,... | collective-permute-start | bytes 3080 | tf_op jit(solution)/shard_map/gather_0/ring/ppermute | solution.py:198
  51.7 14.8 %collective-permute-start.20 = (s32[2,128]{0,1:T(8,128)S(1)}, s32[2,128]{0,1:T(8,128)S(1)}, u32[]{:S(2)}, u32[]{:S(2)}) collective-permute-start(s32[2,128]{0,1:T(8,128)S(1)} %bitcast.95), channel_id=1, source_target_pairs={{0,2},{1,3},{2,6},{3,7},{6,4},{7,5},{4,0},{5,1},{8,10},{9,11},{10,... | collective-permute-start | bytes 3080 | tf_op jit(solution)/shard_map/gather_0/ring/ppermute | solution.py:198
  56.0 7.7 %collective-permute-start.13 = (bf16[128,1024]{1,0:T(8,128)(2,1)S(1)}, bf16[128,1024]{1,0:T(8,128)(2,1)S(1)}, u32[]{:S(2)}, u32[]{:S(2)}) collective-permute-start(bf16[128,1024]{1,0:T(8,128)(2,1)S(1)} %slice.180), channel_id=1, source_target_pairs={{0,1},{1,0},{2,3},{3,2},{4,5},{5,4},{6,7},{7,6},{8,9},{9,8},{10,11... | collective-permute-start | bytes 786440 | tf_op jit(solution)/shard_map/half/ppermute | solution.py:202
  57.2 8.3 %collective-permute-start.14 = (bf16[128,1024]{1,0:T(8,128)(2,1)S(1)}, bf16[128,1024]{1,0:T(8,128)(2,1)S(1)}, u32[]{:S(2)}, u32[]{:S(2)}) collective-permute-start(bf16[128,1024]{1,0:T(8,128)(2,1)S(1)} %slice.181), channel_id=1, source_target_pairs={{0,2},{1,3},{2,6},{3,7},{6,4},{7,5},{4,0},{5,1},{8,10},{9,11},{10,... | collective-permute-start | bytes 786440 | tf_op jit(solution)/shard_map/ring/ppermute | solution.py:198
  65.8 3.2 %copy-start.10 = (f32[2048]{0:T(1024)S(1)}, f32[2048]{0:T(1024)}, u32[]{:S(2)}) copy-start(f32[2048]{0:T(1024)} %param.15) | copy-start | bytes 24580
  65.8 6.7 %copy-start.4 = (bf16[2048,16]{0,1:T(8,128)(2,1)S(1)}, bf16[2048,16]{0,1:T(8,128)(2,1)}, u32[]{:S(2)}) copy-start(bf16[2048,16]{0,1:T(8,128)(2,1)} %param.16) | copy-start | bytes 196612
  66.5 2.0 %collective-permute-start.15 = (f32[128,1024]{1,0:T(8,128)S(1)}, f32[128,1024]{1,0:T(8,128)S(1)}, u32[]{:S(2)}, u32[]{:S(2)}) collective-permute-start(f32[128,1024]{1,0:T(8,128)S(1)} %slice.234), channel_id=1, source_target_pairs={{0,8},{8,0},{16,24},{24,16},{1,9},{9,1},{17,25},{25,17},{2,10},{10... | collective-permute-start | bytes 1572872 | tf_op jit(solution)/shard_map/core/ppermute | solution.py:206
  69.3 14.9 %collective-permute-start.21 = (bf16[128,2048]{1,0:T(8,128)(2,1)S(1)}, bf16[128,2048]{1,0:T(8,128)(2,1)S(1)}, u32[]{:S(2)}, u32[]{:S(2)}) collective-permute-start(bf16[128,2048]{1,0:T(8,128)(2,1)S(1)} %multiply_convert_fusion), channel_id=1, source_target_pairs={{0,2},{1,3},{2,6},{3,7},{6,4},{7,5},{4,0},{5,1},{8,10},{9,11},{10,... | collective-permute-start | bytes 1572872 | tf_op jit(solution)/shard_map/ring/ppermute | solution.py:198
  70.6 5.8 %collective-permute-start.18 = (bf16[32,2048]{1,0:T(8,128)(2,1)S(1)}, bf16[32,2048]{1,0:T(8,128)(2,1)S(1)}, u32[]{:S(2)}, u32[]{:S(2)}) collective-permute-start(bf16[32,2048]{1,0:T(8,128)(2,1)S(1)} %get-tuple-element.102), channel_id=1, source_target_pairs={{0,24},{8,16},{16,8},{24,0},{1,25},{9,17},{17,9},{25,1},{2,26},{10... | collective-permute-start | bytes 393224 | tf_op jit(solution)/shard_map/ppermute | solution.py:287
  70.7 8.6 %collective-permute-start.17 = (bf16[32,2048]{1,0:T(8,128)(2,1)S(1)}, bf16[32,2048]{1,0:T(8,128)(2,1)S(1)}, u32[]{:S(2)}, u32[]{:S(2)}) collective-permute-start(bf16[32,2048]{1,0:T(8,128)(2,1)S(1)} %get-tuple-element.103), channel_id=1, source_target_pairs={{0,16},{8,24},{16,0},{24,8},{1,17},{9,25},{17,1},{25,9},{2,18},{10... | collective-permute-start | bytes 393224 | tf_op jit(solution)/shard_map/ppermute | solution.py:287
  72.1 7.1 %collective-permute-start.16 = (bf16[32,2048]{1,0:T(8,128)(2,1)S(1)}, bf16[32,2048]{1,0:T(8,128)(2,1)S(1)}, u32[]{:S(2)}, u32[]{:S(2)}) collective-permute-start(bf16[32,2048]{1,0:T(8,128)(2,1)S(1)} %get-tuple-element.104), channel_id=1, source_target_pairs={{0,8},{8,0},{16,24},{24,16},{1,9},{9,1},{17,25},{25,17},{2,10},{10... | collective-permute-start | bytes 393224 | tf_op jit(solution)/shard_map/ppermute | solution.py:287
  79.3 14.3 %collective-permute-start.19 = (bf16[128,2048]{1,0:T(8,128)(2,1)S(1)}, bf16[128,2048]{1,0:T(8,128)(2,1)S(1)}, u32[]{:S(2)}, u32[]{:S(2)}) collective-permute-start(bf16[128,2048]{1,0:T(8,128)(2,1)S(1)} %pad_maximum_fusion.own_ref), channel_id=1, source_target_pairs={{0,1},{1,0},{2,3},{3,2},{4,5},{5,4},{6,7},{7,6},{8,9},{9,8},{10,11... | collective-permute-start | bytes 1572872 | tf_op jit(solution)/shard_map/half/ppermute | solution.py:202
  84.2 14.0 %collective-permute-start.27 = (bf16[128,2048]{1,0:T(8,128)(2,1)S(1)}, bf16[128,2048]{1,0:T(8,128)(2,1)S(1)}, u32[]{:S(2)}, u32[]{:S(2)}) collective-permute-start(bf16[128,2048]{1,0:T(8,128)(2,1)S(1)} %collective-permute-done.21), channel_id=1, source_target_pairs={{0,2},{1,3},{2,6},{3,7},{6,4},{7,5},{4,0},{5,1},{8,10},{9,11},{10,... | collective-permute-start | bytes 1572872 | tf_op jit(solution)/shard_map/ring/ppermute | solution.py:198
  84.7 5.8 %collective-permute-start.24 = (bf16[32,2048]{1,0:T(8,128)(2,1)S(1)}, bf16[32,2048]{1,0:T(8,128)(2,1)S(1)}, u32[]{:S(2)}, u32[]{:S(2)}) collective-permute-start(bf16[32,2048]{1,0:T(8,128)(2,1)S(1)} %get-tuple-element.98), channel_id=1, source_target_pairs={{0,24},{8,16},{16,8},{24,0},{1,25},{9,17},{17,9},{25,1},{2,26},{10... | collective-permute-start | bytes 393224 | tf_op jit(solution)/shard_map/ppermute | solution.py:287
  84.7 7.6 %collective-permute-start.23 = (bf16[32,2048]{1,0:T(8,128)(2,1)S(1)}, bf16[32,2048]{1,0:T(8,128)(2,1)S(1)}, u32[]{:S(2)}, u32[]{:S(2)}) collective-permute-start(bf16[32,2048]{1,0:T(8,128)(2,1)S(1)} %get-tuple-element.99), channel_id=1, source_target_pairs={{0,16},{8,24},{16,0},{24,8},{1,17},{9,25},{17,1},{25,9},{2,18},{10... | collective-permute-start | bytes 393224 | tf_op jit(solution)/shard_map/ppermute | solution.py:287
  85.7 6.7 %collective-permute-start.22 = (bf16[32,2048]{1,0:T(8,128)(2,1)S(1)}, bf16[32,2048]{1,0:T(8,128)(2,1)S(1)}, u32[]{:S(2)}, u32[]{:S(2)}) collective-permute-start(bf16[32,2048]{1,0:T(8,128)(2,1)S(1)} %get-tuple-element.100), channel_id=1, source_target_pairs={{0,8},{8,0},{16,24},{24,16},{1,9},{9,1},{17,25},{25,17},{2,10},{10... | collective-permute-start | bytes 393224 | tf_op jit(solution)/shard_map/ppermute | solution.py:287
  92.4 14.5 %collective-permute-start.25 = (bf16[128,2048]{1,0:T(8,128)(2,1)S(1)}, bf16[128,2048]{1,0:T(8,128)(2,1)S(1)}, u32[]{:S(2)}, u32[]{:S(2)}) collective-permute-start(bf16[128,2048]{1,0:T(8,128)(2,1)S(1)} %pad_maximum_fusion.1.own_ref), channel_id=1, source_target_pairs={{0,1},{1,0},{2,3},{3,2},{4,5},{5,4},{6,7},{7,6},{8,9},{9,8},{10,11... | collective-permute-start | bytes 1572872 | tf_op jit(solution)/shard_map/half/ppermute | solution.py:202
  98.7 5.8 %collective-permute-start.36 = (bf16[32,2048]{1,0:T(8,128)(2,1)S(1)}, bf16[32,2048]{1,0:T(8,128)(2,1)S(1)}, u32[]{:S(2)}, u32[]{:S(2)}) collective-permute-start(bf16[32,2048]{1,0:T(8,128)(2,1)S(1)} %get-tuple-element.90), channel_id=1, source_target_pairs={{0,24},{8,16},{16,8},{24,0},{1,25},{9,17},{17,9},{25,1},{2,26},{10... | collective-permute-start | bytes 393224 | tf_op jit(solution)/shard_map/ppermute | solution.py:287
  98.8 6.8 %collective-permute-start.35 = (bf16[32,2048]{1,0:T(8,128)(2,1)S(1)}, bf16[32,2048]{1,0:T(8,128)(2,1)S(1)}, u32[]{:S(2)}, u32[]{:S(2)}) collective-permute-start(bf16[32,2048]{1,0:T(8,128)(2,1)S(1)} %get-tuple-element.91), channel_id=1, source_target_pairs={{0,16},{8,24},{16,0},{24,8},{1,17},{9,25},{17,1},{25,9},{2,18},{10... | collective-permute-start | bytes 393224 | tf_op jit(solution)/shard_map/ppermute | solution.py:287
  99.4 6.2 %collective-permute-start.34 = (bf16[32,2048]{1,0:T(8,128)(2,1)S(1)}, bf16[32,2048]{1,0:T(8,128)(2,1)S(1)}, u32[]{:S(2)}, u32[]{:S(2)}) collective-permute-start(bf16[32,2048]{1,0:T(8,128)(2,1)S(1)} %get-tuple-element.92), channel_id=1, source_target_pairs={{0,8},{8,0},{16,24},{24,16},{1,9},{9,1},{17,25},{25,17},{2,10},{10... | collective-permute-start | bytes 393224 | tf_op jit(solution)/shard_map/ppermute | solution.py:287
  100.6 14.9 %collective-permute-start.28 = (bf16[128,2048]{1,0:T(8,128)(2,1)S(1)}, bf16[128,2048]{1,0:T(8,128)(2,1)S(1)}, u32[]{:S(2)}, u32[]{:S(2)}) collective-permute-start(bf16[128,2048]{1,0:T(8,128)(2,1)S(1)} %collective-permute-done.27), channel_id=1, source_target_pairs={{0,2},{1,3},{2,6},{3,7},{6,4},{7,5},{4,0},{5,1},{8,10},{9,11},{10,... | collective-permute-start | bytes 1572872 | tf_op jit(solution)/shard_map/ring/ppermute | solution.py:198
  105.6 20.1 %collective-permute-start.37 = (bf16[128,2048]{1,0:T(8,128)(2,1)S(1)}, bf16[128,2048]{1,0:T(8,128)(2,1)S(1)}, u32[]{:S(2)}, u32[]{:S(2)}) collective-permute-start(bf16[128,2048]{1,0:T(8,128)(2,1)S(1)} %pad_maximum_fusion.3.refs_1_.own_ref), channel_id=1, source_target_pairs={{0,1},{1,0},{2,3},{3,2},{4,5},{5,4},{6,7},{7,6},{8,9},{9,8},{10,11... | collective-permute-start | bytes 1572872 | tf_op jit(solution)/shard_map/half/ppermute | solution.py:202
  114.4 18.9 %collective-permute-start.38 = (bf16[128,2048]{1,0:T(8,128)(2,1)S(1)}, bf16[128,2048]{1,0:T(8,128)(2,1)S(1)}, u32[]{:S(2)}, u32[]{:S(2)}) collective-permute-start(bf16[128,2048]{1,0:T(8,128)(2,1)S(1)} %get-tuple-element.48), channel_id=1, source_target_pairs={{0,1},{1,0},{2,3},{3,2},{4,5},{5,4},{6,7},{7,6},{8,9},{9,8},{10,11... | collective-permute-start | bytes 1572872 | tf_op jit(solution)/shard_map/half/ppermute | solution.py:202
  116.0 5.2 %collective-permute-start.31 = (bf16[32,2048]{1,0:T(8,128)(2,1)S(1)}, bf16[32,2048]{1,0:T(8,128)(2,1)S(1)}, u32[]{:S(2)}, u32[]{:S(2)}) collective-permute-start(bf16[32,2048]{1,0:T(8,128)(2,1)S(1)} %get-tuple-element.94), channel_id=1, source_target_pairs={{0,24},{8,16},{16,8},{24,0},{1,25},{9,17},{17,9},{25,1},{2,26},{10... | collective-permute-start | bytes 393224 | tf_op jit(solution)/shard_map/ppermute | solution.py:287
  117.3 7.4 %collective-permute-start.30 = (bf16[32,2048]{1,0:T(8,128)(2,1)S(1)}, bf16[32,2048]{1,0:T(8,128)(2,1)S(1)}, u32[]{:S(2)}, u32[]{:S(2)}) collective-permute-start(bf16[32,2048]{1,0:T(8,128)(2,1)S(1)} %get-tuple-element.95), channel_id=1, source_target_pairs={{0,16},{8,24},{16,0},{24,8},{1,17},{9,25},{17,1},{25,9},{2,18},{10... | collective-permute-start | bytes 393224 | tf_op jit(solution)/shard_map/ppermute | solution.py:287
  118.3 6.4 %collective-permute-start.29 = (bf16[32,2048]{1,0:T(8,128)(2,1)S(1)}, bf16[32,2048]{1,0:T(8,128)(2,1)S(1)}, u32[]{:S(2)}, u32[]{:S(2)}) collective-permute-start(bf16[32,2048]{1,0:T(8,128)(2,1)S(1)} %get-tuple-element.96), channel_id=1, source_target_pairs={{0,8},{8,0},{16,24},{24,16},{1,9},{9,1},{17,25},{25,17},{2,10},{10... | collective-permute-start | bytes 393224 | tf_op jit(solution)/shard_map/ppermute | solution.py:287
  124.7 18.2 %collective-permute-start.32 = (bf16[128,2048]{1,0:T(8,128)(2,1)S(1)}, bf16[128,2048]{1,0:T(8,128)(2,1)S(1)}, u32[]{:S(2)}, u32[]{:S(2)}) collective-permute-start(bf16[128,2048]{1,0:T(8,128)(2,1)S(1)} %pad_maximum_fusion.2.refs_0_.own_ref), channel_id=1, source_target_pairs={{0,1},{1,0},{2,3},{3,2},{4,5},{5,4},{6,7},{7,6},{8,9},{9,8},{10,11... | collective-permute-start | bytes 1572872 | tf_op jit(solution)/shard_map/half/ppermute | solution.py:202
  133.5 17.2 %collective-permute-start.41 = (bf16[32,2048]{1,0:T(8,128)(2,1)S(1)}, bf16[32,2048]{1,0:T(8,128)(2,1)S(1)}, u32[]{:S(2)}, u32[]{:S(2)}) collective-permute-start(bf16[32,2048]{1,0:T(8,128)(2,1)S(1)} %get-tuple-element.85), channel_id=1, source_target_pairs={{0,24},{8,16},{16,8},{24,0},{1,25},{9,17},{17,9},{25,1},{2,26},{10... | collective-permute-start | bytes 393224 | tf_op jit(solution)/shard_map/ppermute | solution.py:287
  134.9 15.8 %collective-permute-start.40 = (bf16[32,2048]{1,0:T(8,128)(2,1)S(1)}, bf16[32,2048]{1,0:T(8,128)(2,1)S(1)}, u32[]{:S(2)}, u32[]{:S(2)}) collective-permute-start(bf16[32,2048]{1,0:T(8,128)(2,1)S(1)} %get-tuple-element.86), channel_id=1, source_target_pairs={{0,16},{8,24},{16,0},{24,8},{1,17},{9,25},{17,1},{25,9},{2,18},{10... | collective-permute-start | bytes 393224 | tf_op jit(solution)/shard_map/ppermute | solution.py:287
  135.2 15.5 %collective-permute-start.39 = (bf16[32,2048]{1,0:T(8,128)(2,1)S(1)}, bf16[32,2048]{1,0:T(8,128)(2,1)S(1)}, u32[]{:S(2)}, u32[]{:S(2)}) collective-permute-start(bf16[32,2048]{1,0:T(8,128)(2,1)S(1)} %get-tuple-element.87), channel_id=1, source_target_pairs={{0,8},{8,0},{16,24},{24,16},{1,9},{9,1},{17,25},{25,17},{2,10},{10... | collective-permute-start | bytes 393224 | tf_op jit(solution)/shard_map/ppermute | solution.py:287
  135.4 18.7 %collective-permute-start.47 = (bf16[128,2048]{1,0:T(8,128)(2,1)S(1)}, bf16[128,2048]{1,0:T(8,128)(2,1)S(1)}, u32[]{:S(2)}, u32[]{:S(2)}) collective-permute-start(bf16[128,2048]{1,0:T(8,128)(2,1)S(1)} %get-tuple-element.59), channel_id=1, source_target_pairs={{0,1},{1,0},{2,3},{3,2},{4,5},{5,4},{6,7},{7,6},{8,9},{9,8},{10,11... | collective-permute-start | bytes 1572872 | tf_op jit(solution)/shard_map/half/ppermute | solution.py:202
  151.5 15.0 %collective-permute-start.51 = (bf16[128,2048]{1,0:T(8,128)(2,1)S(1)}, bf16[128,2048]{1,0:T(8,128)(2,1)S(1)}, u32[]{:S(2)}, u32[]{:S(2)}) collective-permute-start(bf16[128,2048]{1,0:T(8,128)(2,1)S(1)} %fusion.5.refs_2_), channel_id=1, source_target_pairs={{0,2},{1,3},{2,6},{3,7},{6,4},{7,5},{4,0},{5,1},{8,10},{9,11},{10,... | collective-permute-start | bytes 1572872 | tf_op jit(solution)/shard_map/ring/ppermute | solution.py:198
  151.8 15.7 %collective-permute-start.46 = (bf16[128,2048]{1,0:T(8,128)(2,1)S(1)}, bf16[128,2048]{1,0:T(8,128)(2,1)S(1)}, u32[]{:S(2)}, u32[]{:S(2)}) collective-permute-start(bf16[128,2048]{1,0:T(8,128)(2,1)S(1)} %get-tuple-element.57), channel_id=1, source_target_pairs={{0,1},{1,0},{2,3},{3,2},{4,5},{5,4},{6,7},{7,6},{8,9},{9,8},{10,11... | collective-permute-start | bytes 1572872 | tf_op jit(solution)/shard_map/half/ppermute | solution.py:202
  154.3 9.8 %collective-permute-start.50 = (bf16[32,2048]{1,0:T(8,128)(2,1)S(1)}, bf16[32,2048]{1,0:T(8,128)(2,1)S(1)}, u32[]{:S(2)}, u32[]{:S(2)}) collective-permute-start(bf16[32,2048]{1,0:T(8,128)(2,1)S(1)} %get-tuple-element.78), channel_id=1, source_target_pairs={{0,24},{8,16},{16,8},{24,0},{1,25},{9,17},{17,9},{25,1},{2,26},{10... | collective-permute-start | bytes 393224 | tf_op jit(solution)/shard_map/ppermute | solution.py:287
  154.7 10.5 %collective-permute-start.49 = (bf16[32,2048]{1,0:T(8,128)(2,1)S(1)}, bf16[32,2048]{1,0:T(8,128)(2,1)S(1)}, u32[]{:S(2)}, u32[]{:S(2)}) collective-permute-start(bf16[32,2048]{1,0:T(8,128)(2,1)S(1)} %get-tuple-element.79), channel_id=1, source_target_pairs={{0,16},{8,24},{16,0},{24,8},{1,17},{9,25},{17,1},{25,9},{2,18},{10... | collective-permute-start | bytes 393224 | tf_op jit(solution)/shard_map/ppermute | solution.py:287
  156.6 8.7 %collective-permute-start.48 = (bf16[32,2048]{1,0:T(8,128)(2,1)S(1)}, bf16[32,2048]{1,0:T(8,128)(2,1)S(1)}, u32[]{:S(2)}, u32[]{:S(2)}) collective-permute-start(bf16[32,2048]{1,0:T(8,128)(2,1)S(1)} %get-tuple-element.80), channel_id=1, source_target_pairs={{0,8},{8,0},{16,24},{24,16},{1,9},{9,1},{17,25},{25,17},{2,10},{10... | collective-permute-start | bytes 393224 | tf_op jit(solution)/shard_map/ppermute | solution.py:287
  164.1 14.4 %collective-permute-start.42 = (bf16[128,2048]{1,0:T(8,128)(2,1)S(1)}, bf16[128,2048]{1,0:T(8,128)(2,1)S(1)}, u32[]{:S(2)}, u32[]{:S(2)}) collective-permute-start(bf16[128,2048]{1,0:T(8,128)(2,1)S(1)} %get-tuple-element.55), channel_id=1, source_target_pairs={{0,1},{1,0},{2,3},{3,2},{4,5},{5,4},{6,7},{7,6},{8,9},{9,8},{10,11... | collective-permute-start | bytes 1572872 | tf_op jit(solution)/shard_map/half/ppermute | solution.py:202
  166.5 29.4 %copy-start.1 = (bf16[256,2048]{1,0:T(8,128)(2,1)S(1)}, bf16[256,2048]{1,0:T(8,128)(2,1)}, u32[]{:S(2)}) copy-start(bf16[256,2048]{1,0:T(8,128)(2,1)} %param.14) | copy-start | bytes 3145732
  166.9 14.2 %collective-permute-start.55 = (bf16[128,2048]{1,0:T(8,128)(2,1)S(1)}, bf16[128,2048]{1,0:T(8,128)(2,1)S(1)}, u32[]{:S(2)}, u32[]{:S(2)}) collective-permute-start(bf16[128,2048]{1,0:T(8,128)(2,1)S(1)} %fusion.6), channel_id=1, source_target_pairs={{0,2},{1,3},{2,6},{3,7},{6,4},{7,5},{4,0},{5,1},{8,10},{9,11},{10,... | collective-permute-start | bytes 1572872 | tf_op jit(solution)/shard_map/ring/ppermute | solution.py:198
  167.8 10.9 %collective-permute-start.54 = (bf16[32,2048]{1,0:T(8,128)(2,1)S(1)}, bf16[32,2048]{1,0:T(8,128)(2,1)S(1)}, u32[]{:S(2)}, u32[]{:S(2)}) collective-permute-start(bf16[32,2048]{1,0:T(8,128)(2,1)S(1)} %get-tuple-element.74), channel_id=1, source_target_pairs={{0,24},{8,16},{16,8},{24,0},{1,25},{9,17},{17,9},{25,1},{2,26},{10... | collective-permute-start | bytes 393224 | tf_op jit(solution)/shard_map/ppermute | solution.py:287
  168.6 10.0 %collective-permute-start.53 = (bf16[32,2048]{1,0:T(8,128)(2,1)S(1)}, bf16[32,2048]{1,0:T(8,128)(2,1)S(1)}, u32[]{:S(2)}, u32[]{:S(2)}) collective-permute-start(bf16[32,2048]{1,0:T(8,128)(2,1)S(1)} %get-tuple-element.75), channel_id=1, source_target_pairs={{0,16},{8,24},{16,0},{24,8},{1,17},{9,25},{17,1},{25,9},{2,18},{10... | collective-permute-start | bytes 393224 | tf_op jit(solution)/shard_map/ppermute | solution.py:287
  169.7 9.0 %collective-permute-start.52 = (bf16[32,2048]{1,0:T(8,128)(2,1)S(1)}, bf16[32,2048]{1,0:T(8,128)(2,1)S(1)}, u32[]{:S(2)}, u32[]{:S(2)}) collective-permute-start(bf16[32,2048]{1,0:T(8,128)(2,1)S(1)} %get-tuple-element.76), channel_id=1, source_target_pairs={{0,8},{8,0},{16,24},{24,16},{1,9},{9,1},{17,25},{25,17},{2,10},{10... | collective-permute-start | bytes 393224 | tf_op jit(solution)/shard_map/ppermute | solution.py:287
  181.4 13.2 %collective-permute-start.56 = (bf16[128,2048]{1,0:T(8,128)(2,1)S(1)}, bf16[128,2048]{1,0:T(8,128)(2,1)S(1)}, u32[]{:S(2)}, u32[]{:S(2)}) collective-permute-start(bf16[128,2048]{1,0:T(8,128)(2,1)S(1)} %fusion.7), channel_id=1, source_target_pairs={{0,2},{1,3},{2,6},{3,7},{6,4},{7,5},{4,0},{5,1},{8,10},{9,11},{10,... | collective-permute-start | bytes 1572872 | tf_op jit(solution)/shard_map/home/ring/ppermute | solution.py:198
  182.1 5.9 %collective-permute-start.45 = (bf16[32,2048]{1,0:T(8,128)(2,1)S(1)}, bf16[32,2048]{1,0:T(8,128)(2,1)S(1)}, u32[]{:S(2)}, u32[]{:S(2)}) collective-permute-start(bf16[32,2048]{1,0:T(8,128)(2,1)S(1)} %get-tuple-element.82), channel_id=1, source_target_pairs={{0,24},{8,16},{16,8},{24,0},{1,25},{9,17},{17,9},{25,1},{2,26},{10... | collective-permute-start | bytes 393224 | tf_op jit(solution)/shard_map/ppermute | solution.py:287
  182.2 8.3 %collective-permute-start.44 = (bf16[32,2048]{1,0:T(8,128)(2,1)S(1)}, bf16[32,2048]{1,0:T(8,128)(2,1)S(1)}, u32[]{:S(2)}, u32[]{:S(2)}) collective-permute-start(bf16[32,2048]{1,0:T(8,128)(2,1)S(1)} %get-tuple-element.83), channel_id=1, source_target_pairs={{0,16},{8,24},{16,0},{24,8},{1,17},{9,25},{17,1},{25,9},{2,18},{10... | collective-permute-start | bytes 393224 | tf_op jit(solution)/shard_map/ppermute | solution.py:287
  183.5 6.9 %collective-permute-start.43 = (bf16[32,2048]{1,0:T(8,128)(2,1)S(1)}, bf16[32,2048]{1,0:T(8,128)(2,1)S(1)}, u32[]{:S(2)}, u32[]{:S(2)}) collective-permute-start(bf16[32,2048]{1,0:T(8,128)(2,1)S(1)} %get-tuple-element.84), channel_id=1, source_target_pairs={{0,8},{8,0},{16,24},{24,16},{1,9},{9,1},{17,25},{25,17},{2,10},{10... | collective-permute-start | bytes 393224 | tf_op jit(solution)/shard_map/ppermute | solution.py:287
  (4 other events, 7.4 us)

commit v4 on v3

--- a/solution.py
+++ b/solution.py
@@ -9,7 +9,7 @@
 
 HEADS = 16
 HALVES = 2
-TIES = {"E1": ["D0", "W2"], "E2": ["W3"], "H1": ["E2"], "H2": ["P1"], "H3": ["E0"], "E0": ["D1", "E3", "P1"], "X3": ["E0", "P2"], "S1": ["W0"], "Z2": ["W0"], "Z3": ["D0"], "G1": ["E3"], "E3": ["H1"]}
+TIES = {"E1": ["D0", "W2"], "E2": ["W3"], "H1": ["E2"], "H2": ["E3", "P1"], "H3": ["E0"], "E0": ["E3", "H2"], "X3": ["E0", "P2"], "S1": ["W0"], "Z2": ["W0"], "Z3": ["D0"], "G1": ["E3"]}
 ECOST = 4000000000
 ACOST = 1000
 

time: 196 us -> 195 us (level)
  transfers between devices with their start and end apart: 57 -> 57, of which waited for: 29 -> 28; matrix products, arithmetic and copies ran while one was open for 8% -> 8% of each run, Pallas kernels for 19% -> 19%
where the time goes in v4:
time: 195 us; the launch traced here: 194 us
  waiting for transfers between devices  87.4 us (45%)
  starting transfers between devices  49.6 us (25%)
  Pallas kernels  36.4 us (19%)
  matrix products  13.5 us (7%)
  local copies, waits for them, and re-layouts  4.14 us (2%)
  other arithmetic  2.57 us (1%)
    ppermute x13, waiting for transfers between devices, around(): return lax.ppermute(block, 'expert', ring_pairs[hop])  30.5 us
    pallas_call x4, Pallas kernels, expert_half(): pl.pallas_call(expert_kernel, in_specs=[anywhere] * (4 + len(earlier)), o...  30.3 us
    ppermute x24, waiting for transfers between devices, exchange(): parts[i] = lax.ppermute(parts[i], 'seq', swap_pairs(seq_count, i))  28.9 us
    ppermute x12, waiting for transfers between devices, other_half(): return lax.ppermute(block, 'expert', half_pairs)  18.4 us
    ppermute x13, starting transfers between devices, around(): return lax.ppermute(block, 'expert', ring_pairs[hop])  16.3 us
    ppermute x24, starting transfers between devices, exchange(): parts[i] = lax.ppermute(parts[i], 'seq', swap_pairs(seq_count, i))  15.7 us
    ppermute x12, starting transfers between devices, other_half(): return lax.ppermute(block, 'expert', half_pairs)  14 us
    ppermute x2, waiting for transfers between devices, on_device(): lax.ppermute(sources[which], 'seq', swap_pairs(seq_count, across))  8.39 us
  transfers between devices with their start and end apart: 57, of which 28 were waited for; matrix products, arithmetic and copies ran while one was open for 8% of the time, Pallas kernels for 19%

profile of v4, /device:TPU:0, one launch (start us, length us, event | category | flops | bytes accessed | tf_op | source)
XLA Modules:
  0.0 194.3 jit_solution(15678774908406539407)
XLA Ops:
  0.0 1.2 copy-done
  1.3 3.1 %collective-permute-start.2 = (bf16[256,1024]{1,0:T(8,128)(2,1)S(1)}, bf16[256,1024]{1,0:T(8,128)(2,1)}, u32[]{:S(2)}, u32[]{:S(2)}) collective-permute-start(bf16[256,1024]{1,0:T(8,128)(2,1)S(1)} %constant_dynamic-slice_fusion), channel_id=1, source_target_pairs={{0,2},{1,3},{2,6},{3,7},{6,4},{7,5},{4,0},{5,1},{8,10},{9,11},{10,... | collective-permute-start | bytes 1572872 | tf_op jit(solution)/shard_map/gather_0/ring/ppermute | solution.py:198
  4.3 1.5 collective-permute-start.1
  5.9 1.5 collective-permute-start.3
  9.6 7.8 %collective-permute-done.2 = bf16[256,1024]{1,0:T(8,128)(2,1)} collective-permute-done((bf16[256,1024]{1,0:T(8,128)(2,1)S(1)}, bf16[256,1024]{1,0:T(8,128)(2,1)}, u32[]{:S(2)}, u32[]{:S(2)}) %collective-permute-start.2) | collective-permute-done | bytes 524320 | tf_op jit(solution)/shard_map/gather_0/ring/ppermute | solution.py:198
  17.7 1.4 collective-permute-done.3.refs_3_
  19.2 1.5 collective-permute-start.8
  20.7 2.6 %collective-permute-start.7 = (bf16[256,1024]{1,0:T(8,128)(2,1)}, bf16[256,1024]{1,0:T(8,128)(2,1)}, u32[]{:S(2)}, u32[]{:S(2)}) collective-permute-start(bf16[256,1024]{1,0:T(8,128)(2,1)} %collective-permute-done.2), channel_id=1, source_target_pairs={{0,2},{1,3},{2,6},{3,7},{6,4},{7,5},{4,0},{5,1},{8,10},{9,11},{10,... | collective-permute-start | bytes 1572872 | tf_op jit(solution)/shard_map/gather_1/ring/ppermute | solution.py:198
  23.3 0.9 collective-permute-start.6
  24.6 6.9 %collective-permute-done.8.refs_7_ = bf16[128,2048]{1,0:T(8,128)(2,1)S(1)} collective-permute-done((bf16[128,2048]{1,0:T(8,128)(2,1)}, bf16[128,2048]{1,0:T(8,128)(2,1)S(1)}, u32[]{:S(2)}, u32[]{:S(2)}) %collective-permute-start.8) | collective-permute-done | bytes 524320 | tf_op jit(solution)/shard_map/gather_1/ppermute | solution.py:229
  31.6 2.2 %collective-permute-done.7 = bf16[256,1024]{1,0:T(8,128)(2,1)} collective-permute-done((bf16[256,1024]{1,0:T(8,128)(2,1)}, bf16[256,1024]{1,0:T(8,128)(2,1)}, u32[]{:S(2)}, u32[]{:S(2)}) %collective-permute-start.7) | collective-permute-done | bytes 524320 | tf_op jit(solution)/shard_map/gather_1/ring/ppermute | solution.py:198
  33.8 1.4 collective-permute-done.6
  35.4 1.3 collective-permute-start.12
  36.7 1.5 collective-permute-start.11
  38.2 6.1 %shard_map.100 = bf16[128,2048]{1,0:T(8,128)(2,1)} custom-call(bf16[128,2048]{1,0:T(8,128)(2,1)} %bitcast.96, bf16[128,2048]{1,0:T(8,128)(2,1)} %bitcast.99, bf16[128,2048]{1,0:T(8,128)(2,1)} %copy-done.7, bf16[128,2048]{1,0:T(8,128)(2,1)} %copy-done.5, bf16[128,2048]{1,0:T(8,128)(2,1)} %collective-permute-done.4.refs_4_, bf16[128,2048]{1,0:T(8,128)(2,1)} %bitcast.102, ...), custom_call_target="tpu_custom_call" | custom-call | flops 1000 | bytes 1000 | tf_op jit(solution)/shard_map/pallas_call | solution.py:80
  44.5 1.2 collective-permute-start.33
  45.8 1.7 collective-permute-start.28
  47.4 6.7 %collective-permute-done.33 = s32[2,128]{0,1:T(8,128)S(1)} collective-permute-done((s32[2,128]{0,1:T(8,128)S(1)}, s32[2,128]{0,1:T(8,128)S(1)}, u32[]{:S(2)}, u32[]{:S(2)}) %collective-permute-start.33) | collective-permute-done | bytes 1056 | tf_op jit(solution)/shard_map/gather_0/ring/ppermute | solution.py:198
  54.4 1.2 collective-permute-start.13
  55.6 2.0 %collective-permute-start.14 = (bf16[128,1024]{1,0:T(8,128)(2,1)S(1)}, bf16[128,1024]{1,0:T(8,128)(2,1)S(1)}, u32[]{:S(2)}, u32[]{:S(2)}) collective-permute-start(bf16[128,1024]{1,0:T(8,128)(2,1)S(1)} %slice.181), channel_id=1, source_target_pairs={{0,2},{1,3},{2,6},{3,7},{6,4},{7,5},{4,0},{5,1},{8,10},{9,11},{10,... | collective-permute-start | bytes 786440 | tf_op jit(solution)/shard_map/ring/ppermute | solution.py:198
  57.6 1.4 fusion.26
  59.0 1.4 fusion.30
  60.4 1.2 fusion.32
  62.5 1.3 fusion.28
  65.6 1.2 collective-permute-done.15
  67.7 1.7 collective-permute-start.21
  69.9 1.5 collective-permute-start.17
  72.0 3.6 %collective-permute-done.18 = bf16[32,2048]{1,0:T(8,128)(2,1)S(1)} collective-permute-done((bf16[32,2048]{1,0:T(8,128)(2,1)S(1)}, bf16[32,2048]{1,0:T(8,128)(2,1)S(1)}, u32[]{:S(2)}, u32[]{:S(2)}) %collective-permute-start.18) | collective-permute-done | bytes 131104 | tf_op jit(solution)/shard_map/ppermute | solution.py:287
  75.6 2.9 %collective-permute-done.17 = bf16[32,2048]{1,0:T(8,128)(2,1)S(1)} collective-permute-done((bf16[32,2048]{1,0:T(8,128)(2,1)S(1)}, bf16[32,2048]{1,0:T(8,128)(2,1)S(1)}, u32[]{:S(2)}, u32[]{:S(2)}) %collective-permute-start.17) | collective-permute-done | bytes 131104 | tf_op jit(solution)/shard_map/ppermute | solution.py:287
  78.5 1.2 collective-permute-start.19
  79.7 2.8 %collective-permute-done.21 = bf16[128,2048]{1,0:T(8,128)(2,1)S(1)} collective-permute-done((bf16[128,2048]{1,0:T(8,128)(2,1)S(1)}, bf16[128,2048]{1,0:T(8,128)(2,1)S(1)}, u32[]{:S(2)}, u32[]{:S(2)}) %collective-permute-start.21) | collective-permute-done | bytes 524320 | tf_op jit(solution)/shard_map/ring/ppermute | solution.py:198
  84.5 1.2 collective-permute-start.34
  86.0 3.6 %collective-permute-done.36 = bf16[32,2048]{1,0:T(8,128)(2,1)S(1)} collective-permute-done((bf16[32,2048]{1,0:T(8,128)(2,1)S(1)}, bf16[32,2048]{1,0:T(8,128)(2,1)S(1)}, u32[]{:S(2)}, u32[]{:S(2)}) %collective-permute-start.36) | collective-permute-done | bytes 131104 | tf_op jit(solution)/shard_map/ppermute | solution.py:287
  89.6 1.3 collective-permute-done.35
  90.9 1.2 collective-permute-start.37
  92.5 4.1 %collective-permute-done.22 = bf16[128,2048]{1,0:T(8,128)(2,1)S(1)} collective-permute-done((bf16[128,2048]{1,0:T(8,128)(2,1)S(1)}, bf16[128,2048]{1,0:T(8,128)(2,1)S(1)}, u32[]{:S(2)}, u32[]{:S(2)}) %collective-permute-start.22) | collective-permute-done | bytes 524320 | tf_op jit(solution)/shard_map/ring/ppermute | solution.py:198
  97.8 1.3 collective-permute-start.29
  99.3 3.6 %collective-permute-done.31 = bf16[32,2048]{1,0:T(8,128)(2,1)S(1)} collective-permute-done((bf16[32,2048]{1,0:T(8,128)(2,1)S(1)}, bf16[32,2048]{1,0:T(8,128)(2,1)S(1)}, u32[]{:S(2)}, u32[]{:S(2)}) %collective-permute-start.31) | collective-permute-done | bytes 131104 | tf_op jit(solution)/shard_map/ppermute | solution.py:287
  102.9 1.0 collective-permute-done.30
  104.0 1.0 collective-permute-start.32
  105.7 7.5 %shard_map.103 = (bf16[128,2048]{1,0:T(8,128)(2,1)S(1)}, bf16[128,2048]{1,0:T(8,128)(2,1)S(1)}) custom-call(bf16[128,2048]{1,0:T(8,128)(2,1)S(1)} %pad_maximum_fusion.3.own_ref, bf16[128,2048]{1,0:T(8,128)(2,1)S(1)} %collective-permute-done.37.other_ref, bf16[2048,2048]{1,0:T(8,128)(2,1)} %bitcast.82, bf16[2048,2048]{1,0:T(8,128)(2,1)} %bitcast.86, ...), custom_call_target="tpu_custom_call" | custom-call | flops 4000000000 | bytes 1000 | tf_op jit(solution)/shard_map/pallas_call | solution.py:145
  113.2 1.2 collective-permute-start.38
  115.7 1.0 collective-permute-start.25
  117.1 3.5 %collective-permute-done.26 = bf16[32,2048]{1,0:T(8,128)(2,1)S(1)} collective-permute-done((bf16[32,2048]{1,0:T(8,128)(2,1)S(1)}, bf16[32,2048]{1,0:T(8,128)(2,1)S(1)}, u32[]{:S(2)}, u32[]{:S(2)}) %collective-permute-start.26) | collective-permute-done | bytes 131104 | tf_op jit(solution)/shard_map/ppermute | solution.py:287
  120.7 2.9 %collective-permute-done.25 = bf16[32,2048]{1,0:T(8,128)(2,1)S(1)} collective-permute-done((bf16[32,2048]{1,0:T(8,128)(2,1)S(1)}, bf16[32,2048]{1,0:T(8,128)(2,1)S(1)}, u32[]{:S(2)}, u32[]{:S(2)}) %collective-permute-start.25) | collective-permute-done | bytes 131104 | tf_op jit(solution)/shard_map/ppermute | solution.py:287
  123.7 0.9 collective-permute-start.27
  124.6 7.5 %shard_map.102 = (bf16[128,2048]{1,0:T(8,128)(2,1)S(1)}, bf16[128,2048]{1,0:T(8,128)(2,1)S(1)}) custom-call(bf16[128,2048]{1,0:T(8,128)(2,1)S(1)} %pad_maximum_fusion.2.own_ref.refs_1_, bf16[128,2048]{1,0:T(8,128)(2,1)S(1)} %collective-permute-done.32.other_ref, bf16[2048,2048]{1,0:T(8,128)(2,1)} %bitcast.83, bf16[2048,2048]{1,0:T(8,128)(2,1)} %bitcast.87, ...), custom_call_target="tpu_custom_call" | custom-call | flops 4000000000 | bytes 1000 | tf_op jit(solution)/shard_map/pallas_call | solution.py:145
  134.2 1.2 collective-permute-start.42
  135.4 5.9 %collective-permute-done.27.other_ref = bf16[128,2048]{1,0:T(8,128)(2,1)S(1)} collective-permute-done((bf16[128,2048]{1,0:T(8,128)(2,1)S(1)}, bf16[128,2048]{1,0:T(8,128)(2,1)S(1)}, u32[]{:S(2)}, u32[]{:S(2)}) %collective-permute-start.27) | collective-permute-done | bytes 524320 | tf_op jit(solution)/shard_map/half/ppermute | solution.py:202
  141.3 7.7 %shard_map.101 = (bf16[128,2048]{1,0:T(8,128)(2,1)S(1)}, bf16[128,2048]{1,0:T(8,128)(2,1)S(1)}) custom-call(bf16[128,2048]{1,0:T(8,128)(2,1)S(1)} %pad_maximum_fusion.1.own_ref.refs_0_, bf16[128,2048]{1,0:T(8,128)(2,1)S(1)} %collective-permute-done.27.other_ref, bf16[2048,2048]{1,0:T(8,128)(2,1)} %bitcast.84, bf16[2048,2048]{1,0:T(8,128)(2,1)} %bitcast.88), custom_call_target="tpu_custom_call" | custom-call | flops 4000000000 | bytes 1000 | tf_op jit(solution)/shard_map/pallas_call | solution.py:145
  150.4 1.0 collective-permute-start.47
  151.3 1.2 collective-permute-done.42
  153.1 1.8 collective-permute-start.49
  154.9 7.5 %shard_map.104 = (bf16[128,2048]{1,0:T(8,128)(2,1)S(1)}, bf16[128,2048]{1,0:T(8,128)(2,1)S(1)}) custom-call(bf16[128,2048]{1,0:T(8,128)(2,1)S(1)} %pad_maximum_fusion.own_ref, bf16[128,2048]{1,0:T(8,128)(2,1)S(1)} %collective-permute-done.19.refs_0_.other_ref, bf16[2048,2048]{1,0:T(8,128)(2,1)} %bitcast.85, bf16[2048,2048]{1,0:T(8,128)(2,1)} %bitcast.89, ...), custom_call_target="tpu_custom_call" | custom-call | flops 4000000000 | bytes 1000 | tf_op jit(solution)/shard_map/pallas_call | solution.py:145
  162.4 1.1 collective-permute-start.43
  163.9 1.0 collective-permute-done.51
  167.1 1.0 collective-permute-start.53
  168.2 8.6 %collective-permute-done.43 = bf16[128,2048]{1,0:T(8,128)(2,1)S(1)} collective-permute-done((bf16[128,2048]{1,0:T(8,128)(2,1)S(1)}, bf16[128,2048]{1,0:T(8,128)(2,1)S(1)}, u32[]{:S(2)}, u32[]{:S(2)}) %collective-permute-start.43) | collective-permute-done | bytes 524320 | tf_op jit(solution)/shard_map/half/ppermute | solution.py:202
  177.3 2.1 %collective-permute-done.55 = bf16[128,2048]{1,0:T(8,128)(2,1)S(1)} collective-permute-done((bf16[128,2048]{1,0:T(8,128)(2,1)S(1)}, bf16[128,2048]{1,0:T(8,128)(2,1)S(1)}, u32[]{:S(2)}, u32[]{:S(2)}) %collective-permute-start.55) | collective-permute-done | bytes 524320 | tf_op jit(solution)/shard_map/ring/ppermute | solution.py:198
  180.7 1.3 collective-permute-start.45
  182.5 3.9 %collective-permute-done.46 = bf16[32,2048]{1,0:T(8,128)(2,1)S(1)} collective-permute-done((bf16[32,2048]{1,0:T(8,128)(2,1)S(1)}, bf16[32,2048]{1,0:T(8,128)(2,1)S(1)}, u32[]{:S(2)}, u32[]{:S(2)}) %collective-permute-start.46) | collective-permute-done | bytes 131104 | tf_op jit(solution)/shard_map/ppermute | solution.py:287
  186.5 2.5 %collective-permute-done.45 = bf16[32,2048]{1,0:T(8,128)(2,1)S(1)} collective-permute-done((bf16[32,2048]{1,0:T(8,128)(2,1)S(1)}, bf16[32,2048]{1,0:T(8,128)(2,1)S(1)}, u32[]{:S(2)}, u32[]{:S(2)}) %collective-permute-start.45) | collective-permute-done | bytes 131104 | tf_op jit(solution)/shard_map/ppermute | solution.py:287
  189.3 3.8 %collective-permute-done.56 = bf16[128,2048]{1,0:T(8,128)(2,1)S(1)} collective-permute-done((bf16[128,2048]{1,0:T(8,128)(2,1)S(1)}, bf16[128,2048]{1,0:T(8,128)(2,1)S(1)}, u32[]{:S(2)}, u32[]{:S(2)}) %collective-permute-start.56) | collective-permute-done | bytes 524320 | tf_op jit(solution)/shard_map/home/ring/ppermute | solution.py:198
  193.1 1.2 fusion.8
  (164 shorter events, 23.9 us)
Async XLA Ops:
  1.3 16.1 %collective-permute-start.2 = (bf16[256,1024]{1,0:T(8,128)(2,1)S(1)}, bf16[256,1024]{1,0:T(8,128)(2,1)}, u32[]{:S(2)}, u32[]{:S(2)}) collective-permute-start(bf16[256,1024]{1,0:T(8,128)(2,1)S(1)} %constant_dynamic-slice_fusion), channel_id=1, source_target_pairs={{0,2},{1,3},{2,6},{3,7},{6,4},{7,5},{4,0},{5,1},{8,10},{9,11},{10,... | collective-permute-start | bytes 1572872 | tf_op jit(solution)/shard_map/gather_0/ring/ppermute | solution.py:198
  4.3 13.4 %collective-permute-start.1 = (bf16[256,1024]{1,0:T(8,128)(2,1)S(1)}, bf16[256,1024]{1,0:T(8,128)(2,1)S(1)}, u32[]{:S(2)}, u32[]{:S(2)}) collective-permute-start(bf16[256,1024]{1,0:T(8,128)(2,1)S(1)} %constant_dynamic-slice_fusion), channel_id=1, source_target_pairs={{0,1},{1,0},{2,3},{3,2},{4,5},{5,4},{6,7},{7,6},{8,9},{9,8},{10,11... | collective-permute-start | bytes 1572872 | tf_op jit(solution)/shard_map/gather_0/half/ppermute | solution.py:202
  5.9 13.3 %collective-permute-start.3 = (bf16[128,2048]{1,0:T(8,128)(2,1)}, bf16[128,2048]{1,0:T(8,128)(2,1)S(1)}, u32[]{:S(2)}, u32[]{:S(2)}) collective-permute-start(bf16[128,2048]{1,0:T(8,128)(2,1)} %bitcast.97), channel_id=1, source_target_pairs={{0,16},{8,24},{16,0},{24,8},{1,17},{9,25},{17,1},{25,9},{2,18},{10... | collective-permute-start | bytes 1572872 | tf_op jit(solution)/shard_map/gather_0/ppermute | solution.py:229
  19.2 19.0 %copy-start.5 = (bf16[128,2048]{1,0:T(8,128)(2,1)}, bf16[128,2048]{1,0:T(8,128)(2,1)S(1)}, u32[]{:S(2)}) copy-start(bf16[128,2048]{1,0:T(8,128)(2,1)S(1)} %collective-permute-done.3.refs_3_) | copy-start | bytes 1572868
  19.2 12.4 %collective-permute-start.8 = (bf16[128,2048]{1,0:T(8,128)(2,1)}, bf16[128,2048]{1,0:T(8,128)(2,1)S(1)}, u32[]{:S(2)}, u32[]{:S(2)}) collective-permute-start(bf16[128,2048]{1,0:T(8,128)(2,1)} %bitcast.100), channel_id=1, source_target_pairs={{0,16},{8,24},{16,0},{24,8},{1,17},{9,25},{17,1},{25,9},{2,18},{10... | collective-permute-start | bytes 1572872 | tf_op jit(solution)/shard_map/gather_1/ppermute | solution.py:229
  20.7 13.1 %collective-permute-start.7 = (bf16[256,1024]{1,0:T(8,128)(2,1)}, bf16[256,1024]{1,0:T(8,128)(2,1)}, u32[]{:S(2)}, u32[]{:S(2)}) collective-permute-start(bf16[256,1024]{1,0:T(8,128)(2,1)} %collective-permute-done.2), channel_id=1, source_target_pairs={{0,2},{1,3},{2,6},{3,7},{6,4},{7,5},{4,0},{5,1},{8,10},{9,11},{10,... | collective-permute-start | bytes 1572872 | tf_op jit(solution)/shard_map/gather_1/ring/ppermute | solution.py:198
  23.3 11.9 %collective-permute-start.6 = (bf16[256,1024]{1,0:T(8,128)(2,1)}, bf16[256,1024]{1,0:T(8,128)(2,1)}, u32[]{:S(2)}, u32[]{:S(2)}) collective-permute-start(bf16[256,1024]{1,0:T(8,128)(2,1)} %collective-permute-done.2), channel_id=1, source_target_pairs={{0,1},{1,0},{2,3},{3,2},{4,5},{5,4},{6,7},{7,6},{8,9},{9,8},{10,11... | collective-permute-start | bytes 1572872 | tf_op jit(solution)/shard_map/gather_1/half/ppermute | solution.py:202
  24.1 12.6 %collective-permute-start = (bf16[128,2048]{1,0:T(8,128)(2,1)}, bf16[128,2048]{1,0:T(8,128)(2,1)S(1)}, u32[]{:S(2)}, u32[]{:S(2)}) collective-permute-start(bf16[128,2048]{1,0:T(8,128)(2,1)} %bitcast.98), channel_id=1, source_target_pairs={{0,8},{8,0},{16,24},{24,16},{1,9},{9,1},{17,25},{25,17},{2,10},{10... | collective-permute-start | bytes 1572872 | tf_op jit(solution)/shard_map/core/ppermute | solution.py:206
  24.1 14.1 %collective-permute-start.5 = (bf16[128,2048]{1,0:T(8,128)(2,1)}, bf16[128,2048]{1,0:T(8,128)(2,1)}, u32[]{:S(2)}, u32[]{:S(2)}) collective-permute-start(bf16[128,2048]{1,0:T(8,128)(2,1)} %bitcast.101), channel_id=1, source_target_pairs={{0,8},{8,0},{16,24},{24,16},{1,9},{9,1},{17,25},{25,17},{2,10},{10... | collective-permute-start | bytes 1572872 | tf_op jit(solution)/shard_map/core/ppermute | solution.py:206
  31.6 6.6 %copy-start.6 = (bf16[128,2048]{1,0:T(8,128)(2,1)}, bf16[128,2048]{1,0:T(8,128)(2,1)S(1)}, u32[]{:S(2)}) copy-start(bf16[128,2048]{1,0:T(8,128)(2,1)S(1)} %collective-permute-done.8.refs_7_) | copy-start | bytes 1572868
  31.6 6.6 %collective-permute-start.4 = (bf16[128,2048]{1,0:T(8,128)(2,1)S(1)}, bf16[128,2048]{1,0:T(8,128)(2,1)}, u32[]{:S(2)}, u32[]{:S(2)}) collective-permute-start(bf16[128,2048]{1,0:T(8,128)(2,1)S(1)} %collective-permute-done.3.refs_3_), channel_id=1, source_target_pairs={{0,8},{8,0},{16,24},{24,16},{1,9},{9,1},{17,25},{25,17},{2,10},{10... | collective-permute-start | bytes 1572872 | tf_op jit(solution)/shard_map/core/ppermute | solution.py:206
  35.2 3.0 %collective-permute-start.9 = (bf16[128,2048]{1,0:T(8,128)(2,1)S(1)}, bf16[128,2048]{1,0:T(8,128)(2,1)}, u32[]{:S(2)}, u32[]{:S(2)}) collective-permute-start(bf16[128,2048]{1,0:T(8,128)(2,1)S(1)} %collective-permute-done.8.refs_7_), channel_id=1, source_target_pairs={{0,8},{8,0},{16,24},{24,16},{1,9},{9,1},{17,25},{25,17},{2,10},{10... | collective-permute-start | bytes 1572872 | tf_op jit(solution)/shard_map/core/ppermute | solution.py:206
  35.4 18.9 %collective-permute-start.12 = (bf16[256,1024]{1,0:T(8,128)(2,1)}, bf16[256,1024]{1,0:T(8,128)(2,1)S(1)}, u32[]{:S(2)}, u32[]{:S(2)}) collective-permute-start(bf16[256,1024]{1,0:T(8,128)(2,1)} %collective-permute-done.7), channel_id=1, source_target_pairs={{0,2},{1,3},{2,6},{3,7},{6,4},{7,5},{4,0},{5,1},{8,10},{9,11},{10,... | collective-permute-start | bytes 1572872 | tf_op jit(solution)/shard_map/gather_2/ring/ppermute | solution.py:198
  36.7 17.6 %collective-permute-start.11 = (bf16[256,1024]{1,0:T(8,128)(2,1)}, bf16[256,1024]{1,0:T(8,128)(2,1)S(1)}, u32[]{:S(2)}, u32[]{:S(2)}) collective-permute-start(bf16[256,1024]{1,0:T(8,128)(2,1)} %collective-permute-done.7), channel_id=1, source_target_pairs={{0,1},{1,0},{2,3},{3,2},{4,5},{5,4},{6,7},{7,6},{8,9},{9,8},{10,11... | collective-permute-start | bytes 1572872 | tf_op jit(solution)/shard_map/gather_2/half/ppermute | solution.py:202
  44.4 17.2 %copy-start.2 = (bf16[128,2048]{1,0:T(8,128)(2,1)S(1)}, bf16[128,2048]{1,0:T(8,128)(2,1)}, u32[]{:S(2)}) copy-start(bf16[128,2048]{1,0:T(8,128)(2,1)} %shard_map.100) | copy-start | bytes 1572868
  44.4 17.5 %copy-start.9 = (bf16[256,1024]{1,0:T(8,128)(2,1)S(1)}, bf16[256,1024]{1,0:T(8,128)(2,1)}, u32[]{:S(2)}) copy-start(bf16[256,1024]{1,0:T(8,128)(2,1)} %copy-done.8) | copy-start | bytes 1572868
  44.4 13.3 %collective-permute-start.10 = (bf16[128,2048]{1,0:T(8,128)(2,1)}, bf16[128,2048]{1,0:T(8,128)(2,1)S(1)}, u32[]{:S(2)}, u32[]{:S(2)}) collective-permute-start(bf16[128,2048]{1,0:T(8,128)(2,1)} %shard_map.100), channel_id=1, source_target_pairs={{0,8},{8,0},{16,24},{24,16},{1,9},{9,1},{17,25},{25,17},{2,10},{10... | collective-permute-start | bytes 1572872 | tf_op jit(solution)/shard_map/core/ppermute | solution.py:206
  44.5 9.6 %collective-permute-start.33 = (s32[2,128]{0,1:T(8,128)S(1)}, s32[2,128]{0,1:T(8,128)S(1)}, u32[]{:S(2)}, u32[]{:S(2)}) collective-permute-start(s32[2,128]{0,1:T(8,128)S(1)} %bitcast.93), channel_id=1, source_target_pairs={{0,2},{1,3},{2,6},{3,7},{6,4},{7,5},{4,0},{5,1},{8,10},{9,11},{10,... | collective-permute-start | bytes 3080 | tf_op jit(solution)/shard_map/gather_0/ring/ppermute | solution.py:198
  45.8 8.4 %collective-permute-start.28 = (s32[2,128]{0,1:T(8,128)S(1)}, s32[2,128]{0,1:T(8,128)S(1)}, u32[]{:S(2)}, u32[]{:S(2)}) collective-permute-start(s32[2,128]{0,1:T(8,128)S(1)} %bitcast.94), channel_id=1, source_target_pairs={{0,6},{1,7},{2,4},{3,5},{6,0},{7,1},{4,2},{5,3},{8,14},{9,15},{10,... | collective-permute-start | bytes 3080 | tf_op jit(solution)/shard_map/gather_0/ring/ppermute | solution.py:198
  54.1 10.8 %collective-permute-start.20 = (s32[2,128]{0,1:T(8,128)S(1)}, s32[2,128]{0,1:T(8,128)S(1)}, u32[]{:S(2)}, u32[]{:S(2)}) collective-permute-start(s32[2,128]{0,1:T(8,128)S(1)} %bitcast.95), channel_id=1, source_target_pairs={{0,4},{1,5},{2,0},{3,1},{6,2},{7,3},{4,6},{5,7},{8,12},{9,13},{10,... | collective-permute-start | bytes 3080 | tf_op jit(solution)/shard_map/gather_0/ring/ppermute | solution.py:198
  54.4 7.8 %collective-permute-start.13 = (bf16[128,1024]{1,0:T(8,128)(2,1)S(1)}, bf16[128,1024]{1,0:T(8,128)(2,1)S(1)}, u32[]{:S(2)}, u32[]{:S(2)}) collective-permute-start(bf16[128,1024]{1,0:T(8,128)(2,1)S(1)} %slice.180), channel_id=1, source_target_pairs={{0,1},{1,0},{2,3},{3,2},{4,5},{5,4},{6,7},{7,6},{8,9},{9,8},{10,11... | collective-permute-start | bytes 786440 | tf_op jit(solution)/shard_map/half/ppermute | solution.py:202
  55.6 8.3 %collective-permute-start.14 = (bf16[128,1024]{1,0:T(8,128)(2,1)S(1)}, bf16[128,1024]{1,0:T(8,128)(2,1)S(1)}, u32[]{:S(2)}, u32[]{:S(2)}) collective-permute-start(bf16[128,1024]{1,0:T(8,128)(2,1)S(1)} %slice.181), channel_id=1, source_target_pairs={{0,2},{1,3},{2,6},{3,7},{6,4},{7,5},{4,0},{5,1},{8,10},{9,11},{10,... | collective-permute-start | bytes 786440 | tf_op jit(solution)/shard_map/ring/ppermute | solution.py:198
  64.2 3.2 %copy-start.10 = (f32[2048]{0:T(1024)S(1)}, f32[2048]{0:T(1024)}, u32[]{:S(2)}) copy-start(f32[2048]{0:T(1024)} %param.15) | copy-start | bytes 24580
  64.2 7.5 %copy-start.4 = (bf16[2048,16]{0,1:T(8,128)(2,1)S(1)}, bf16[2048,16]{0,1:T(8,128)(2,1)}, u32[]{:S(2)}) copy-start(bf16[2048,16]{0,1:T(8,128)(2,1)} %param.16) | copy-start | bytes 196612
  64.8 2.0 %collective-permute-start.15 = (f32[128,1024]{1,0:T(8,128)S(1)}, f32[128,1024]{1,0:T(8,128)S(1)}, u32[]{:S(2)}, u32[]{:S(2)}) collective-permute-start(f32[128,1024]{1,0:T(8,128)S(1)} %slice.234), channel_id=1, source_target_pairs={{0,8},{8,0},{16,24},{24,16},{1,9},{9,1},{17,25},{25,17},{2,10},{10... | collective-permute-start | bytes 1572872 | tf_op jit(solution)/shard_map/core/ppermute | solution.py:206
  67.7 14.9 %collective-permute-start.21 = (bf16[128,2048]{1,0:T(8,128)(2,1)S(1)}, bf16[128,2048]{1,0:T(8,128)(2,1)S(1)}, u32[]{:S(2)}, u32[]{:S(2)}) collective-permute-start(bf16[128,2048]{1,0:T(8,128)(2,1)S(1)} %multiply_convert_fusion), channel_id=1, source_target_pairs={{0,2},{1,3},{2,6},{3,7},{6,4},{7,5},{4,0},{5,1},{8,10},{9,11},{10,... | collective-permute-start | bytes 1572872 | tf_op jit(solution)/shard_map/ring/ppermute | solution.py:198
  69.8 5.8 %collective-permute-start.18 = (bf16[32,2048]{1,0:T(8,128)(2,1)S(1)}, bf16[32,2048]{1,0:T(8,128)(2,1)S(1)}, u32[]{:S(2)}, u32[]{:S(2)}) collective-permute-start(bf16[32,2048]{1,0:T(8,128)(2,1)S(1)} %get-tuple-element.102), channel_id=1, source_target_pairs={{0,24},{8,16},{16,8},{24,0},{1,25},{9,17},{17,9},{25,1},{2,26},{10... | collective-permute-start | bytes 393224 | tf_op jit(solution)/shard_map/ppermute | solution.py:287
  69.9 8.6 %collective-permute-start.17 = (bf16[32,2048]{1,0:T(8,128)(2,1)S(1)}, bf16[32,2048]{1,0:T(8,128)(2,1)S(1)}, u32[]{:S(2)}, u32[]{:S(2)}) collective-permute-start(bf16[32,2048]{1,0:T(8,128)(2,1)S(1)} %get-tuple-element.103), channel_id=1, source_target_pairs={{0,16},{8,24},{16,0},{24,8},{1,17},{9,25},{17,1},{25,9},{2,18},{10... | collective-permute-start | bytes 393224 | tf_op jit(solution)/shard_map/ppermute | solution.py:287
  71.4 7.1 %collective-permute-start.16 = (bf16[32,2048]{1,0:T(8,128)(2,1)S(1)}, bf16[32,2048]{1,0:T(8,128)(2,1)S(1)}, u32[]{:S(2)}, u32[]{:S(2)}) collective-permute-start(bf16[32,2048]{1,0:T(8,128)(2,1)S(1)} %get-tuple-element.104), channel_id=1, source_target_pairs={{0,8},{8,0},{16,24},{24,16},{1,9},{9,1},{17,25},{25,17},{2,10},{10... | collective-permute-start | bytes 393224 | tf_op jit(solution)/shard_map/ppermute | solution.py:287
  78.5 14.0 %collective-permute-start.19 = (bf16[128,2048]{1,0:T(8,128)(2,1)S(1)}, bf16[128,2048]{1,0:T(8,128)(2,1)S(1)}, u32[]{:S(2)}, u32[]{:S(2)}) collective-permute-start(bf16[128,2048]{1,0:T(8,128)(2,1)S(1)} %pad_maximum_fusion.own_ref), channel_id=1, source_target_pairs={{0,1},{1,0},{2,3},{3,2},{4,5},{5,4},{6,7},{7,6},{8,9},{9,8},{10,11... | collective-permute-start | bytes 1572872 | tf_op jit(solution)/shard_map/half/ppermute | solution.py:202
  82.6 14.0 %collective-permute-start.22 = (bf16[128,2048]{1,0:T(8,128)(2,1)S(1)}, bf16[128,2048]{1,0:T(8,128)(2,1)S(1)}, u32[]{:S(2)}, u32[]{:S(2)}) collective-permute-start(bf16[128,2048]{1,0:T(8,128)(2,1)S(1)} %collective-permute-done.21), channel_id=1, source_target_pairs={{0,2},{1,3},{2,6},{3,7},{6,4},{7,5},{4,0},{5,1},{8,10},{9,11},{10,... | collective-permute-start | bytes 1572872 | tf_op jit(solution)/shard_map/ring/ppermute | solution.py:198
  83.8 5.8 %collective-permute-start.36 = (bf16[32,2048]{1,0:T(8,128)(2,1)S(1)}, bf16[32,2048]{1,0:T(8,128)(2,1)S(1)}, u32[]{:S(2)}, u32[]{:S(2)}) collective-permute-start(bf16[32,2048]{1,0:T(8,128)(2,1)S(1)} %get-tuple-element.90), channel_id=1, source_target_pairs={{0,24},{8,16},{16,8},{24,0},{1,25},{9,17},{17,9},{25,1},{2,26},{10... | collective-permute-start | bytes 393224 | tf_op jit(solution)/shard_map/ppermute | solution.py:287
  83.8 7.0 %collective-permute-start.35 = (bf16[32,2048]{1,0:T(8,128)(2,1)S(1)}, bf16[32,2048]{1,0:T(8,128)(2,1)S(1)}, u32[]{:S(2)}, u32[]{:S(2)}) collective-permute-start(bf16[32,2048]{1,0:T(8,128)(2,1)S(1)} %get-tuple-element.91), channel_id=1, source_target_pairs={{0,16},{8,24},{16,0},{24,8},{1,17},{9,25},{17,1},{25,9},{2,18},{10... | collective-permute-start | bytes 393224 | tf_op jit(solution)/shard_map/ppermute | solution.py:287
  84.5 6.4 %collective-permute-start.34 = (bf16[32,2048]{1,0:T(8,128)(2,1)S(1)}, bf16[32,2048]{1,0:T(8,128)(2,1)S(1)}, u32[]{:S(2)}, u32[]{:S(2)}) collective-permute-start(bf16[32,2048]{1,0:T(8,128)(2,1)S(1)} %get-tuple-element.92), channel_id=1, source_target_pairs={{0,8},{8,0},{16,24},{24,16},{1,9},{9,1},{17,25},{25,17},{2,10},{10... | collective-permute-start | bytes 393224 | tf_op jit(solution)/shard_map/ppermute | solution.py:287
  90.9 14.8 %collective-permute-start.37 = (bf16[128,2048]{1,0:T(8,128)(2,1)S(1)}, bf16[128,2048]{1,0:T(8,128)(2,1)S(1)}, u32[]{:S(2)}, u32[]{:S(2)}) collective-permute-start(bf16[128,2048]{1,0:T(8,128)(2,1)S(1)} %pad_maximum_fusion.3.own_ref), channel_id=1, source_target_pairs={{0,1},{1,0},{2,3},{3,2},{4,5},{5,4},{6,7},{7,6},{8,9},{9,8},{10,11... | collective-permute-start | bytes 1572872 | tf_op jit(solution)/shard_map/half/ppermute | solution.py:202
  97.1 5.8 %collective-permute-start.31 = (bf16[32,2048]{1,0:T(8,128)(2,1)S(1)}, bf16[32,2048]{1,0:T(8,128)(2,1)S(1)}, u32[]{:S(2)}, u32[]{:S(2)}) collective-permute-start(bf16[32,2048]{1,0:T(8,128)(2,1)S(1)} %get-tuple-element.94), channel_id=1, source_target_pairs={{0,24},{8,16},{16,8},{24,0},{1,25},{9,17},{17,9},{25,1},{2,26},{10... | collective-permute-start | bytes 393224 | tf_op jit(solution)/shard_map/ppermute | solution.py:287
  97.2 6.8 %collective-permute-start.30 = (bf16[32,2048]{1,0:T(8,128)(2,1)S(1)}, bf16[32,2048]{1,0:T(8,128)(2,1)S(1)}, u32[]{:S(2)}, u32[]{:S(2)}) collective-permute-start(bf16[32,2048]{1,0:T(8,128)(2,1)S(1)} %get-tuple-element.95), channel_id=1, source_target_pairs={{0,16},{8,24},{16,0},{24,8},{1,17},{9,25},{17,1},{25,9},{2,18},{10... | collective-permute-start | bytes 393224 | tf_op jit(solution)/shard_map/ppermute | solution.py:287
  97.8 6.2 %collective-permute-start.29 = (bf16[32,2048]{1,0:T(8,128)(2,1)S(1)}, bf16[32,2048]{1,0:T(8,128)(2,1)S(1)}, u32[]{:S(2)}, u32[]{:S(2)}) collective-permute-start(bf16[32,2048]{1,0:T(8,128)(2,1)S(1)} %get-tuple-element.96), channel_id=1, source_target_pairs={{0,8},{8,0},{16,24},{24,16},{1,9},{9,1},{17,25},{25,17},{2,10},{10... | collective-permute-start | bytes 393224 | tf_op jit(solution)/shard_map/ppermute | solution.py:287
  99.0 15.4 %collective-permute-start.23 = (bf16[128,2048]{1,0:T(8,128)(2,1)S(1)}, bf16[128,2048]{1,0:T(8,128)(2,1)S(1)}, u32[]{:S(2)}, u32[]{:S(2)}) collective-permute-start(bf16[128,2048]{1,0:T(8,128)(2,1)S(1)} %collective-permute-done.22), channel_id=1, source_target_pairs={{0,2},{1,3},{2,6},{3,7},{6,4},{7,5},{4,0},{5,1},{8,10},{9,11},{10,... | collective-permute-start | bytes 1572872 | tf_op jit(solution)/shard_map/ring/ppermute | solution.py:198
  104.0 20.6 %collective-permute-start.32 = (bf16[128,2048]{1,0:T(8,128)(2,1)S(1)}, bf16[128,2048]{1,0:T(8,128)(2,1)S(1)}, u32[]{:S(2)}, u32[]{:S(2)}) collective-permute-start(bf16[128,2048]{1,0:T(8,128)(2,1)S(1)} %pad_maximum_fusion.2.own_ref.refs_1_), channel_id=1, source_target_pairs={{0,1},{1,0},{2,3},{3,2},{4,5},{5,4},{6,7},{7,6},{8,9},{9,8},{10,11... | collective-permute-start | bytes 1572872 | tf_op jit(solution)/shard_map/half/ppermute | solution.py:202
  113.2 18.9 %collective-permute-start.38 = (bf16[128,2048]{1,0:T(8,128)(2,1)S(1)}, bf16[128,2048]{1,0:T(8,128)(2,1)S(1)}, u32[]{:S(2)}, u32[]{:S(2)}) collective-permute-start(bf16[128,2048]{1,0:T(8,128)(2,1)S(1)} %get-tuple-element.49), channel_id=1, source_target_pairs={{0,1},{1,0},{2,3},{3,2},{4,5},{5,4},{6,7},{7,6},{8,9},{9,8},{10,11... | collective-permute-start | bytes 1572872 | tf_op jit(solution)/shard_map/half/ppermute | solution.py:202
  114.9 5.7 %collective-permute-start.26 = (bf16[32,2048]{1,0:T(8,128)(2,1)S(1)}, bf16[32,2048]{1,0:T(8,128)(2,1)S(1)}, u32[]{:S(2)}, u32[]{:S(2)}) collective-permute-start(bf16[32,2048]{1,0:T(8,128)(2,1)S(1)} %get-tuple-element.98), channel_id=1, source_target_pairs={{0,24},{8,16},{16,8},{24,0},{1,25},{9,17},{17,9},{25,1},{2,26},{10... | collective-permute-start | bytes 393224 | tf_op jit(solution)/shard_map/ppermute | solution.py:287
  115.7 7.9 %collective-permute-start.25 = (bf16[32,2048]{1,0:T(8,128)(2,1)S(1)}, bf16[32,2048]{1,0:T(8,128)(2,1)S(1)}, u32[]{:S(2)}, u32[]{:S(2)}) collective-permute-start(bf16[32,2048]{1,0:T(8,128)(2,1)S(1)} %get-tuple-element.99), channel_id=1, source_target_pairs={{0,16},{8,24},{16,0},{24,8},{1,17},{9,25},{17,1},{25,9},{2,18},{10... | collective-permute-start | bytes 393224 | tf_op jit(solution)/shard_map/ppermute | solution.py:287
  116.6 7.0 %collective-permute-start.24 = (bf16[32,2048]{1,0:T(8,128)(2,1)S(1)}, bf16[32,2048]{1,0:T(8,128)(2,1)S(1)}, u32[]{:S(2)}, u32[]{:S(2)}) collective-permute-start(bf16[32,2048]{1,0:T(8,128)(2,1)S(1)} %get-tuple-element.100), channel_id=1, source_target_pairs={{0,8},{8,0},{16,24},{24,16},{1,9},{9,1},{17,25},{25,17},{2,10},{10... | collective-permute-start | bytes 393224 | tf_op jit(solution)/shard_map/ppermute | solution.py:287
  123.7 17.6 %collective-permute-start.27 = (bf16[128,2048]{1,0:T(8,128)(2,1)S(1)}, bf16[128,2048]{1,0:T(8,128)(2,1)S(1)}, u32[]{:S(2)}, u32[]{:S(2)}) collective-permute-start(bf16[128,2048]{1,0:T(8,128)(2,1)S(1)} %pad_maximum_fusion.1.own_ref.refs_0_), channel_id=1, source_target_pairs={{0,1},{1,0},{2,3},{3,2},{4,5},{5,4},{6,7},{7,6},{8,9},{9,8},{10,11... | collective-permute-start | bytes 1572872 | tf_op jit(solution)/shard_map/half/ppermute | solution.py:202
  132.3 16.7 %collective-permute-start.41 = (bf16[32,2048]{1,0:T(8,128)(2,1)S(1)}, bf16[32,2048]{1,0:T(8,128)(2,1)S(1)}, u32[]{:S(2)}, u32[]{:S(2)}) collective-permute-start(bf16[32,2048]{1,0:T(8,128)(2,1)S(1)} %get-tuple-element.85), channel_id=1, source_target_pairs={{0,24},{8,16},{16,8},{24,0},{1,25},{9,17},{17,9},{25,1},{2,26},{10... | collective-permute-start | bytes 393224 | tf_op jit(solution)/shard_map/ppermute | solution.py:287
  133.2 15.9 %collective-permute-start.40 = (bf16[32,2048]{1,0:T(8,128)(2,1)S(1)}, bf16[32,2048]{1,0:T(8,128)(2,1)S(1)}, u32[]{:S(2)}, u32[]{:S(2)}) collective-permute-start(bf16[32,2048]{1,0:T(8,128)(2,1)S(1)} %get-tuple-element.86), channel_id=1, source_target_pairs={{0,16},{8,24},{16,0},{24,8},{1,17},{9,25},{17,1},{25,9},{2,18},{10... | collective-permute-start | bytes 393224 | tf_op jit(solution)/shard_map/ppermute | solution.py:287
  133.6 15.4 %collective-permute-start.39 = (bf16[32,2048]{1,0:T(8,128)(2,1)S(1)}, bf16[32,2048]{1,0:T(8,128)(2,1)S(1)}, u32[]{:S(2)}, u32[]{:S(2)}) collective-permute-start(bf16[32,2048]{1,0:T(8,128)(2,1)S(1)} %get-tuple-element.87), channel_id=1, source_target_pairs={{0,8},{8,0},{16,24},{24,16},{1,9},{9,1},{17,25},{25,17},{2,10},{10... | collective-permute-start | bytes 393224 | tf_op jit(solution)/shard_map/ppermute | solution.py:287
  134.2 18.3 %collective-permute-start.42 = (bf16[128,2048]{1,0:T(8,128)(2,1)S(1)}, bf16[128,2048]{1,0:T(8,128)(2,1)S(1)}, u32[]{:S(2)}, u32[]{:S(2)}) collective-permute-start(bf16[128,2048]{1,0:T(8,128)(2,1)S(1)} %get-tuple-element.55), channel_id=1, source_target_pairs={{0,1},{1,0},{2,3},{3,2},{4,5},{5,4},{6,7},{7,6},{8,9},{9,8},{10,11... | collective-permute-start | bytes 1572872 | tf_op jit(solution)/shard_map/half/ppermute | solution.py:202
  149.9 15.0 %collective-permute-start.51 = (bf16[128,2048]{1,0:T(8,128)(2,1)S(1)}, bf16[128,2048]{1,0:T(8,128)(2,1)S(1)}, u32[]{:S(2)}, u32[]{:S(2)}) collective-permute-start(bf16[128,2048]{1,0:T(8,128)(2,1)S(1)} %fusion.5), channel_id=1, source_target_pairs={{0,2},{1,3},{2,6},{3,7},{6,4},{7,5},{4,0},{5,1},{8,10},{9,11},{10,... | collective-permute-start | bytes 1572872 | tf_op jit(solution)/shard_map/ring/ppermute | solution.py:198
  150.4 15.7 %collective-permute-start.47 = (bf16[128,2048]{1,0:T(8,128)(2,1)S(1)}, bf16[128,2048]{1,0:T(8,128)(2,1)S(1)}, u32[]{:S(2)}, u32[]{:S(2)}) collective-permute-start(bf16[128,2048]{1,0:T(8,128)(2,1)S(1)} %get-tuple-element.59), channel_id=1, source_target_pairs={{0,1},{1,0},{2,3},{3,2},{4,5},{5,4},{6,7},{7,6},{8,9},{9,8},{10,11... | collective-permute-start | bytes 1572872 | tf_op jit(solution)/shard_map/half/ppermute | solution.py:202
  152.7 9.7 %collective-permute-start.50 = (bf16[32,2048]{1,0:T(8,128)(2,1)S(1)}, bf16[32,2048]{1,0:T(8,128)(2,1)S(1)}, u32[]{:S(2)}, u32[]{:S(2)}) collective-permute-start(bf16[32,2048]{1,0:T(8,128)(2,1)S(1)} %get-tuple-element.78), channel_id=1, source_target_pairs={{0,24},{8,16},{16,8},{24,0},{1,25},{9,17},{17,9},{25,1},{2,26},{10... | collective-permute-start | bytes 393224 | tf_op jit(solution)/shard_map/ppermute | solution.py:287
  153.1 10.5 %collective-permute-start.49 = (bf16[32,2048]{1,0:T(8,128)(2,1)S(1)}, bf16[32,2048]{1,0:T(8,128)(2,1)S(1)}, u32[]{:S(2)}, u32[]{:S(2)}) collective-permute-start(bf16[32,2048]{1,0:T(8,128)(2,1)S(1)} %get-tuple-element.79), channel_id=1, source_target_pairs={{0,16},{8,24},{16,0},{24,8},{1,17},{9,25},{17,1},{25,9},{2,18},{10... | collective-permute-start | bytes 393224 | tf_op jit(solution)/shard_map/ppermute | solution.py:287
  154.9 8.7 %collective-permute-start.48 = (bf16[32,2048]{1,0:T(8,128)(2,1)S(1)}, bf16[32,2048]{1,0:T(8,128)(2,1)S(1)}, u32[]{:S(2)}, u32[]{:S(2)}) collective-permute-start(bf16[32,2048]{1,0:T(8,128)(2,1)S(1)} %get-tuple-element.80), channel_id=1, source_target_pairs={{0,8},{8,0},{16,24},{24,16},{1,9},{9,1},{17,25},{25,17},{2,10},{10... | collective-permute-start | bytes 393224 | tf_op jit(solution)/shard_map/ppermute | solution.py:287
  162.4 14.4 %collective-permute-start.43 = (bf16[128,2048]{1,0:T(8,128)(2,1)S(1)}, bf16[128,2048]{1,0:T(8,128)(2,1)S(1)}, u32[]{:S(2)}, u32[]{:S(2)}) collective-permute-start(bf16[128,2048]{1,0:T(8,128)(2,1)S(1)} %get-tuple-element.57), channel_id=1, source_target_pairs={{0,1},{1,0},{2,3},{3,2},{4,5},{5,4},{6,7},{7,6},{8,9},{9,8},{10,11... | collective-permute-start | bytes 1572872 | tf_op jit(solution)/shard_map/half/ppermute | solution.py:202
  164.9 29.4 %copy-start.1 = (bf16[256,2048]{1,0:T(8,128)(2,1)S(1)}, bf16[256,2048]{1,0:T(8,128)(2,1)}, u32[]{:S(2)}) copy-start(bf16[256,2048]{1,0:T(8,128)(2,1)} %param.14) | copy-start | bytes 3145732
  165.3 14.2 %collective-permute-start.55 = (bf16[128,2048]{1,0:T(8,128)(2,1)S(1)}, bf16[128,2048]{1,0:T(8,128)(2,1)S(1)}, u32[]{:S(2)}, u32[]{:S(2)}) collective-permute-start(bf16[128,2048]{1,0:T(8,128)(2,1)S(1)} %fusion.6), channel_id=1, source_target_pairs={{0,2},{1,3},{2,6},{3,7},{6,4},{7,5},{4,0},{5,1},{8,10},{9,11},{10,... | collective-permute-start | bytes 1572872 | tf_op jit(solution)/shard_map/ring/ppermute | solution.py:198
  166.3 10.7 %collective-permute-start.54 = (bf16[32,2048]{1,0:T(8,128)(2,1)S(1)}, bf16[32,2048]{1,0:T(8,128)(2,1)S(1)}, u32[]{:S(2)}, u32[]{:S(2)}) collective-permute-start(bf16[32,2048]{1,0:T(8,128)(2,1)S(1)} %get-tuple-element.74), channel_id=1, source_target_pairs={{0,24},{8,16},{16,8},{24,0},{1,25},{9,17},{17,9},{25,1},{2,26},{10... | collective-permute-start | bytes 393224 | tf_op jit(solution)/shard_map/ppermute | solution.py:287
  167.1 9.8 %collective-permute-start.53 = (bf16[32,2048]{1,0:T(8,128)(2,1)S(1)}, bf16[32,2048]{1,0:T(8,128)(2,1)S(1)}, u32[]{:S(2)}, u32[]{:S(2)}) collective-permute-start(bf16[32,2048]{1,0:T(8,128)(2,1)S(1)} %get-tuple-element.75), channel_id=1, source_target_pairs={{0,16},{8,24},{16,0},{24,8},{1,17},{9,25},{17,1},{25,9},{2,18},{10... | collective-permute-start | bytes 393224 | tf_op jit(solution)/shard_map/ppermute | solution.py:287
  168.2 8.8 %collective-permute-start.52 = (bf16[32,2048]{1,0:T(8,128)(2,1)S(1)}, bf16[32,2048]{1,0:T(8,128)(2,1)S(1)}, u32[]{:S(2)}, u32[]{:S(2)}) collective-permute-start(bf16[32,2048]{1,0:T(8,128)(2,1)S(1)} %get-tuple-element.76), channel_id=1, source_target_pairs={{0,8},{8,0},{16,24},{24,16},{1,9},{9,1},{17,25},{25,17},{2,10},{10... | collective-permute-start | bytes 393224 | tf_op jit(solution)/shard_map/ppermute | solution.py:287
  179.8 13.2 %collective-permute-start.56 = (bf16[128,2048]{1,0:T(8,128)(2,1)S(1)}, bf16[128,2048]{1,0:T(8,128)(2,1)S(1)}, u32[]{:S(2)}, u32[]{:S(2)}) collective-permute-start(bf16[128,2048]{1,0:T(8,128)(2,1)S(1)} %fusion.7), channel_id=1, source_target_pairs={{0,2},{1,3},{2,6},{3,7},{6,4},{7,5},{4,0},{5,1},{8,10},{9,11},{10,... | collective-permute-start | bytes 1572872 | tf_op jit(solution)/shard_map/home/ring/ppermute | solution.py:198
  180.6 5.9 %collective-permute-start.46 = (bf16[32,2048]{1,0:T(8,128)(2,1)S(1)}, bf16[32,2048]{1,0:T(8,128)(2,1)S(1)}, u32[]{:S(2)}, u32[]{:S(2)}) collective-permute-start(bf16[32,2048]{1,0:T(8,128)(2,1)S(1)} %get-tuple-element.82), channel_id=1, source_target_pairs={{0,24},{8,16},{16,8},{24,0},{1,25},{9,17},{17,9},{25,1},{2,26},{10... | collective-permute-start | bytes 393224 | tf_op jit(solution)/shard_map/ppermute | solution.py:287
  180.7 8.3 %collective-permute-start.45 = (bf16[32,2048]{1,0:T(8,128)(2,1)S(1)}, bf16[32,2048]{1,0:T(8,128)(2,1)S(1)}, u32[]{:S(2)}, u32[]{:S(2)}) collective-permute-start(bf16[32,2048]{1,0:T(8,128)(2,1)S(1)} %get-tuple-element.83), channel_id=1, source_target_pairs={{0,16},{8,24},{16,0},{24,8},{1,17},{9,25},{17,1},{25,9},{2,18},{10... | collective-permute-start | bytes 393224 | tf_op jit(solution)/shard_map/ppermute | solution.py:287
  182.0 6.9 %collective-permute-start.44 = (bf16[32,2048]{1,0:T(8,128)(2,1)S(1)}, bf16[32,2048]{1,0:T(8,128)(2,1)S(1)}, u32[]{:S(2)}, u32[]{:S(2)}) collective-permute-start(bf16[32,2048]{1,0:T(8,128)(2,1)S(1)} %get-tuple-element.84), channel_id=1, source_target_pairs={{0,8},{8,0},{16,24},{24,16},{1,9},{9,1},{17,25},{25,17},{2,10},{10... | collective-permute-start | bytes 393224 | tf_op jit(solution)/shard_map/ppermute | solution.py:287
  (4 other events, 7.3 us)

commit v5 on v4

--- a/solution.py
+++ b/solution.py
@@ -9,7 +9,7 @@
 
 HEADS = 16
 HALVES = 2
-TIES = {"E1": ["D0", "W2"], "E2": ["W3"], "H1": ["E2"], "H2": ["E3", "P1"], "H3": ["E0"], "E0": ["E3", "H2"], "X3": ["E0", "P2"], "S1": ["W0"], "Z2": ["W0"], "Z3": ["D0"], "G1": ["E3"]}
+TIES = {"E1": ["D0", "W2"], "E2": ["W3"], "H1": ["E2"], "H2": ["E3", "P1"], "H3": ["E0"], "E0": ["E3", "H2"], "X3": ["E0", "P2"], "S1": ["W0"], "Z2": ["W0"], "G1": ["E3"]}
 ECOST = 4000000000
 ACOST = 1000
 

time: 195 us -> 195 us (level)
    ppermute x12, waiting for transfers between devices: 18.4 us -> 15.7 us  [other_half(): return lax.ppermute(block, 'expert', half_pairs)]
where the time goes in v5:
time: 195 us; the launch traced here: 194 us
  waiting for transfers between devices  85.9 us (44%)
  starting transfers between devices  51.1 us (26%)
  Pallas kernels  36.4 us (19%)
  matrix products  13.5 us (7%)
  local copies, waits for them, and re-layouts  4.14 us (2%)
  other arithmetic  2.57 us (1%)
    ppermute x13, waiting for transfers between devices, around(): return lax.ppermute(block, 'expert', ring_pairs[hop])  32.3 us
    pallas_call x4, Pallas kernels, expert_half(): pl.pallas_call(expert_kernel, in_specs=[anywhere] * (4 + len(earlier)), o...  30.3 us
    ppermute x24, waiting for transfers between devices, exchange(): parts[i] = lax.ppermute(parts[i], 'seq', swap_pairs(seq_count, i))  28.2 us
    ppermute x13, starting transfers between devices, around(): return lax.ppermute(block, 'expert', ring_pairs[hop])  17.2 us
    ppermute x24, starting transfers between devices, exchange(): parts[i] = lax.ppermute(parts[i], 'seq', swap_pairs(seq_count, i))  16.4 us
    ppermute x12, waiting for transfers between devices, other_half(): return lax.ppermute(block, 'expert', half_pairs)  15.7 us
    ppermute x12, starting transfers between devices, other_half(): return lax.ppermute(block, 'expert', half_pairs)  13.9 us
    ppermute x2, waiting for transfers between devices, on_device(): lax.ppermute(sources[which], 'seq', swap_pairs(seq_count, across))  8.39 us
  transfers between devices with their start and end apart: 57, of which 28 were waited for; matrix products, arithmetic and copies ran while one was open for 8% of the time, Pallas kernels for 19%

profile of v5, /device:TPU:0, one launch (start us, length us, event | category | flops | bytes accessed | tf_op | source)
XLA Modules:
  0.0 194.3 jit_solution(18132638934131736251)
XLA Ops:
  0.0 1.2 copy-done
  1.3 3.1 %collective-permute-start.2 = (bf16[256,1024]{1,0:T(8,128)(2,1)S(1)}, bf16[256,1024]{1,0:T(8,128)(2,1)}, u32[]{:S(2)}, u32[]{:S(2)}) collective-permute-start(bf16[256,1024]{1,0:T(8,128)(2,1)S(1)} %constant_dynamic-slice_fusion), channel_id=1, source_target_pairs={{0,2},{1,3},{2,6},{3,7},{6,4},{7,5},{4,0},{5,1},{8,10},{9,11},{10,... | collective-permute-start | bytes 1572872 | tf_op jit(solution)/shard_map/gather_0/ring/ppermute | solution.py:198
  4.3 1.5 collective-permute-start.1
  5.9 1.5 collective-permute-start.3
  9.6 7.8 %collective-permute-done.2 = bf16[256,1024]{1,0:T(8,128)(2,1)} collective-permute-done((bf16[256,1024]{1,0:T(8,128)(2,1)S(1)}, bf16[256,1024]{1,0:T(8,128)(2,1)}, u32[]{:S(2)}, u32[]{:S(2)}) %collective-permute-start.2) | collective-permute-done | bytes 524320 | tf_op jit(solution)/shard_map/gather_0/ring/ppermute | solution.py:198
  17.7 1.4 collective-permute-done.3.refs_3_
  19.2 1.5 collective-permute-start.8
  20.7 2.6 %collective-permute-start.7 = (bf16[256,1024]{1,0:T(8,128)(2,1)}, bf16[256,1024]{1,0:T(8,128)(2,1)}, u32[]{:S(2)}, u32[]{:S(2)}) collective-permute-start(bf16[256,1024]{1,0:T(8,128)(2,1)} %collective-permute-done.2), channel_id=1, source_target_pairs={{0,2},{1,3},{2,6},{3,7},{6,4},{7,5},{4,0},{5,1},{8,10},{9,11},{10,... | collective-permute-start | bytes 1572872 | tf_op jit(solution)/shard_map/gather_1/ring/ppermute | solution.py:198
  24.6 6.9 %collective-permute-done.8.refs_7_ = bf16[128,2048]{1,0:T(8,128)(2,1)S(1)} collective-permute-done((bf16[128,2048]{1,0:T(8,128)(2,1)}, bf16[128,2048]{1,0:T(8,128)(2,1)S(1)}, u32[]{:S(2)}, u32[]{:S(2)}) %collective-permute-start.8) | collective-permute-done | bytes 524320 | tf_op jit(solution)/shard_map/gather_1/ppermute | solution.py:229
  31.6 2.2 %collective-permute-done.7 = bf16[256,1024]{1,0:T(8,128)(2,1)} collective-permute-done((bf16[256,1024]{1,0:T(8,128)(2,1)}, bf16[256,1024]{1,0:T(8,128)(2,1)}, u32[]{:S(2)}, u32[]{:S(2)}) %collective-permute-start.7) | collective-permute-done | bytes 524320 | tf_op jit(solution)/shard_map/gather_1/ring/ppermute | solution.py:198
  33.8 1.4 collective-permute-done.6
  35.4 1.3 collective-permute-start.12
  36.7 1.5 collective-permute-start.11
  38.2 6.1 %shard_map.100 = bf16[128,2048]{1,0:T(8,128)(2,1)} custom-call(bf16[128,2048]{1,0:T(8,128)(2,1)} %bitcast.96, bf16[128,2048]{1,0:T(8,128)(2,1)} %bitcast.99, bf16[128,2048]{1,0:T(8,128)(2,1)} %copy-done.7, bf16[128,2048]{1,0:T(8,128)(2,1)} %copy-done.5, bf16[128,2048]{1,0:T(8,128)(2,1)} %collective-permute-done.4.refs_4_, bf16[128,2048]{1,0:T(8,128)(2,1)} %bitcast.102, ...), custom_call_target="tpu_custom_call" | custom-call | flops 1000 | bytes 1000 | tf_op jit(solution)/shard_map/pallas_call | solution.py:80
  44.5 1.2 collective-permute-start.33
  45.8 1.7 collective-permute-start.28
  47.4 6.7 %collective-permute-done.33 = s32[2,128]{0,1:T(8,128)S(1)} collective-permute-done((s32[2,128]{0,1:T(8,128)S(1)}, s32[2,128]{0,1:T(8,128)S(1)}, u32[]{:S(2)}, u32[]{:S(2)}) %collective-permute-start.33) | collective-permute-done | bytes 1056 | tf_op jit(solution)/shard_map/gather_0/ring/ppermute | solution.py:198
  54.4 1.2 collective-permute-start.13
  55.6 2.0 %collective-permute-start.14 = (bf16[128,1024]{1,0:T(8,128)(2,1)S(1)}, bf16[128,1024]{1,0:T(8,128)(2,1)S(1)}, u32[]{:S(2)}, u32[]{:S(2)}) collective-permute-start(bf16[128,1024]{1,0:T(8,128)(2,1)S(1)} %slice.181), channel_id=1, source_target_pairs={{0,2},{1,3},{2,6},{3,7},{6,4},{7,5},{4,0},{5,1},{8,10},{9,11},{10,... | collective-permute-start | bytes 786440 | tf_op jit(solution)/shard_map/ring/ppermute | solution.py:198
  57.6 1.4 fusion.26
  59.0 1.4 fusion.30
  60.4 1.2 fusion.32
  62.5 1.3 fusion.28
  65.6 1.2 collective-permute-done.15
  67.7 1.7 collective-permute-start.21
  69.9 1.5 collective-permute-start.17
  72.0 3.6 %collective-permute-done.18 = bf16[32,2048]{1,0:T(8,128)(2,1)S(1)} collective-permute-done((bf16[32,2048]{1,0:T(8,128)(2,1)S(1)}, bf16[32,2048]{1,0:T(8,128)(2,1)S(1)}, u32[]{:S(2)}, u32[]{:S(2)}) %collective-permute-start.18) | collective-permute-done | bytes 131104 | tf_op jit(solution)/shard_map/ppermute | solution.py:287
  75.6 2.9 %collective-permute-done.17 = bf16[32,2048]{1,0:T(8,128)(2,1)S(1)} collective-permute-done((bf16[32,2048]{1,0:T(8,128)(2,1)S(1)}, bf16[32,2048]{1,0:T(8,128)(2,1)S(1)}, u32[]{:S(2)}, u32[]{:S(2)}) %collective-permute-start.17) | collective-permute-done | bytes 131104 | tf_op jit(solution)/shard_map/ppermute | solution.py:287
  78.5 1.2 collective-permute-start.19
  79.7 2.8 %collective-permute-done.21 = bf16[128,2048]{1,0:T(8,128)(2,1)S(1)} collective-permute-done((bf16[128,2048]{1,0:T(8,128)(2,1)S(1)}, bf16[128,2048]{1,0:T(8,128)(2,1)S(1)}, u32[]{:S(2)}, u32[]{:S(2)}) %collective-permute-start.21) | collective-permute-done | bytes 524320 | tf_op jit(solution)/shard_map/ring/ppermute | solution.py:198
  84.5 1.2 collective-permute-start.34
  86.0 3.6 %collective-permute-done.36 = bf16[32,2048]{1,0:T(8,128)(2,1)S(1)} collective-permute-done((bf16[32,2048]{1,0:T(8,128)(2,1)S(1)}, bf16[32,2048]{1,0:T(8,128)(2,1)S(1)}, u32[]{:S(2)}, u32[]{:S(2)}) %collective-permute-start.36) | collective-permute-done | bytes 131104 | tf_op jit(solution)/shard_map/ppermute | solution.py:287
  89.6 1.3 collective-permute-done.35
  90.9 1.2 collective-permute-start.37
  92.2 4.5 %collective-permute-done.22 = bf16[128,2048]{1,0:T(8,128)(2,1)S(1)} collective-permute-done((bf16[128,2048]{1,0:T(8,128)(2,1)S(1)}, bf16[128,2048]{1,0:T(8,128)(2,1)S(1)}, u32[]{:S(2)}, u32[]{:S(2)}) %collective-permute-start.22) | collective-permute-done | bytes 524320 | tf_op jit(solution)/shard_map/ring/ppermute | solution.py:198
  97.8 1.3 collective-permute-start.29
  99.3 3.6 %collective-permute-done.31 = bf16[32,2048]{1,0:T(8,128)(2,1)S(1)} collective-permute-done((bf16[32,2048]{1,0:T(8,128)(2,1)S(1)}, bf16[32,2048]{1,0:T(8,128)(2,1)S(1)}, u32[]{:S(2)}, u32[]{:S(2)}) %collective-permute-start.31) | collective-permute-done | bytes 131104 | tf_op jit(solution)/shard_map/ppermute | solution.py:287
  102.9 1.0 collective-permute-done.30
  104.0 1.0 collective-permute-start.32
  105.7 7.5 %shard_map.103 = (bf16[128,2048]{1,0:T(8,128)(2,1)S(1)}, bf16[128,2048]{1,0:T(8,128)(2,1)S(1)}) custom-call(bf16[128,2048]{1,0:T(8,128)(2,1)S(1)} %pad_maximum_fusion.3.own_ref, bf16[128,2048]{1,0:T(8,128)(2,1)S(1)} %collective-permute-done.37.other_ref, bf16[2048,2048]{1,0:T(8,128)(2,1)} %bitcast.82, bf16[2048,2048]{1,0:T(8,128)(2,1)} %bitcast.86, ...), custom_call_target="tpu_custom_call" | custom-call | flops 4000000000 | bytes 1000 | tf_op jit(solution)/shard_map/pallas_call | solution.py:145
  113.2 1.2 collective-permute-start.38
  114.5 1.5 collective-permute-done.23
  116.5 1.5 collective-permute-start.26
  117.9 1.1 collective-permute-start.25
  119.3 2.1 %collective-permute-done.26 = bf16[32,2048]{1,0:T(8,128)(2,1)S(1)} collective-permute-done((bf16[32,2048]{1,0:T(8,128)(2,1)S(1)}, bf16[32,2048]{1,0:T(8,128)(2,1)S(1)}, u32[]{:S(2)}, u32[]{:S(2)}) %collective-permute-start.26) | collective-permute-done | bytes 131104 | tf_op jit(solution)/shard_map/ppermute | solution.py:287
  121.5 3.7 %collective-permute-done.25 = bf16[32,2048]{1,0:T(8,128)(2,1)S(1)} collective-permute-done((bf16[32,2048]{1,0:T(8,128)(2,1)S(1)}, bf16[32,2048]{1,0:T(8,128)(2,1)S(1)}, u32[]{:S(2)}, u32[]{:S(2)}) %collective-permute-start.25) | collective-permute-done | bytes 131104 | tf_op jit(solution)/shard_map/ppermute | solution.py:287
  125.2 1.0 collective-permute-start.27
  126.2 7.5 %shard_map.102 = (bf16[128,2048]{1,0:T(8,128)(2,1)S(1)}, bf16[128,2048]{1,0:T(8,128)(2,1)S(1)}) custom-call(bf16[128,2048]{1,0:T(8,128)(2,1)S(1)} %pad_maximum_fusion.2.own_ref.refs_1_, bf16[128,2048]{1,0:T(8,128)(2,1)S(1)} %collective-permute-done.32.other_ref, bf16[2048,2048]{1,0:T(8,128)(2,1)} %bitcast.83, bf16[2048,2048]{1,0:T(8,128)(2,1)} %bitcast.87, ...), custom_call_target="tpu_custom_call" | custom-call | flops 4000000000 | bytes 1000 | tf_op jit(solution)/shard_map/pallas_call | solution.py:145
  133.9 1.5 collective-permute-start.41
  135.9 1.1 collective-permute-start.42
  136.9 4.4 %collective-permute-done.27.other_ref = bf16[128,2048]{1,0:T(8,128)(2,1)S(1)} collective-permute-done((bf16[128,2048]{1,0:T(8,128)(2,1)S(1)}, bf16[128,2048]{1,0:T(8,128)(2,1)S(1)}, u32[]{:S(2)}, u32[]{:S(2)}) %collective-permute-start.27) | collective-permute-done | bytes 524320 | tf_op jit(solution)/shard_map/half/ppermute | solution.py:202
  141.3 7.7 %shard_map.101 = (bf16[128,2048]{1,0:T(8,128)(2,1)S(1)}, bf16[128,2048]{1,0:T(8,128)(2,1)S(1)}) custom-call(bf16[128,2048]{1,0:T(8,128)(2,1)S(1)} %pad_maximum_fusion.1.own_ref.refs_0_, bf16[128,2048]{1,0:T(8,128)(2,1)S(1)} %collective-permute-done.27.other_ref, bf16[2048,2048]{1,0:T(8,128)(2,1)} %bitcast.84, bf16[2048,2048]{1,0:T(8,128)(2,1)} %bitcast.88), custom_call_target="tpu_custom_call" | custom-call | flops 4000000000 | bytes 1000 | tf_op jit(solution)/shard_map/pallas_call | solution.py:145
  149.9 1.4 collective-permute-start.51
  153.1 1.9 collective-permute-start.49
  155.0 7.5 %shard_map.104 = (bf16[128,2048]{1,0:T(8,128)(2,1)S(1)}, bf16[128,2048]{1,0:T(8,128)(2,1)S(1)}) custom-call(bf16[128,2048]{1,0:T(8,128)(2,1)S(1)} %pad_maximum_fusion.own_ref, bf16[128,2048]{1,0:T(8,128)(2,1)S(1)} %collective-permute-done.19.refs_0_.other_ref, bf16[2048,2048]{1,0:T(8,128)(2,1)} %bitcast.85, bf16[2048,2048]{1,0:T(8,128)(2,1)} %bitcast.89, ...), custom_call_target="tpu_custom_call" | custom-call | flops 4000000000 | bytes 1000 | tf_op jit(solution)/shard_map/pallas_call | solution.py:145
  162.5 1.0 collective-permute-start.43
  167.1 1.0 collective-permute-start.53
  168.2 8.6 %collective-permute-done.43 = bf16[128,2048]{1,0:T(8,128)(2,1)S(1)} collective-permute-done((bf16[128,2048]{1,0:T(8,128)(2,1)S(1)}, bf16[128,2048]{1,0:T(8,128)(2,1)S(1)}, u32[]{:S(2)}, u32[]{:S(2)}) %collective-permute-start.43) | collective-permute-done | bytes 524320 | tf_op jit(solution)/shard_map/half/ppermute | solution.py:202
  177.4 2.0 %collective-permute-done.55 = bf16[128,2048]{1,0:T(8,128)(2,1)S(1)} collective-permute-done((bf16[128,2048]{1,0:T(8,128)(2,1)S(1)}, bf16[128,2048]{1,0:T(8,128)(2,1)S(1)}, u32[]{:S(2)}, u32[]{:S(2)}) %collective-permute-start.55) | collective-permute-done | bytes 524320 | tf_op jit(solution)/shard_map/ring/ppermute | solution.py:198
  180.7 1.3 collective-permute-start.45
  182.5 3.9 %collective-permute-done.46 = bf16[32,2048]{1,0:T(8,128)(2,1)S(1)} collective-permute-done((bf16[32,2048]{1,0:T(8,128)(2,1)S(1)}, bf16[32,2048]{1,0:T(8,128)(2,1)S(1)}, u32[]{:S(2)}, u32[]{:S(2)}) %collective-permute-start.46) | collective-permute-done | bytes 131104 | tf_op jit(solution)/shard_map/ppermute | solution.py:287
  186.5 2.5 %collective-permute-done.45 = bf16[32,2048]{1,0:T(8,128)(2,1)S(1)} collective-permute-done((bf16[32,2048]{1,0:T(8,128)(2,1)S(1)}, bf16[32,2048]{1,0:T(8,128)(2,1)S(1)}, u32[]{:S(2)}, u32[]{:S(2)}) %collective-permute-start.45) | collective-permute-done | bytes 131104 | tf_op jit(solution)/shard_map/ppermute | solution.py:287
  189.3 3.8 %collective-permute-done.56 = bf16[128,2048]{1,0:T(8,128)(2,1)S(1)} collective-permute-done((bf16[128,2048]{1,0:T(8,128)(2,1)S(1)}, bf16[128,2048]{1,0:T(8,128)(2,1)S(1)}, u32[]{:S(2)}, u32[]{:S(2)}) %collective-permute-start.56) | collective-permute-done | bytes 524320 | tf_op jit(solution)/shard_map/home/ring/ppermute | solution.py:198
  193.1 1.2 fusion.8
  (164 shorter events, 23.8 us)
Async XLA Ops:
  1.3 16.1 %collective-permute-start.2 = (bf16[256,1024]{1,0:T(8,128)(2,1)S(1)}, bf16[256,1024]{1,0:T(8,128)(2,1)}, u32[]{:S(2)}, u32[]{:S(2)}) collective-permute-start(bf16[256,1024]{1,0:T(8,128)(2,1)S(1)} %constant_dynamic-slice_fusion), channel_id=1, source_target_pairs={{0,2},{1,3},{2,6},{3,7},{6,4},{7,5},{4,0},{5,1},{8,10},{9,11},{10,... | collective-permute-start | bytes 1572872 | tf_op jit(solution)/shard_map/gather_0/ring/ppermute | solution.py:198
  4.3 13.4 %collective-permute-start.1 = (bf16[256,1024]{1,0:T(8,128)(2,1)S(1)}, bf16[256,1024]{1,0:T(8,128)(2,1)S(1)}, u32[]{:S(2)}, u32[]{:S(2)}) collective-permute-start(bf16[256,1024]{1,0:T(8,128)(2,1)S(1)} %constant_dynamic-slice_fusion), channel_id=1, source_target_pairs={{0,1},{1,0},{2,3},{3,2},{4,5},{5,4},{6,7},{7,6},{8,9},{9,8},{10,11... | collective-permute-start | bytes 1572872 | tf_op jit(solution)/shard_map/gather_0/half/ppermute | solution.py:202
  5.9 13.3 %collective-permute-start.3 = (bf16[128,2048]{1,0:T(8,128)(2,1)}, bf16[128,2048]{1,0:T(8,128)(2,1)S(1)}, u32[]{:S(2)}, u32[]{:S(2)}) collective-permute-start(bf16[128,2048]{1,0:T(8,128)(2,1)} %bitcast.97), channel_id=1, source_target_pairs={{0,16},{8,24},{16,0},{24,8},{1,17},{9,25},{17,1},{25,9},{2,18},{10... | collective-permute-start | bytes 1572872 | tf_op jit(solution)/shard_map/gather_0/ppermute | solution.py:229
  19.2 19.0 %copy-start.5 = (bf16[128,2048]{1,0:T(8,128)(2,1)}, bf16[128,2048]{1,0:T(8,128)(2,1)S(1)}, u32[]{:S(2)}) copy-start(bf16[128,2048]{1,0:T(8,128)(2,1)S(1)} %collective-permute-done.3.refs_3_) | copy-start | bytes 1572868
  19.2 12.4 %collective-permute-start.8 = (bf16[128,2048]{1,0:T(8,128)(2,1)}, bf16[128,2048]{1,0:T(8,128)(2,1)S(1)}, u32[]{:S(2)}, u32[]{:S(2)}) collective-permute-start(bf16[128,2048]{1,0:T(8,128)(2,1)} %bitcast.100), channel_id=1, source_target_pairs={{0,16},{8,24},{16,0},{24,8},{1,17},{9,25},{17,1},{25,9},{2,18},{10... | collective-permute-start | bytes 1572872 | tf_op jit(solution)/shard_map/gather_1/ppermute | solution.py:229
  20.7 13.1 %collective-permute-start.7 = (bf16[256,1024]{1,0:T(8,128)(2,1)}, bf16[256,1024]{1,0:T(8,128)(2,1)}, u32[]{:S(2)}, u32[]{:S(2)}) collective-permute-start(bf16[256,1024]{1,0:T(8,128)(2,1)} %collective-permute-done.2), channel_id=1, source_target_pairs={{0,2},{1,3},{2,6},{3,7},{6,4},{7,5},{4,0},{5,1},{8,10},{9,11},{10,... | collective-permute-start | bytes 1572872 | tf_op jit(solution)/shard_map/gather_1/ring/ppermute | solution.py:198
  23.3 11.9 %collective-permute-start.6 = (bf16[256,1024]{1,0:T(8,128)(2,1)}, bf16[256,1024]{1,0:T(8,128)(2,1)}, u32[]{:S(2)}, u32[]{:S(2)}) collective-permute-start(bf16[256,1024]{1,0:T(8,128)(2,1)} %collective-permute-done.2), channel_id=1, source_target_pairs={{0,1},{1,0},{2,3},{3,2},{4,5},{5,4},{6,7},{7,6},{8,9},{9,8},{10,11... | collective-permute-start | bytes 1572872 | tf_op jit(solution)/shard_map/gather_1/half/ppermute | solution.py:202
  24.1 12.6 %collective-permute-start = (bf16[128,2048]{1,0:T(8,128)(2,1)}, bf16[128,2048]{1,0:T(8,128)(2,1)S(1)}, u32[]{:S(2)}, u32[]{:S(2)}) collective-permute-start(bf16[128,2048]{1,0:T(8,128)(2,1)} %bitcast.98), channel_id=1, source_target_pairs={{0,8},{8,0},{16,24},{24,16},{1,9},{9,1},{17,25},{25,17},{2,10},{10... | collective-permute-start | bytes 1572872 | tf_op jit(solution)/shard_map/core/ppermute | solution.py:206
  24.1 14.1 %collective-permute-start.5 = (bf16[128,2048]{1,0:T(8,128)(2,1)}, bf16[128,2048]{1,0:T(8,128)(2,1)}, u32[]{:S(2)}, u32[]{:S(2)}) collective-permute-start(bf16[128,2048]{1,0:T(8,128)(2,1)} %bitcast.101), channel_id=1, source_target_pairs={{0,8},{8,0},{16,24},{24,16},{1,9},{9,1},{17,25},{25,17},{2,10},{10... | collective-permute-start | bytes 1572872 | tf_op jit(solution)/shard_map/core/ppermute | solution.py:206
  31.6 6.6 %copy-start.6 = (bf16[128,2048]{1,0:T(8,128)(2,1)}, bf16[128,2048]{1,0:T(8,128)(2,1)S(1)}, u32[]{:S(2)}) copy-start(bf16[128,2048]{1,0:T(8,128)(2,1)S(1)} %collective-permute-done.8.refs_7_) | copy-start | bytes 1572868
  31.6 6.6 %collective-permute-start.4 = (bf16[128,2048]{1,0:T(8,128)(2,1)S(1)}, bf16[128,2048]{1,0:T(8,128)(2,1)}, u32[]{:S(2)}, u32[]{:S(2)}) collective-permute-start(bf16[128,2048]{1,0:T(8,128)(2,1)S(1)} %collective-permute-done.3.refs_3_), channel_id=1, source_target_pairs={{0,8},{8,0},{16,24},{24,16},{1,9},{9,1},{17,25},{25,17},{2,10},{10... | collective-permute-start | bytes 1572872 | tf_op jit(solution)/shard_map/core/ppermute | solution.py:206
  35.2 3.0 %collective-permute-start.9 = (bf16[128,2048]{1,0:T(8,128)(2,1)S(1)}, bf16[128,2048]{1,0:T(8,128)(2,1)}, u32[]{:S(2)}, u32[]{:S(2)}) collective-permute-start(bf16[128,2048]{1,0:T(8,128)(2,1)S(1)} %collective-permute-done.8.refs_7_), channel_id=1, source_target_pairs={{0,8},{8,0},{16,24},{24,16},{1,9},{9,1},{17,25},{25,17},{2,10},{10... | collective-permute-start | bytes 1572872 | tf_op jit(solution)/shard_map/core/ppermute | solution.py:206
  35.4 18.9 %collective-permute-start.12 = (bf16[256,1024]{1,0:T(8,128)(2,1)}, bf16[256,1024]{1,0:T(8,128)(2,1)S(1)}, u32[]{:S(2)}, u32[]{:S(2)}) collective-permute-start(bf16[256,1024]{1,0:T(8,128)(2,1)} %collective-permute-done.7), channel_id=1, source_target_pairs={{0,2},{1,3},{2,6},{3,7},{6,4},{7,5},{4,0},{5,1},{8,10},{9,11},{10,... | collective-permute-start | bytes 1572872 | tf_op jit(solution)/shard_map/gather_2/ring/ppermute | solution.py:198
  36.7 17.6 %collective-permute-start.11 = (bf16[256,1024]{1,0:T(8,128)(2,1)}, bf16[256,1024]{1,0:T(8,128)(2,1)S(1)}, u32[]{:S(2)}, u32[]{:S(2)}) collective-permute-start(bf16[256,1024]{1,0:T(8,128)(2,1)} %collective-permute-done.7), channel_id=1, source_target_pairs={{0,1},{1,0},{2,3},{3,2},{4,5},{5,4},{6,7},{7,6},{8,9},{9,8},{10,11... | collective-permute-start | bytes 1572872 | tf_op jit(solution)/shard_map/gather_2/half/ppermute | solution.py:202
  44.4 17.2 %copy-start.2 = (bf16[128,2048]{1,0:T(8,128)(2,1)S(1)}, bf16[128,2048]{1,0:T(8,128)(2,1)}, u32[]{:S(2)}) copy-start(bf16[128,2048]{1,0:T(8,128)(2,1)} %shard_map.100) | copy-start | bytes 1572868
  44.4 17.5 %copy-start.9 = (bf16[256,1024]{1,0:T(8,128)(2,1)S(1)}, bf16[256,1024]{1,0:T(8,128)(2,1)}, u32[]{:S(2)}) copy-start(bf16[256,1024]{1,0:T(8,128)(2,1)} %copy-done.8) | copy-start | bytes 1572868
  44.4 13.3 %collective-permute-start.10 = (bf16[128,2048]{1,0:T(8,128)(2,1)}, bf16[128,2048]{1,0:T(8,128)(2,1)S(1)}, u32[]{:S(2)}, u32[]{:S(2)}) collective-permute-start(bf16[128,2048]{1,0:T(8,128)(2,1)} %shard_map.100), channel_id=1, source_target_pairs={{0,8},{8,0},{16,24},{24,16},{1,9},{9,1},{17,25},{25,17},{2,10},{10... | collective-permute-start | bytes 1572872 | tf_op jit(solution)/shard_map/core/ppermute | solution.py:206
  44.5 9.6 %collective-permute-start.33 = (s32[2,128]{0,1:T(8,128)S(1)}, s32[2,128]{0,1:T(8,128)S(1)}, u32[]{:S(2)}, u32[]{:S(2)}) collective-permute-start(s32[2,128]{0,1:T(8,128)S(1)} %bitcast.93), channel_id=1, source_target_pairs={{0,2},{1,3},{2,6},{3,7},{6,4},{7,5},{4,0},{5,1},{8,10},{9,11},{10,... | collective-permute-start | bytes 3080 | tf_op jit(solution)/shard_map/gather_0/ring/ppermute | solution.py:198
  45.8 8.4 %collective-permute-start.28 = (s32[2,128]{0,1:T(8,128)S(1)}, s32[2,128]{0,1:T(8,128)S(1)}, u32[]{:S(2)}, u32[]{:S(2)}) collective-permute-start(s32[2,128]{0,1:T(8,128)S(1)} %bitcast.94), channel_id=1, source_target_pairs={{0,6},{1,7},{2,4},{3,5},{6,0},{7,1},{4,2},{5,3},{8,14},{9,15},{10,... | collective-permute-start | bytes 3080 | tf_op jit(solution)/shard_map/gather_0/ring/ppermute | solution.py:198
  54.1 10.8 %collective-permute-start.20 = (s32[2,128]{0,1:T(8,128)S(1)}, s32[2,128]{0,1:T(8,128)S(1)}, u32[]{:S(2)}, u32[]{:S(2)}) collective-permute-start(s32[2,128]{0,1:T(8,128)S(1)} %bitcast.95), channel_id=1, source_target_pairs={{0,4},{1,5},{2,0},{3,1},{6,2},{7,3},{4,6},{5,7},{8,12},{9,13},{10,... | collective-permute-start | bytes 3080 | tf_op jit(solution)/shard_map/gather_0/ring/ppermute | solution.py:198
  54.4 7.8 %collective-permute-start.13 = (bf16[128,1024]{1,0:T(8,128)(2,1)S(1)}, bf16[128,1024]{1,0:T(8,128)(2,1)S(1)}, u32[]{:S(2)}, u32[]{:S(2)}) collective-permute-start(bf16[128,1024]{1,0:T(8,128)(2,1)S(1)} %slice.180), channel_id=1, source_target_pairs={{0,1},{1,0},{2,3},{3,2},{4,5},{5,4},{6,7},{7,6},{8,9},{9,8},{10,11... | collective-permute-start | bytes 786440 | tf_op jit(solution)/shard_map/half/ppermute | solution.py:202
  55.6 8.3 %collective-permute-start.14 = (bf16[128,1024]{1,0:T(8,128)(2,1)S(1)}, bf16[128,1024]{1,0:T(8,128)(2,1)S(1)}, u32[]{:S(2)}, u32[]{:S(2)}) collective-permute-start(bf16[128,1024]{1,0:T(8,128)(2,1)S(1)} %slice.181), channel_id=1, source_target_pairs={{0,2},{1,3},{2,6},{3,7},{6,4},{7,5},{4,0},{5,1},{8,10},{9,11},{10,... | collective-permute-start | bytes 786440 | tf_op jit(solution)/shard_map/ring/ppermute | solution.py:198
  64.2 3.2 %copy-start.10 = (f32[2048]{0:T(1024)S(1)}, f32[2048]{0:T(1024)}, u32[]{:S(2)}) copy-start(f32[2048]{0:T(1024)} %param.15) | copy-start | bytes 24580
  64.2 7.5 %copy-start.4 = (bf16[2048,16]{0,1:T(8,128)(2,1)S(1)}, bf16[2048,16]{0,1:T(8,128)(2,1)}, u32[]{:S(2)}) copy-start(bf16[2048,16]{0,1:T(8,128)(2,1)} %param.16) | copy-start | bytes 196612
  64.8 2.0 %collective-permute-start.15 = (f32[128,1024]{1,0:T(8,128)S(1)}, f32[128,1024]{1,0:T(8,128)S(1)}, u32[]{:S(2)}, u32[]{:S(2)}) collective-permute-start(f32[128,1024]{1,0:T(8,128)S(1)} %slice.234), channel_id=1, source_target_pairs={{0,8},{8,0},{16,24},{24,16},{1,9},{9,1},{17,25},{25,17},{2,10},{10... | collective-permute-start | bytes 1572872 | tf_op jit(solution)/shard_map/core/ppermute | solution.py:206
  67.7 14.9 %collective-permute-start.21 = (bf16[128,2048]{1,0:T(8,128)(2,1)S(1)}, bf16[128,2048]{1,0:T(8,128)(2,1)S(1)}, u32[]{:S(2)}, u32[]{:S(2)}) collective-permute-start(bf16[128,2048]{1,0:T(8,128)(2,1)S(1)} %multiply_convert_fusion), channel_id=1, source_target_pairs={{0,2},{1,3},{2,6},{3,7},{6,4},{7,5},{4,0},{5,1},{8,10},{9,11},{10,... | collective-permute-start | bytes 1572872 | tf_op jit(solution)/shard_map/ring/ppermute | solution.py:198
  69.8 5.8 %collective-permute-start.18 = (bf16[32,2048]{1,0:T(8,128)(2,1)S(1)}, bf16[32,2048]{1,0:T(8,128)(2,1)S(1)}, u32[]{:S(2)}, u32[]{:S(2)}) collective-permute-start(bf16[32,2048]{1,0:T(8,128)(2,1)S(1)} %get-tuple-element.100), channel_id=1, source_target_pairs={{0,24},{8,16},{16,8},{24,0},{1,25},{9,17},{17,9},{25,1},{2,26},{10... | collective-permute-start | bytes 393224 | tf_op jit(solution)/shard_map/ppermute | solution.py:287
  69.9 8.6 %collective-permute-start.17 = (bf16[32,2048]{1,0:T(8,128)(2,1)S(1)}, bf16[32,2048]{1,0:T(8,128)(2,1)S(1)}, u32[]{:S(2)}, u32[]{:S(2)}) collective-permute-start(bf16[32,2048]{1,0:T(8,128)(2,1)S(1)} %get-tuple-element.101), channel_id=1, source_target_pairs={{0,16},{8,24},{16,0},{24,8},{1,17},{9,25},{17,1},{25,9},{2,18},{10... | collective-permute-start | bytes 393224 | tf_op jit(solution)/shard_map/ppermute | solution.py:287
  71.4 7.1 %collective-permute-start.16 = (bf16[32,2048]{1,0:T(8,128)(2,1)S(1)}, bf16[32,2048]{1,0:T(8,128)(2,1)S(1)}, u32[]{:S(2)}, u32[]{:S(2)}) collective-permute-start(bf16[32,2048]{1,0:T(8,128)(2,1)S(1)} %get-tuple-element.102), channel_id=1, source_target_pairs={{0,8},{8,0},{16,24},{24,16},{1,9},{9,1},{17,25},{25,17},{2,10},{10... | collective-permute-start | bytes 393224 | tf_op jit(solution)/shard_map/ppermute | solution.py:287
  78.5 26.5 %collective-permute-start.19 = (bf16[128,2048]{1,0:T(8,128)(2,1)S(1)}, bf16[128,2048]{1,0:T(8,128)(2,1)S(1)}, u32[]{:S(2)}, u32[]{:S(2)}) collective-permute-start(bf16[128,2048]{1,0:T(8,128)(2,1)S(1)} %pad_maximum_fusion.own_ref), channel_id=1, source_target_pairs={{0,1},{1,0},{2,3},{3,2},{4,5},{5,4},{6,7},{7,6},{8,9},{9,8},{10,11... | collective-permute-start | bytes 1572872 | tf_op jit(solution)/shard_map/half/ppermute | solution.py:202
  82.6 14.0 %collective-permute-start.22 = (bf16[128,2048]{1,0:T(8,128)(2,1)S(1)}, bf16[128,2048]{1,0:T(8,128)(2,1)S(1)}, u32[]{:S(2)}, u32[]{:S(2)}) collective-permute-start(bf16[128,2048]{1,0:T(8,128)(2,1)S(1)} %collective-permute-done.21), channel_id=1, source_target_pairs={{0,2},{1,3},{2,6},{3,7},{6,4},{7,5},{4,0},{5,1},{8,10},{9,11},{10,... | collective-permute-start | bytes 1572872 | tf_op jit(solution)/shard_map/ring/ppermute | solution.py:198
  83.8 5.8 %collective-permute-start.36 = (bf16[32,2048]{1,0:T(8,128)(2,1)S(1)}, bf16[32,2048]{1,0:T(8,128)(2,1)S(1)}, u32[]{:S(2)}, u32[]{:S(2)}) collective-permute-start(bf16[32,2048]{1,0:T(8,128)(2,1)S(1)} %get-tuple-element.88), channel_id=1, source_target_pairs={{0,24},{8,16},{16,8},{24,0},{1,25},{9,17},{17,9},{25,1},{2,26},{10... | collective-permute-start | bytes 393224 | tf_op jit(solution)/shard_map/ppermute | solution.py:287
  83.8 7.0 %collective-permute-start.35 = (bf16[32,2048]{1,0:T(8,128)(2,1)S(1)}, bf16[32,2048]{1,0:T(8,128)(2,1)S(1)}, u32[]{:S(2)}, u32[]{:S(2)}) collective-permute-start(bf16[32,2048]{1,0:T(8,128)(2,1)S(1)} %get-tuple-element.89), channel_id=1, source_target_pairs={{0,16},{8,24},{16,0},{24,8},{1,17},{9,25},{17,1},{25,9},{2,18},{10... | collective-permute-start | bytes 393224 | tf_op jit(solution)/shard_map/ppermute | solution.py:287
  84.5 6.4 %collective-permute-start.34 = (bf16[32,2048]{1,0:T(8,128)(2,1)S(1)}, bf16[32,2048]{1,0:T(8,128)(2,1)S(1)}, u32[]{:S(2)}, u32[]{:S(2)}) collective-permute-start(bf16[32,2048]{1,0:T(8,128)(2,1)S(1)} %get-tuple-element.90), channel_id=1, source_target_pairs={{0,8},{8,0},{16,24},{24,16},{1,9},{9,1},{17,25},{25,17},{2,10},{10... | collective-permute-start | bytes 393224 | tf_op jit(solution)/shard_map/ppermute | solution.py:287
  90.9 14.8 %collective-permute-start.37 = (bf16[128,2048]{1,0:T(8,128)(2,1)S(1)}, bf16[128,2048]{1,0:T(8,128)(2,1)S(1)}, u32[]{:S(2)}, u32[]{:S(2)}) collective-permute-start(bf16[128,2048]{1,0:T(8,128)(2,1)S(1)} %pad_maximum_fusion.3.own_ref), channel_id=1, source_target_pairs={{0,1},{1,0},{2,3},{3,2},{4,5},{5,4},{6,7},{7,6},{8,9},{9,8},{10,11... | collective-permute-start | bytes 1572872 | tf_op jit(solution)/shard_map/half/ppermute | solution.py:202
  97.1 5.8 %collective-permute-start.31 = (bf16[32,2048]{1,0:T(8,128)(2,1)S(1)}, bf16[32,2048]{1,0:T(8,128)(2,1)S(1)}, u32[]{:S(2)}, u32[]{:S(2)}) collective-permute-start(bf16[32,2048]{1,0:T(8,128)(2,1)S(1)} %get-tuple-element.92), channel_id=1, source_target_pairs={{0,24},{8,16},{16,8},{24,0},{1,25},{9,17},{17,9},{25,1},{2,26},{10... | collective-permute-start | bytes 393224 | tf_op jit(solution)/shard_map/ppermute | solution.py:287
  97.2 6.8 %collective-permute-start.30 = (bf16[32,2048]{1,0:T(8,128)(2,1)S(1)}, bf16[32,2048]{1,0:T(8,128)(2,1)S(1)}, u32[]{:S(2)}, u32[]{:S(2)}) collective-permute-start(bf16[32,2048]{1,0:T(8,128)(2,1)S(1)} %get-tuple-element.93), channel_id=1, source_target_pairs={{0,16},{8,24},{16,0},{24,8},{1,17},{9,25},{17,1},{25,9},{2,18},{10... | collective-permute-start | bytes 393224 | tf_op jit(solution)/shard_map/ppermute | solution.py:287
  97.8 6.2 %collective-permute-start.29 = (bf16[32,2048]{1,0:T(8,128)(2,1)S(1)}, bf16[32,2048]{1,0:T(8,128)(2,1)S(1)}, u32[]{:S(2)}, u32[]{:S(2)}) collective-permute-start(bf16[32,2048]{1,0:T(8,128)(2,1)S(1)} %get-tuple-element.94), channel_id=1, source_target_pairs={{0,8},{8,0},{16,24},{24,16},{1,9},{9,1},{17,25},{25,17},{2,10},{10... | collective-permute-start | bytes 393224 | tf_op jit(solution)/shard_map/ppermute | solution.py:287
  102.9 13.1 %collective-permute-start.23 = (bf16[128,2048]{1,0:T(8,128)(2,1)S(1)}, bf16[128,2048]{1,0:T(8,128)(2,1)S(1)}, u32[]{:S(2)}, u32[]{:S(2)}) collective-permute-start(bf16[128,2048]{1,0:T(8,128)(2,1)S(1)} %collective-permute-done.22), channel_id=1, source_target_pairs={{0,2},{1,3},{2,6},{3,7},{6,4},{7,5},{4,0},{5,1},{8,10},{9,11},{10,... | collective-permute-start | bytes 1572872 | tf_op jit(solution)/shard_map/ring/ppermute | solution.py:198
  104.0 22.2 %collective-permute-start.32 = (bf16[128,2048]{1,0:T(8,128)(2,1)S(1)}, bf16[128,2048]{1,0:T(8,128)(2,1)S(1)}, u32[]{:S(2)}, u32[]{:S(2)}) collective-permute-start(bf16[128,2048]{1,0:T(8,128)(2,1)S(1)} %pad_maximum_fusion.2.own_ref.refs_1_), channel_id=1, source_target_pairs={{0,1},{1,0},{2,3},{3,2},{4,5},{5,4},{6,7},{7,6},{8,9},{9,8},{10,11... | collective-permute-start | bytes 1572872 | tf_op jit(solution)/shard_map/half/ppermute | solution.py:202
  113.2 20.5 %collective-permute-start.38 = (bf16[128,2048]{1,0:T(8,128)(2,1)S(1)}, bf16[128,2048]{1,0:T(8,128)(2,1)S(1)}, u32[]{:S(2)}, u32[]{:S(2)}) collective-permute-start(bf16[128,2048]{1,0:T(8,128)(2,1)S(1)} %get-tuple-element.47), channel_id=1, source_target_pairs={{0,1},{1,0},{2,3},{3,2},{4,5},{5,4},{6,7},{7,6},{8,9},{9,8},{10,11... | collective-permute-start | bytes 1572872 | tf_op jit(solution)/shard_map/half/ppermute | solution.py:202
  116.5 5.0 %collective-permute-start.26 = (bf16[32,2048]{1,0:T(8,128)(2,1)S(1)}, bf16[32,2048]{1,0:T(8,128)(2,1)S(1)}, u32[]{:S(2)}, u32[]{:S(2)}) collective-permute-start(bf16[32,2048]{1,0:T(8,128)(2,1)S(1)} %get-tuple-element.96), channel_id=1, source_target_pairs={{0,24},{8,16},{16,8},{24,0},{1,25},{9,17},{17,9},{25,1},{2,26},{10... | collective-permute-start | bytes 393224 | tf_op jit(solution)/shard_map/ppermute | solution.py:287
  117.9 7.2 %collective-permute-start.25 = (bf16[32,2048]{1,0:T(8,128)(2,1)S(1)}, bf16[32,2048]{1,0:T(8,128)(2,1)S(1)}, u32[]{:S(2)}, u32[]{:S(2)}) collective-permute-start(bf16[32,2048]{1,0:T(8,128)(2,1)S(1)} %get-tuple-element.97), channel_id=1, source_target_pairs={{0,16},{8,24},{16,0},{24,8},{1,17},{9,25},{17,1},{25,9},{2,18},{10... | collective-permute-start | bytes 393224 | tf_op jit(solution)/shard_map/ppermute | solution.py:287
  119.0 6.1 %collective-permute-start.24 = (bf16[32,2048]{1,0:T(8,128)(2,1)S(1)}, bf16[32,2048]{1,0:T(8,128)(2,1)S(1)}, u32[]{:S(2)}, u32[]{:S(2)}) collective-permute-start(bf16[32,2048]{1,0:T(8,128)(2,1)S(1)} %get-tuple-element.98), channel_id=1, source_target_pairs={{0,8},{8,0},{16,24},{24,16},{1,9},{9,1},{17,25},{25,17},{2,10},{10... | collective-permute-start | bytes 393224 | tf_op jit(solution)/shard_map/ppermute | solution.py:287
  125.2 16.1 %collective-permute-start.27 = (bf16[128,2048]{1,0:T(8,128)(2,1)S(1)}, bf16[128,2048]{1,0:T(8,128)(2,1)S(1)}, u32[]{:S(2)}, u32[]{:S(2)}) collective-permute-start(bf16[128,2048]{1,0:T(8,128)(2,1)S(1)} %pad_maximum_fusion.1.own_ref.refs_0_), channel_id=1, source_target_pairs={{0,1},{1,0},{2,3},{3,2},{4,5},{5,4},{6,7},{7,6},{8,9},{9,8},{10,11... | collective-permute-start | bytes 1572872 | tf_op jit(solution)/shard_map/half/ppermute | solution.py:202
  133.9 15.1 %collective-permute-start.41 = (bf16[32,2048]{1,0:T(8,128)(2,1)S(1)}, bf16[32,2048]{1,0:T(8,128)(2,1)S(1)}, u32[]{:S(2)}, u32[]{:S(2)}) collective-permute-start(bf16[32,2048]{1,0:T(8,128)(2,1)S(1)} %get-tuple-element.83), channel_id=1, source_target_pairs={{0,24},{8,16},{16,8},{24,0},{1,25},{9,17},{17,9},{25,1},{2,26},{10... | collective-permute-start | bytes 393224 | tf_op jit(solution)/shard_map/ppermute | solution.py:287
  135.4 13.6 %collective-permute-start.40 = (bf16[32,2048]{1,0:T(8,128)(2,1)S(1)}, bf16[32,2048]{1,0:T(8,128)(2,1)S(1)}, u32[]{:S(2)}, u32[]{:S(2)}) collective-permute-start(bf16[32,2048]{1,0:T(8,128)(2,1)S(1)} %get-tuple-element.84), channel_id=1, source_target_pairs={{0,16},{8,24},{16,0},{24,8},{1,17},{9,25},{17,1},{25,9},{2,18},{10... | collective-permute-start | bytes 393224 | tf_op jit(solution)/shard_map/ppermute | solution.py:287
  135.7 13.3 %collective-permute-start.39 = (bf16[32,2048]{1,0:T(8,128)(2,1)S(1)}, bf16[32,2048]{1,0:T(8,128)(2,1)S(1)}, u32[]{:S(2)}, u32[]{:S(2)}) collective-permute-start(bf16[32,2048]{1,0:T(8,128)(2,1)S(1)} %get-tuple-element.85), channel_id=1, source_target_pairs={{0,8},{8,0},{16,24},{24,16},{1,9},{9,1},{17,25},{25,17},{2,10},{10... | collective-permute-start | bytes 393224 | tf_op jit(solution)/shard_map/ppermute | solution.py:287
  135.9 16.7 %collective-permute-start.42 = (bf16[128,2048]{1,0:T(8,128)(2,1)S(1)}, bf16[128,2048]{1,0:T(8,128)(2,1)S(1)}, u32[]{:S(2)}, u32[]{:S(2)}) collective-permute-start(bf16[128,2048]{1,0:T(8,128)(2,1)S(1)} %get-tuple-element.53), channel_id=1, source_target_pairs={{0,1},{1,0},{2,3},{3,2},{4,5},{5,4},{6,7},{7,6},{8,9},{9,8},{10,11... | collective-permute-start | bytes 1572872 | tf_op jit(solution)/shard_map/half/ppermute | solution.py:202
  149.9 15.0 %collective-permute-start.51 = (bf16[128,2048]{1,0:T(8,128)(2,1)S(1)}, bf16[128,2048]{1,0:T(8,128)(2,1)S(1)}, u32[]{:S(2)}, u32[]{:S(2)}) collective-permute-start(bf16[128,2048]{1,0:T(8,128)(2,1)S(1)} %fusion.5), channel_id=1, source_target_pairs={{0,2},{1,3},{2,6},{3,7},{6,4},{7,5},{4,0},{5,1},{8,10},{9,11},{10,... | collective-permute-start | bytes 1572872 | tf_op jit(solution)/shard_map/ring/ppermute | solution.py:198
  151.3 14.8 %collective-permute-start.47 = (bf16[128,2048]{1,0:T(8,128)(2,1)S(1)}, bf16[128,2048]{1,0:T(8,128)(2,1)S(1)}, u32[]{:S(2)}, u32[]{:S(2)}) collective-permute-start(bf16[128,2048]{1,0:T(8,128)(2,1)S(1)} %get-tuple-element.57), channel_id=1, source_target_pairs={{0,1},{1,0},{2,3},{3,2},{4,5},{5,4},{6,7},{7,6},{8,9},{9,8},{10,11... | collective-permute-start | bytes 1572872 | tf_op jit(solution)/shard_map/half/ppermute | solution.py:202
  152.7 9.8 %collective-permute-start.50 = (bf16[32,2048]{1,0:T(8,128)(2,1)S(1)}, bf16[32,2048]{1,0:T(8,128)(2,1)S(1)}, u32[]{:S(2)}, u32[]{:S(2)}) collective-permute-start(bf16[32,2048]{1,0:T(8,128)(2,1)S(1)} %get-tuple-element.76), channel_id=1, source_target_pairs={{0,24},{8,16},{16,8},{24,0},{1,25},{9,17},{17,9},{25,1},{2,26},{10... | collective-permute-start | bytes 393224 | tf_op jit(solution)/shard_map/ppermute | solution.py:287
  153.1 10.5 %collective-permute-start.49 = (bf16[32,2048]{1,0:T(8,128)(2,1)S(1)}, bf16[32,2048]{1,0:T(8,128)(2,1)S(1)}, u32[]{:S(2)}, u32[]{:S(2)}) collective-permute-start(bf16[32,2048]{1,0:T(8,128)(2,1)S(1)} %get-tuple-element.77), channel_id=1, source_target_pairs={{0,16},{8,24},{16,0},{24,8},{1,17},{9,25},{17,1},{25,9},{2,18},{10... | collective-permute-start | bytes 393224 | tf_op jit(solution)/shard_map/ppermute | solution.py:287
  155.0 8.6 %collective-permute-start.48 = (bf16[32,2048]{1,0:T(8,128)(2,1)S(1)}, bf16[32,2048]{1,0:T(8,128)(2,1)S(1)}, u32[]{:S(2)}, u32[]{:S(2)}) collective-permute-start(bf16[32,2048]{1,0:T(8,128)(2,1)S(1)} %get-tuple-element.78), channel_id=1, source_target_pairs={{0,8},{8,0},{16,24},{24,16},{1,9},{9,1},{17,25},{25,17},{2,10},{10... | collective-permute-start | bytes 393224 | tf_op jit(solution)/shard_map/ppermute | solution.py:287
  162.5 14.4 %collective-permute-start.43 = (bf16[128,2048]{1,0:T(8,128)(2,1)S(1)}, bf16[128,2048]{1,0:T(8,128)(2,1)S(1)}, u32[]{:S(2)}, u32[]{:S(2)}) collective-permute-start(bf16[128,2048]{1,0:T(8,128)(2,1)S(1)} %get-tuple-element.55), channel_id=1, source_target_pairs={{0,1},{1,0},{2,3},{3,2},{4,5},{5,4},{6,7},{7,6},{8,9},{9,8},{10,11... | collective-permute-start | bytes 1572872 | tf_op jit(solution)/shard_map/half/ppermute | solution.py:202
  164.9 29.4 %copy-start.1 = (bf16[256,2048]{1,0:T(8,128)(2,1)S(1)}, bf16[256,2048]{1,0:T(8,128)(2,1)}, u32[]{:S(2)}) copy-start(bf16[256,2048]{1,0:T(8,128)(2,1)} %param.14) | copy-start | bytes 3145732
  165.3 14.2 %collective-permute-start.55 = (bf16[128,2048]{1,0:T(8,128)(2,1)S(1)}, bf16[128,2048]{1,0:T(8,128)(2,1)S(1)}, u32[]{:S(2)}, u32[]{:S(2)}) collective-permute-start(bf16[128,2048]{1,0:T(8,128)(2,1)S(1)} %fusion.6), channel_id=1, source_target_pairs={{0,2},{1,3},{2,6},{3,7},{6,4},{7,5},{4,0},{5,1},{8,10},{9,11},{10,... | collective-permute-start | bytes 1572872 | tf_op jit(solution)/shard_map/ring/ppermute | solution.py:198
  166.3 10.7 %collective-permute-start.54 = (bf16[32,2048]{1,0:T(8,128)(2,1)S(1)}, bf16[32,2048]{1,0:T(8,128)(2,1)S(1)}, u32[]{:S(2)}, u32[]{:S(2)}) collective-permute-start(bf16[32,2048]{1,0:T(8,128)(2,1)S(1)} %get-tuple-element.72), channel_id=1, source_target_pairs={{0,24},{8,16},{16,8},{24,0},{1,25},{9,17},{17,9},{25,1},{2,26},{10... | collective-permute-start | bytes 393224 | tf_op jit(solution)/shard_map/ppermute | solution.py:287
  167.1 9.9 %collective-permute-start.53 = (bf16[32,2048]{1,0:T(8,128)(2,1)S(1)}, bf16[32,2048]{1,0:T(8,128)(2,1)S(1)}, u32[]{:S(2)}, u32[]{:S(2)}) collective-permute-start(bf16[32,2048]{1,0:T(8,128)(2,1)S(1)} %get-tuple-element.73), channel_id=1, source_target_pairs={{0,16},{8,24},{16,0},{24,8},{1,17},{9,25},{17,1},{25,9},{2,18},{10... | collective-permute-start | bytes 393224 | tf_op jit(solution)/shard_map/ppermute | solution.py:287
  168.2 8.9 %collective-permute-start.52 = (bf16[32,2048]{1,0:T(8,128)(2,1)S(1)}, bf16[32,2048]{1,0:T(8,128)(2,1)S(1)}, u32[]{:S(2)}, u32[]{:S(2)}) collective-permute-start(bf16[32,2048]{1,0:T(8,128)(2,1)S(1)} %get-tuple-element.74), channel_id=1, source_target_pairs={{0,8},{8,0},{16,24},{24,16},{1,9},{9,1},{17,25},{25,17},{2,10},{10... | collective-permute-start | bytes 393224 | tf_op jit(solution)/shard_map/ppermute | solution.py:287
  179.8 13.2 %collective-permute-start.56 = (bf16[128,2048]{1,0:T(8,128)(2,1)S(1)}, bf16[128,2048]{1,0:T(8,128)(2,1)S(1)}, u32[]{:S(2)}, u32[]{:S(2)}) collective-permute-start(bf16[128,2048]{1,0:T(8,128)(2,1)S(1)} %fusion.7), channel_id=1, source_target_pairs={{0,2},{1,3},{2,6},{3,7},{6,4},{7,5},{4,0},{5,1},{8,10},{9,11},{10,... | collective-permute-start | bytes 1572872 | tf_op jit(solution)/shard_map/home/ring/ppermute | solution.py:198
  180.6 5.9 %collective-permute-start.46 = (bf16[32,2048]{1,0:T(8,128)(2,1)S(1)}, bf16[32,2048]{1,0:T(8,128)(2,1)S(1)}, u32[]{:S(2)}, u32[]{:S(2)}) collective-permute-start(bf16[32,2048]{1,0:T(8,128)(2,1)S(1)} %get-tuple-element.80), channel_id=1, source_target_pairs={{0,24},{8,16},{16,8},{24,0},{1,25},{9,17},{17,9},{25,1},{2,26},{10... | collective-permute-start | bytes 393224 | tf_op jit(solution)/shard_map/ppermute | solution.py:287
  180.7 8.3 %collective-permute-start.45 = (bf16[32,2048]{1,0:T(8,128)(2,1)S(1)}, bf16[32,2048]{1,0:T(8,128)(2,1)S(1)}, u32[]{:S(2)}, u32[]{:S(2)}) collective-permute-start(bf16[32,2048]{1,0:T(8,128)(2,1)S(1)} %get-tuple-element.81), channel_id=1, source_target_pairs={{0,16},{8,24},{16,0},{24,8},{1,17},{9,25},{17,1},{25,9},{2,18},{10... | collective-permute-start | bytes 393224 | tf_op jit(solution)/shard_map/ppermute | solution.py:287
  182.0 6.9 %collective-permute-start.44 = (bf16[32,2048]{1,0:T(8,128)(2,1)S(1)}, bf16[32,2048]{1,0:T(8,128)(2,1)S(1)}, u32[]{:S(2)}, u32[]{:S(2)}) collective-permute-start(bf16[32,2048]{1,0:T(8,128)(2,1)S(1)} %get-tuple-element.82), channel_id=1, source_target_pairs={{0,8},{8,0},{16,24},{24,16},{1,9},{9,1},{17,25},{25,17},{2,10},{10... | collective-permute-start | bytes 393224 | tf_op jit(solution)/shard_map/ppermute | solution.py:287
  (4 other events, 7.3 us)
